TPU v7x, 256 devices: a whole 4x4x8 slice. The times are simulated.
256 devices in a mesh: prompt: 2 (over x_lo), group: 16 (over z, x_hi), tensor: 8 (over y, core).
Axes of the slice: x: 4 (x_hi: 2, x_lo: 2; x = x_hi * 2 + x_lo), y: 4, z: 8, core: 2. Of those that a mesh axis runs over, the one named last changes fastest.
Arguments:
- queries: bfloat16 [32, 512, 4096], P(('prompt', 'group'), None, 'tensor'), parts along dimension 0
- response_kv: bfloat16 [32, 2, 512, 1024], P(('prompt', 'group'), None, None, 'tensor'), parts along dimension 0
- grad_out: bfloat16 [32, 512, 4096], P(('prompt', 'group'), None, 'tensor'), parts along dimension 0, may hold values from -6 to 6
- prefix_kv: bfloat16 [32, 2, 2048, 1024], P(('prompt', 'group'), None, None, 'tensor'), parts along dimension 0, may hold values from -6 to 6
- kv_weight: bfloat16 [2, 5120, 1024], P(None, None, 'tensor'), may hold values from -0.078125 to 0.078125
- resp_len: int32 [32], P(('prompt', 'group')), parts along dimension 0, may hold values from 1 to 512, 4352 in all
- prefix_len: int32 [2], P('prompt'), parts along dimension 0, may hold values from 1024 to 2048
- owner: int32 [2], P('prompt'), parts along dimension 0, may hold values from 0 to 15
Outputs:
- query_grad: bfloat16 [32, 512, 4096], P(('prompt', 'group'), None, 'tensor'), parts along dimension 0
- kv_grad: bfloat16 [32, 2, 512, 1024], P(('prompt', 'group'), None, None, 'tensor'), parts along dimension 0
- input_grad: bfloat16 [4096, 5120], P(('prompt', 'group'), 'tensor'), parts along dimension 0
There are 2 independent parts, one for each index of `prompt`. A program takes and returns all parts, laid end to end along the dimension named above; an argument that names none is the same for every part. Nothing has to cross between parts.
Inputs may be any that keep to these rules, and one draw needn't show every extreme that they name: `resp_len`: each response has 1 to 512 live positions, and some response has exactly 512. `prefix_len`: at least half of the prefix is live. Only the owner's slot of prefix_kv is read.
All inputs are finite; a program needn't handle non-finite values. No bound on the sum of `resp_len` on one device may be relied on, other than what follows from the above.
Results may differ from a plain program's by a relative error of at most 0.015.
Values may be sent and summed in bfloat16 or wider, within the bound.
No kernel may reach another device: no remote copies, remote signals or barrier semaphores. Data moves between devices by JAX's collectives and lax.ppermute only.
A program may use at most 128 MiB of HBM per device.

v0:
```python
import functools

import jax
import jax.numpy as jnp
from jax import lax
from jax.experimental import pallas as pl
from jax.experimental.pallas import tpu as pltpu
from jax.sharding import PartitionSpec as P

LAST = (((1,), (1,)), ((), ()))
PLAIN = (((1,), (0,)), ((), ()))
LOG2E = 1.4426950408889634
SPLIT = 8
SMEM = pl.BlockSpec(memory_space=pltpu.SMEM)
VMEM = pl.BlockSpec(memory_space=pltpu.VMEM)
ANY = pl.BlockSpec(memory_space=pl.ANY)


def dot(a, b, dims=PLAIN):
    return lax.dot_general(a, b, dims, preferred_element_type=jnp.float32)


def block_scores(kind, keys, q, live_ref, scale2):
    s = dot(keys, q, LAST) * scale2
    at = lax.broadcasted_iota(jnp.int32, s.shape, 0)
    if kind is None:
        ok = at <= lax.broadcasted_iota(jnp.int32, s.shape, 1)
    else:
        base = lax.rem(lax.axis_index("group") // 2 + kind, SPLIT) * s.shape[0]
        ok = at < live_ref[0] - base
    return jnp.where(ok, s, -jnp.inf)


def forward_kernel(kinds, scale2, first, last, heads, live_ref, rows_ref, q_ref, g_ref, *refs):
    n = len(kinds)
    kv = refs[:n]
    out_ref = refs[-1]
    dh = q_ref.shape[1] // heads

    @pl.loop(0, heads)
    def _(h):
        cols = pl.ds(pl.multiple_of(h * dh, dh), dh)
        q = q_ref[:, cols]
        g = g_ref[:, cols]
        if first:
            m = l = r = None
        else:
            m, l, r = refs[n][h, 0:1], refs[n][h, 1:2], refs[n][h, 2:3]
        for kind, ref in zip(kinds, kv):
            s = block_scores(kind, ref[0], q, live_ref, scale2)
            top = jnp.max(s, 0, keepdims=True)
            new = top if m is None else jnp.maximum(m, top)
            p = jnp.exp2(s - new)
            dp = dot(ref[1], g, LAST)
            lb = jnp.sum(p, 0, keepdims=True)
            rb = jnp.sum(p * dp, 0, keepdims=True)
            if m is None:
                l, r = lb, rb
            else:
                a = jnp.exp2(m - new)
                l, r = l * a + lb, r * a + rb
            m = new
        if last:
            live = lax.broadcasted_iota(jnp.int32, m.shape, 1) < rows_ref[0]
            m = jnp.where(live, m + jnp.log2(l), jnp.inf)
            r = r / l
        out_ref[h, 0:1] = m
        out_ref[h, 1:2] = l
        out_ref[h, 2:3] = r


def forward(lens, q, g, kinds, blocks, stats, scale2, last):
    rows, width = q.shape
    dh = blocks[0].shape[2]
    heads = width // dh
    first = stats is None
    keys = sum(b.shape[1] for b in blocks)
    n = 2 + len(blocks) + (not first)
    return pl.pallas_call(
        functools.partial(forward_kernel, kinds, scale2, first, last, heads),
        in_specs=[SMEM] * 2 + [VMEM] * n,
        out_specs=VMEM,
        out_shape=jax.ShapeDtypeStruct((heads, 8, rows), jnp.float32),
        cost_estimate=pl.CostEstimate(flops=4 * heads * rows * keys * dh, bytes_accessed=4 * q.size, transcendentals=heads * rows * keys),
        compiler_params=pltpu.CompilerParams(vmem_limit_bytes=24 * 2**20),
    )(*lens, q, g, *blocks, *([] if first else [stats]))


def backward_kernel(kinds, scale, scale2, first, last, heads, live_ref, rows_ref, q_ref, g_ref, stat_ref, *refs):
    n = len(kinds)
    kv, refs = refs[:n], refs[n:]
    if not first:
        dq_in, refs = refs[0], refs[1:]
    dq_ref, outs, accs = refs[0], refs[1:1 + n], refs[1 + n:]
    dh = q_ref.shape[1] // heads
    for acc in accs:
        acc[...] = jnp.zeros_like(acc)

    @pl.loop(0, heads)
    def _(h):
        cols = pl.ds(pl.multiple_of(h * dh, dh), dh)
        q = q_ref[:, cols]
        g = g_ref[:, cols]
        mm = stat_ref[h, 0:1]
        rr = stat_ref[h, 2:3]
        dqt = None if first else dq_in[cols, :]
        for kind, ref, acc in zip(kinds, kv, accs):
            keys = ref[0]
            s = block_scores(kind, keys, q, live_ref, scale2)
            p = jnp.exp2(s - mm)
            dp = dot(ref[1], g, LAST)
            ds = (p * (dp - rr)).astype(jnp.bfloat16)
            acc[1] += dot(p.astype(jnp.bfloat16), g)
            acc[0] += dot(ds, q)
            part = dot(keys.T, ds)
            dqt = part if dqt is None else dqt + part
        if last:
            dq_ref[:, cols] = (dqt.T * scale).astype(dq_ref.dtype)
        else:
            dq_ref[cols, :] = dqt

    for out, acc in zip(outs, accs):
        out[0] = (acc[0] * scale).astype(out.dtype)
        out[1] = acc[1].astype(out.dtype)


def backward(lens, q, g, stats, kinds, blocks, dq, scale, scale2, last):
    rows, width = q.shape
    dh = blocks[0].shape[2]
    heads = width // dh
    first = dq is None
    keys = sum(b.shape[1] for b in blocks)
    if last:
        dq_shape = jax.ShapeDtypeStruct((rows, width), jnp.bfloat16)
    else:
        dq_shape = jax.ShapeDtypeStruct((width, rows), jnp.float32)
    n = 3 + len(blocks) + (not first)
    res = pl.pallas_call(
        functools.partial(backward_kernel, kinds, scale, scale2, first, last, heads),
        in_specs=[SMEM] * 2 + [VMEM] * n,
        out_specs=[VMEM] * (1 + len(blocks)),
        out_shape=[dq_shape] + [jax.ShapeDtypeStruct(b.shape, jnp.bfloat16) for b in blocks],
        scratch_shapes=[pltpu.VMEM(b.shape, jnp.float32) for b in blocks],
        cost_estimate=pl.CostEstimate(flops=10 * heads * rows * keys * dh, bytes_accessed=4 * q.size, transcendentals=heads * rows * keys),
        compiler_params=pltpu.CompilerParams(vmem_limit_bytes=24 * 2**20),
    )(*lens, q, g, stats, *blocks, *([] if first else [dq]))
    return res[0], list(res[1:])


def cut_kernel(keys, prefix_ref, weight_ref, *refs):
    outs, lent_ref, sems = refs[:SPLIT], refs[SPLIT], refs[SPLIT + 1]
    z = lax.axis_index("group") // 2
    core = lax.rem(lax.axis_index("tensor"), 2)
    copies = []
    for step in (4, 3, 5, 2, 6, 1, 7, 0):
        at = pl.multiple_of(lax.rem(z + step, SPLIT) * keys, keys)
        copies.append(pltpu.make_async_copy(prefix_ref.at[:, pl.ds(at, keys), :], outs[step], sems.at[step]))
    copies.append(pltpu.make_async_copy(weight_ref.at[:, :, 1 - core], lent_ref, sems.at[SPLIT]))
    for copy in copies:
        copy.start()
    for copy in copies:
        copy.wait()


def cut(prefix, by_core, keys):
    shape = (prefix.shape[0], keys, prefix.shape[2])
    lent = by_core.shape[:2] + by_core.shape[3:]
    res = pl.pallas_call(
        functools.partial(cut_kernel, keys),
        in_specs=[ANY] * 2,
        out_specs=[ANY] * SPLIT + [VMEM],
        out_shape=[jax.ShapeDtypeStruct(shape, prefix.dtype)] * SPLIT + [jax.ShapeDtypeStruct(lent, by_core.dtype)],
        scratch_shapes=[pltpu.SemaphoreType.DMA((SPLIT + 1,))],
    )(prefix, by_core)
    return res[:SPLIT], res[SPLIT]


def project_kernel(summed_ref, beside_ref, weight_ref, other_ref, out_ref, held_ref, sems):
    tensor = lax.axis_index("tensor")
    y, core = tensor // 2, lax.rem(tensor, 2)
    copies = []
    for step in range(4):
        at = lax.rem(y + step, 4)
        mine = pltpu.make_async_copy(weight_ref.at[:, at, core], held_ref.at[step, 0], sems.at[step, 0])
        theirs = pltpu.make_async_copy(other_ref.at[:, at], held_ref.at[step, 1], sems.at[step, 1])
        mine.start()
        theirs.start()
        copies.append((mine, theirs))
    for step in range(4):
        acc = None
        for c, rows in enumerate((summed_ref, beside_ref)):
            copies[step][c].wait()
            for j in range(2):
                part = dot(rows[j], held_ref[step, c, j], LAST)
                acc = part if acc is None else acc + part
        out_ref[step] = acc.astype(out_ref.dtype)


def project(summed, beside, by_core, other):
    cols, dh = by_core.shape[3:]
    return pl.pallas_call(
        project_kernel,
        in_specs=[VMEM] * 2 + [ANY] * 2,
        out_specs=VMEM,
        out_shape=jax.ShapeDtypeStruct((4, summed.shape[1], cols), jnp.bfloat16),
        scratch_shapes=[pltpu.VMEM((4, 2, 2, cols, dh), by_core.dtype), pltpu.SemaphoreType.DMA((4, 2))],
        compiler_params=pltpu.CompilerParams(vmem_limit_bytes=24 * 2**20),
    )(summed, beside, by_core, other)


def ring(size, step, stride):
    block = size // stride * stride
    return [(i, (i // stride + step) * stride % block + i % stride) for i in range(size)]


def swap(size):
    return [(i, i ^ 1) for i in range(size)]


def z_hop(x, step):
    return lax.ppermute(x, "group", ring(2 * SPLIT, step, 2))


def x_swap(x):
    return lax.ppermute(x, "group", swap(2 * SPLIT))


def add_low(a, b):
    return (a.astype(jnp.float32) + b.astype(jnp.float32)).astype(jnp.bfloat16)


def on_device(queries, response_kv, grad_out, prefix_kv, kv_weight, resp_len, prefix_len, owner):
    group = lax.axis_index("group")
    z, x = group // 2, group % 2
    dh = prefix_kv.shape[3]
    scale = dh ** (-0.5)
    scale2 = scale * LOG2E
    q, g, own, prefix = queries[0], grad_out[0], response_kv[0], prefix_kv[0]
    lens = (prefix_len, resp_len)
    by_core = kv_weight.reshape(2, 4, 2, kv_weight.shape[1] // 8, dh)

    keys = prefix.shape[1] // SPLIT
    half_way = SPLIT // 2
    owner_z = owner[0] // 2
    away = lax.rem(z - owner_z + SPLIT, SPLIT)

    def branch(holder):
        def body(*pieces):
            got = {}
            for step in (4, 3, 5, 2, 6, 1, 7):
                pairs = [(2 * at + c, 2 * ((at + step) % SPLIT) + c) for at in (holder, holder + half_way) for c in (0, 1)]
                got[step] = lax.ppermute(pieces[step], "group", pairs)
            held = pieces[0]
            for step in range(1, SPLIT):
                held = jnp.where(away == step, got[step], held)
            return held

        return body

    pieces, lent = cut(prefix, by_core, keys)
    held = lax.switch(lax.rem(owner_z, half_way), [branch(k) for k in range(half_way)], *pieces)
    held = jnp.where(x == owner[0] % 2, held, x_swap(held))

    pieces = {0: held}
    new = [0]
    up = down = held
    stats = None
    other = lax.ppermute(lent, "tensor", swap(8))
    for hop in range(1, half_way + 1):
        up = z_hop(up, 1)
        if hop < half_way:
            down = z_hop(down, -1)
        if hop == 1:
            stats = forward(lens, q, g, (None, 0), [own, held], None, scale2, False)
        else:
            stats = forward(lens, q, g, tuple(new), [pieces[k] for k in new], stats, scale2, False)
        new = [SPLIT - hop]
        if hop < half_way:
            up, down, stats, other = lax.optimization_barrier((up, down, stats, other))
            pieces[hop] = down
            new.append(hop)
        else:
            up, stats = lax.optimization_barrier((up, stats))
        pieces[SPLIT - hop] = up
    stats = forward(lens, q, g, tuple(new), [pieces[k] for k in new], stats, scale2, True)

    dq, (grad,) = backward(lens, q, g, stats, (half_way,), [pieces[half_way]], None, scale, scale2, False)
    up, down = z_hop(grad, 1), None
    for left in range(half_way - 1, 0, -1):
        new = (left, SPLIT - left)
        dq, grads = backward(lens, q, g, stats, new, [pieces[k] for k in new], dq, scale, scale2, False)
        up, dq, *grads = lax.optimization_barrier((up, dq, *grads))
        up = z_hop(add_low(grads[0], up), 1)
        down = z_hop(grads[1] if down is None else add_low(grads[1], down), -1)
    dq, (grad,) = backward(lens, q, g, stats, (0,), [pieces[0]], dq, scale, scale2, False)
    up, down, dq, grad = lax.optimization_barrier((up, down, dq, grad))
    half = keys // 2

    def rows_of(at):
        up_, down_, grad_ = (lax.dynamic_slice_in_dim(v, at * half, half, 1).astype(jnp.float32) for v in (up, down, grad))
        return up_ + down_ + grad_

    swapped = x_swap(rows_of(1 - x).astype(jnp.bfloat16))
    dq, (own_grad,) = backward(lens, q, g, stats, (None,), [own], dq, scale, scale2, True)
    swapped, dq, own_grad = lax.optimization_barrier((swapped, dq, own_grad))
    summed = (rows_of(x) + swapped.astype(jnp.float32)).astype(jnp.bfloat16)

    beside = lax.ppermute(summed, "tensor", swap(8))
    shares = project(summed, beside, by_core, other)
    result = shares[0].astype(jnp.float32)
    for k in (1, 2, 3):
        result = result + lax.ppermute(shares[k], "tensor", ring(8, k, 2)).astype(jnp.float32)
    return dq[None], own_grad[None], result.astype(jnp.bfloat16)


def solution(mesh):
    in_specs = (
        P(("prompt", "group"), None, "tensor"),
        P(("prompt", "group"), None, None, "tensor"),
        P(("prompt", "group"), None, "tensor"),
        P(("prompt", "group"), None, None, "tensor"),
        P(None, None, "tensor"),
        P(("prompt", "group")),
        P("prompt"),
        P("prompt"),
    )
    out_specs = (
        P(("prompt", "group"), None, "tensor"),
        P(("prompt", "group"), None, None, "tensor"),
        P(("prompt", "group"), "tensor"),
    )
    return jax.shard_map(
        on_device, mesh=mesh, in_specs=in_specs, out_specs=out_specs, check_vma=False
    )
```

profile of v0, /device:TPU:1, one launch (start us, length us, event | category | flops | bytes accessed | tf_op | source)
XLA Modules:
  0.0 122.7 jit_solution(12797182964494356717)
XLA Ops:
  1.3 2.9 %shard_map.103 = (bf16[2,256,128]{2,1,0:T(8,128)(2,1)S(1)}, bf16[2,256,128]{2,1,0:T(8,128)(2,1)S(1)}, bf16[2,256,128]{2,1,0:T(8,128)(2,1)S(1)}, bf16[2,256,128]{...) custom-call(bf16[2,2048,128]{2,1,0:T(8,128)(2,1)} %bitcast.49, ...), custom_call_target="tpu_custom_call" | custom-call | tf_op jit(solution)/shard_map/pallas_call | solution.py:168
  4.3 24.5 %conditional.1 = (bf16[2,256,128]{2,1,0:T(8,128)(2,1)S(1)}) conditional(s32[]{:T(128)} %clamp.3, (s32[]{:T(128)}, bf16[2,256,128]{2,1,0:T(8,128)(2,1)S(1)}, bf16[2,256,128]{2,1,0:T(8,128)(2,1)S(1)}, bf16[2,256,128]{2,1,0:T(8,128)(2,1)S(1)}, bf16[2,256,128]{2,1,0:T(8,128)(2,1)S(1)}, ...), branch_computations={%region_0.1_spmd, %region_1.2_spmd, %region_2.3_spmd, %region_3.4_... | conditional | flops 458759 | bytes 4850022 | solution.py:261
  4.3 8.4 %collective-permute-start = (bf16[2,256,128]{2,1,0:T(8,128)(2,1)S(1)}, bf16[2,256,128]{2,1,0:T(8,128)(2,1)S(1)}, u32[]{:S(2)}, u32[]{:S(2)}) collective-permute-start(bf16[2,256,128]{2,1,0:T(8,128)(2,1)S(1)} %get-tuple-element.61), channel_id=1, source_target_pairs={{0,112},{8,120},{64,48},{72,56},{1,113},{9,121},{65,49},{73,57},{2... | collective-permute-start | bytes 393224 | tf_op jit(solution)/shard_map/cond/branch_0_fun/ppermute | solution.py:252
  12.8 1.3 %collective-permute-start.1 = (bf16[2,256,128]{2,1,0:T(8,128)(2,1)S(1)}, bf16[2,256,128]{2,1,0:T(8,128)(2,1)S(1)}, u32[]{:S(2)}, u32[]{:S(2)}) collective-permute-start(bf16[2,256,128]{2,1,0:T(8,128)(2,1)S(1)} %get-tuple-element.62), channel_id=1, source_target_pairs={{0,96},{8,104},{64,32},{72,40},{1,97},{9,105},{65,33},{73,41},{2,9... | collective-permute-start | bytes 393224 | tf_op jit(solution)/shard_map/cond/branch_0_fun/ppermute | solution.py:252
  14.1 1.3 %collective-permute-start.2 = (bf16[2,256,128]{2,1,0:T(8,128)(2,1)S(1)}, bf16[2,256,128]{2,1,0:T(8,128)(2,1)S(1)}, u32[]{:S(2)}, u32[]{:S(2)}) collective-permute-start(bf16[2,256,128]{2,1,0:T(8,128)(2,1)S(1)} %get-tuple-element.80), channel_id=1, source_target_pairs={{0,80},{8,88},{64,16},{72,24},{1,81},{9,89},{65,17},{73,25},{2,82}... | collective-permute-start | bytes 393224 | tf_op jit(solution)/shard_map/cond/branch_0_fun/ppermute | solution.py:252
  15.4 3.1 %collective-permute-start.3 = (bf16[2,256,128]{2,1,0:T(8,128)(2,1)S(1)}, bf16[2,256,128]{2,1,0:T(8,128)(2,1)S(1)}, u32[]{:S(2)}, u32[]{:S(2)}) collective-permute-start(bf16[2,256,128]{2,1,0:T(8,128)(2,1)S(1)} %get-tuple-element.81), channel_id=1, source_target_pairs={{0,64},{8,72},{64,0},{72,8},{1,65},{9,73},{65,1},{73,9},{2,66},{10... | collective-permute-start | bytes 393224 | tf_op jit(solution)/shard_map/cond/branch_0_fun/ppermute | solution.py:252
  18.5 1.3 %collective-permute-start.4 = (bf16[2,256,128]{2,1,0:T(8,128)(2,1)S(1)}, bf16[2,256,128]{2,1,0:T(8,128)(2,1)S(1)}, u32[]{:S(2)}, u32[]{:S(2)}) collective-permute-start(bf16[2,256,128]{2,1,0:T(8,128)(2,1)S(1)} %get-tuple-element.82), channel_id=1, source_target_pairs={{0,48},{8,56},{64,112},{72,120},{1,49},{9,57},{65,113},{73,121},{2... | collective-permute-start | bytes 393224 | tf_op jit(solution)/shard_map/cond/branch_0_fun/ppermute | solution.py:252
  19.8 1.3 %collective-permute-start.5 = (bf16[2,256,128]{2,1,0:T(8,128)(2,1)S(1)}, bf16[2,256,128]{2,1,0:T(8,128)(2,1)S(1)}, u32[]{:S(2)}, u32[]{:S(2)}) collective-permute-start(bf16[2,256,128]{2,1,0:T(8,128)(2,1)S(1)} %get-tuple-element.83), channel_id=1, source_target_pairs={{0,32},{8,40},{64,96},{72,104},{1,33},{9,41},{65,97},{73,105},{2,3... | collective-permute-start | bytes 393224 | tf_op jit(solution)/shard_map/cond/branch_0_fun/ppermute | solution.py:252
  21.1 1.3 %collective-permute-start.6 = (bf16[2,256,128]{2,1,0:T(8,128)(2,1)S(1)}, bf16[2,256,128]{2,1,0:T(8,128)(2,1)S(1)}, u32[]{:S(2)}, u32[]{:S(2)}) collective-permute-start(bf16[2,256,128]{2,1,0:T(8,128)(2,1)S(1)} %get-tuple-element.84), channel_id=1, source_target_pairs={{0,16},{8,24},{64,80},{72,88},{1,17},{9,25},{65,81},{73,89},{2,18}... | collective-permute-start | bytes 393224 | tf_op jit(solution)/shard_map/cond/branch_0_fun/ppermute | solution.py:252
  22.4 2.6 %collective-permute-done.3 = bf16[2,256,128]{2,1,0:T(8,128)(2,1)S(1)} collective-permute-done((bf16[2,256,128]{2,1,0:T(8,128)(2,1)S(1)}, bf16[2,256,128]{2,1,0:T(8,128)(2,1)S(1)}, u32[]{:S(2)}, u32[]{:S(2)}) %collective-permute-start.3) | collective-permute-done | bytes 131104 | tf_op jit(solution)/shard_map/cond/branch_0_fun/ppermute | solution.py:252
  25.0 0.9 collective-permute-done.5
  25.9 2.8 %collective-permute-done.6 = bf16[2,256,128]{2,1,0:T(8,128)(2,1)S(1)} collective-permute-done((bf16[2,256,128]{2,1,0:T(8,128)(2,1)S(1)}, bf16[2,256,128]{2,1,0:T(8,128)(2,1)S(1)}, u32[]{:S(2)}, u32[]{:S(2)}) %collective-permute-start.6) | collective-permute-done | bytes 131104 | tf_op jit(solution)/shard_map/cond/branch_0_fun/ppermute | solution.py:252
  28.8 2.0 %collective-permute-start.31 = (bf16[2,4,640,128]{3,2,1,0:T(8,128)(2,1)}, bf16[2,4,640,128]{3,2,1,0:T(8,128)(2,1)S(1)}, u32[]{:S(2)}, u32[]{:S(2)}) collective-permute-start(bf16[2,4,640,128]{3,2,1,0:T(8,128)(2,1)} %get-tuple-element.181), channel_id=1, source_target_pairs={{0,1},{1,0},{2,3},{3,2},{4,5},{5,4},{6,7},{7,6},{8,9},{9,8},{10,11... | collective-permute-start | bytes 3932168 | tf_op jit(solution)/shard_map/ppermute | solution.py:268
  30.8 2.8 %collective-permute-start.28 = (bf16[2,256,128]{2,1,0:T(8,128)(2,1)S(1)}, bf16[2,256,128]{2,1,0:T(8,128)(2,1)S(1)}, u32[]{:S(2)}, u32[]{:S(2)}) collective-permute-start(bf16[2,256,128]{2,1,0:T(8,128)(2,1)S(1)} %get-tuple-element.233), channel_id=1, source_target_pairs={{0,8},{8,0},{16,24},{24,16},{32,40},{40,32},{48,56},{56,48},{64,72... | collective-permute-start | bytes 393224 | tf_op jit(solution)/shard_map/ppermute | solution.py:225
  33.5 3.8 %collective-permute-done.28 = bf16[2,256,128]{2,1,0:T(8,128)(2,1)S(1)} collective-permute-done((bf16[2,256,128]{2,1,0:T(8,128)(2,1)S(1)}, bf16[2,256,128]{2,1,0:T(8,128)(2,1)S(1)}, u32[]{:S(2)}, u32[]{:S(2)}) %collective-permute-start.28) | collective-permute-done | bytes 131104 | tf_op jit(solution)/shard_map/ppermute | solution.py:225
  37.3 2.3 %collective-permute-start.29 = (bf16[2,256,128]{2,1,0:T(8,128)(2,1)S(1)}, bf16[2,256,128]{2,1,0:T(8,128)(2,1)S(1)}, u32[]{:S(2)}, u32[]{:S(2)}) collective-permute-start(bf16[2,256,128]{2,1,0:T(8,128)(2,1)S(1)} %broadcast_select_fusion.refs_1_.refs_0_), channel_id=1, source_target_pairs={{0,16},{8,24},{16,32},{24,40},{32,48},{40,56},{48,64},{56,72},{64,... | collective-permute-start | bytes 393224 | tf_op jit(solution)/shard_map/ppermute | solution.py:221
  41.4 2.5 %shard_map.104.refs_2_ = f32[4,8,512]{2,1,0:T(8,128)S(1)} custom-call(s32[1]{0:T(128)S(6)} %copy.16.live_ref, s32[1]{0:T(128)S(6)} %copy.15.rows_ref, bf16[512,512]{1,0:T(8,128)(2,1)S(1)} %bitcast.25, bf16[512,512]{1,0:T(8,128)(2,1)S(1)} %bitcast.36, bf16[2,512,128]{2,1,0:T(8,128)(2,1)S(1)} %bitcast.47, ...), custom_call_target="tpu_custom_call" | custom-call | flops 805306368 | bytes 1048576 | tf_op jit(solution)/shard_map/pallas_call | solution.py:79
  44.0 1.1 collective-permute-start.32
  45.0 1.7 %collective-permute-start.33 = (bf16[2,256,128]{2,1,0:T(8,128)(2,1)S(1)}, bf16[2,256,128]{2,1,0:T(8,128)(2,1)S(1)}, u32[]{:S(2)}, u32[]{:S(2)}) collective-permute-start(bf16[2,256,128]{2,1,0:T(8,128)(2,1)S(1)} %collective-permute-done.30.refs_1_.refs_0_), channel_id=1, source_target_pairs={{0,112},{8,120},{16,0},{24,8},{32,16},{40,24},{48,32},{56,40},{64,... | collective-permute-start | bytes 393224 | tf_op jit(solution)/shard_map/ppermute | solution.py:221
  46.7 2.1 %shard_map.105.refs_2_ = f32[4,8,512]{2,1,0:T(8,128)S(1)} custom-call(s32[1]{0:T(128)S(6)} %copy.16.live_ref, s32[1]{0:T(128)S(6)} %copy.15.rows_ref, bf16[512,512]{1,0:T(8,128)(2,1)S(1)} %bitcast.26, bf16[512,512]{1,0:T(8,128)(2,1)S(1)} %bitcast.37, bf16[2,256,128]{2,1,0:T(8,128)(2,1)S(1)} %collective-permute-done.29.refs_0_.refs_1_, ...), custom_call_target="tpu_custom_call" | custom-call | flops 536870912 | bytes 1048576 | tf_op jit(solution)/shard_map/pallas_call | solution.py:79
  49.1 1.1 collective-permute-start.34
  50.2 1.6 %collective-permute-start.35 = (bf16[2,256,128]{2,1,0:T(8,128)(2,1)S(1)}, bf16[2,256,128]{2,1,0:T(8,128)(2,1)S(1)}, u32[]{:S(2)}, u32[]{:S(2)}) collective-permute-start(bf16[2,256,128]{2,1,0:T(8,128)(2,1)S(1)} %collective-permute-done.33.refs_1_.refs_0_), channel_id=1, source_target_pairs={{0,112},{8,120},{16,0},{24,8},{32,16},{40,24},{48,32},{56,40},{64,... | collective-permute-start | bytes 393224 | tf_op jit(solution)/shard_map/ppermute | solution.py:221
  51.8 2.1 %shard_map.106.refs_2_ = f32[4,8,512]{2,1,0:T(8,128)S(1)} custom-call(s32[1]{0:T(128)S(6)} %copy.16.live_ref, s32[1]{0:T(128)S(6)} %copy.15.rows_ref, bf16[512,512]{1,0:T(8,128)(2,1)S(1)} %bitcast.27, bf16[512,512]{1,0:T(8,128)(2,1)S(1)} %bitcast.38, bf16[2,256,128]{2,1,0:T(8,128)(2,1)S(1)} %collective-permute-done.32.refs_0_.refs_1_, ...), custom_call_target="tpu_custom_call" | custom-call | flops 536870912 | bytes 1048576 | tf_op jit(solution)/shard_map/pallas_call | solution.py:79
  54.1 2.7 %collective-permute-start.36 = (bf16[2,256,128]{2,1,0:T(8,128)(2,1)S(1)}, bf16[2,256,128]{2,1,0:T(8,128)(2,1)S(1)}, u32[]{:S(2)}, u32[]{:S(2)}) collective-permute-start(bf16[2,256,128]{2,1,0:T(8,128)(2,1)S(1)} %collective-permute-done.34.refs_0_.refs_1_), channel_id=1, source_target_pairs={{0,16},{8,24},{16,32},{24,40},{32,48},{40,56},{48,64},{56,72},{64,... | collective-permute-start | bytes 393224 | tf_op jit(solution)/shard_map/ppermute | solution.py:221
  56.8 2.1 %shard_map.107.refs_1_ = f32[4,8,512]{2,1,0:T(8,128)S(1)} custom-call(s32[1]{0:T(128)S(6)} %copy.16.live_ref, s32[1]{0:T(128)S(6)} %copy.15.rows_ref, bf16[512,512]{1,0:T(8,128)(2,1)S(1)} %bitcast.28, bf16[512,512]{1,0:T(8,128)(2,1)S(1)} %bitcast.39, bf16[2,256,128]{2,1,0:T(8,128)(2,1)S(1)} %collective-permute-done.34.refs_0_.refs_1_, ...), custom_call_target="tpu_custom_call" | custom-call | flops 536870912 | bytes 1048576 | tf_op jit(solution)/shard_map/pallas_call | solution.py:79
  59.2 1.5 %shard_map.108.stat_ref = f32[4,8,512]{2,1,0:T(8,128)S(1)} custom-call(s32[1]{0:T(128)S(6)} %copy.16.live_ref, s32[1]{0:T(128)S(6)} %copy.15.rows_ref, bf16[512,512]{1,0:T(8,128)(2,1)S(1)} %bitcast.29, bf16[512,512]{1,0:T(8,128)(2,1)S(1)} %bitcast.40, bf16[2,256,128]{2,1,0:T(8,128)(2,1)S(1)} %collective-permute-done.36.refs_0_, ...), custom_call_target="tpu_custom_call" | custom-call | flops 268435456 | bytes 1048576 | tf_op jit(solution)/shard_map/pallas_call | solution.py:79
  60.6 2.0 %shard_map.109 = (f32[512,512]{1,0:T(8,128)S(1)}, bf16[2,256,128]{2,1,0:T(8,128)(2,1)S(1)}) custom-call(s32[1]{0:T(128)S(6)} %copy.16.live_ref, s32[1]{0:T(128)S(6)} %copy.15.rows_ref, bf16[512,512]{1,0:T(8,128)(2,1)S(1)} %bitcast.30, bf16[512,512]{1,0:T(8,128)(2,1)S(1)} %bitcast.41, f32[4,8,512]{2,1,0:T(8,128)S(1)} %shard_map.108.stat_ref, ...), custom_call_target="tpu_custom_call" | custom-call | flops 671088640 | bytes 1048576 | tf_op jit(solution)/shard_map/pallas_call | solution.py:138
  62.6 1.7 %collective-permute-start.37 = (bf16[2,256,128]{2,1,0:T(8,128)(2,1)S(1)}, bf16[2,256,128]{2,1,0:T(8,128)(2,1)S(1)}, u32[]{:S(2)}, u32[]{:S(2)}) collective-permute-start(bf16[2,256,128]{2,1,0:T(8,128)(2,1)S(1)} %get-tuple-element.195), channel_id=1, source_target_pairs={{0,16},{8,24},{16,32},{24,40},{32,48},{40,56},{48,64},{56,72},{64,... | collective-permute-start | bytes 393224 | tf_op jit(solution)/shard_map/ppermute | solution.py:221
  64.3 3.3 %shard_map.110 = (f32[512,512]{1,0:T(8,128)S(1)}, bf16[2,256,128]{2,1,0:T(8,128)(2,1)S(1)}, bf16[2,256,128]{2,1,0:T(8,128)(2,1)S(1)}) custom-call(s32[1]{0:T(128)S(6)} %copy.16.live_ref, s32[1]{0:T(128)S(6)} %copy.15.rows_ref, bf16[512,512]{1,0:T(8,128)(2,1)S(1)} %bitcast.31, bf16[512,512]{1,0:T(8,128)(2,1)S(1)} %bitcast.42, ...), custom_call_target="tpu_custom_call" | custom-call | flops 1342177280 | bytes 1048576 | tf_op jit(solution)/shard_map/pallas_call | solution.py:138
  67.9 1.3 %collective-permute-start.38 = (bf16[2,256,128]{2,1,0:T(8,128)(2,1)S(1)}, bf16[2,256,128]{2,1,0:T(8,128)(2,1)S(1)}, u32[]{:S(2)}, u32[]{:S(2)}) collective-permute-start(bf16[2,256,128]{2,1,0:T(8,128)(2,1)S(1)} %add_convert_fusion.4), channel_id=1, source_target_pairs={{0,16},{8,24},{16,32},{24,40},{32,48},{40,56},{48,64},{56,72},{64,... | collective-permute-start | bytes 393224 | tf_op jit(solution)/shard_map/ppermute | solution.py:221
  69.3 1.4 %collective-permute-start.41 = (bf16[2,256,128]{2,1,0:T(8,128)(2,1)S(1)}, bf16[2,256,128]{2,1,0:T(8,128)(2,1)S(1)}, u32[]{:S(2)}, u32[]{:S(2)}) collective-permute-start(bf16[2,256,128]{2,1,0:T(8,128)(2,1)S(1)} %get-tuple-element.216), channel_id=1, source_target_pairs={{0,112},{8,120},{16,0},{24,8},{32,16},{40,24},{48,32},{56,40},{64,... | collective-permute-start | bytes 393224 | tf_op jit(solution)/shard_map/ppermute | solution.py:221
  70.7 3.3 %shard_map.111 = (f32[512,512]{1,0:T(8,128)S(1)}, bf16[2,256,128]{2,1,0:T(8,128)(2,1)S(1)}, bf16[2,256,128]{2,1,0:T(8,128)(2,1)S(1)}) custom-call(s32[1]{0:T(128)S(6)} %copy.16.live_ref, s32[1]{0:T(128)S(6)} %copy.15.rows_ref, bf16[512,512]{1,0:T(8,128)(2,1)S(1)} %bitcast.32, bf16[512,512]{1,0:T(8,128)(2,1)S(1)} %bitcast.43, ...), custom_call_target="tpu_custom_call" | custom-call | flops 1342177280 | bytes 1048576 | tf_op jit(solution)/shard_map/pallas_call | solution.py:138
  74.4 2.6 %collective-permute-start.42 = (bf16[2,256,128]{2,1,0:T(8,128)(2,1)S(1)}, bf16[2,256,128]{2,1,0:T(8,128)(2,1)S(1)}, u32[]{:S(2)}, u32[]{:S(2)}) collective-permute-start(bf16[2,256,128]{2,1,0:T(8,128)(2,1)S(1)} %add_convert_fusion.1), channel_id=1, source_target_pairs={{0,112},{8,120},{16,0},{24,8},{32,16},{40,24},{48,32},{56,40},{64,... | collective-permute-start | bytes 393224 | tf_op jit(solution)/shard_map/ppermute | solution.py:221
  76.9 3.3 %shard_map.112 = (f32[512,512]{1,0:T(8,128)S(1)}, bf16[2,256,128]{2,1,0:T(8,128)(2,1)S(1)}, bf16[2,256,128]{2,1,0:T(8,128)(2,1)S(1)}) custom-call(s32[1]{0:T(128)S(6)} %copy.16.live_ref, s32[1]{0:T(128)S(6)} %copy.15.rows_ref, bf16[512,512]{1,0:T(8,128)(2,1)S(1)} %bitcast.33, bf16[512,512]{1,0:T(8,128)(2,1)S(1)} %bitcast.44, ...), custom_call_target="tpu_custom_call" | custom-call | flops 1342177280 | bytes 1048576 | tf_op jit(solution)/shard_map/pallas_call | solution.py:138
  80.3 1.0 copy-done.4
  81.5 2.7 %collective-permute-start.43 = (bf16[2,256,128]{2,1,0:T(8,128)(2,1)S(1)}, bf16[2,256,128]{2,1,0:T(8,128)(2,1)S(1)}, u32[]{:S(2)}, u32[]{:S(2)}) collective-permute-start(bf16[2,256,128]{2,1,0:T(8,128)(2,1)S(1)} %add_convert_fusion), channel_id=1, source_target_pairs={{0,112},{8,120},{16,0},{24,8},{32,16},{40,24},{48,32},{56,40},{64,... | collective-permute-start | bytes 393224 | tf_op jit(solution)/shard_map/ppermute | solution.py:221
  84.2 1.2 copy-done.5
  85.4 2.0 %shard_map.113 = (f32[512,512]{1,0:T(8,128)S(1)}, bf16[2,256,128]{2,1,0:T(8,128)(2,1)S(1)}) custom-call(s32[1]{0:T(128)S(6)} %copy.16.live_ref, s32[1]{0:T(128)S(6)} %copy.15.rows_ref, bf16[512,512]{1,0:T(8,128)(2,1)S(1)} %bitcast.34, bf16[512,512]{1,0:T(8,128)(2,1)S(1)} %bitcast.45, f32[4,8,512]{2,1,0:T(8,128)S(1)} %shard_map.108.stat_ref, ...), custom_call_target="tpu_custom_call" | custom-call | flops 671088640 | bytes 1048576 | tf_op jit(solution)/shard_map/pallas_call | solution.py:138
  87.5 2.8 %collective-permute-start.44 = (bf16[2,128,128]{2,1,0:T(8,128)(2,1)S(1)}, bf16[2,128,128]{2,1,0:T(8,128)(2,1)S(1)}, u32[]{:S(2)}, u32[]{:S(2)}) collective-permute-start(bf16[2,128,128]{2,1,0:T(8,128)(2,1)S(1)} %add_convert_fusion.6), channel_id=1, source_target_pairs={{0,8},{8,0},{16,24},{24,16},{32,40},{40,32},{48,56},{56,48},{64,72... | collective-permute-start | bytes 196616 | tf_op jit(solution)/shard_map/ppermute | solution.py:225
  90.3 4.5 %shard_map.114 = (bf16[512,512]{1,0:T(8,128)(2,1)}, bf16[2,512,128]{2,1,0:T(8,128)(2,1)}) custom-call(s32[1]{0:T(128)S(6)} %copy.16.live_ref, s32[1]{0:T(128)S(6)} %copy.15.rows_ref, bf16[512,512]{1,0:T(8,128)(2,1)S(1)} %bitcast.35, bf16[512,512]{1,0:T(8,128)(2,1)S(1)} %bitcast.46, f32[4,8,512]{2,1,0:T(8,128)S(1)} %shard_map.108.stat_ref, ...), custom_call_target="tpu_custom_call" | custom-call | flops 1342177280 | bytes 1048576 | tf_op jit(solution)/shard_map/pallas_call | solution.py:138
  94.9 9.3 %collective-permute-start.45 = (bf16[2,128,128]{2,1,0:T(8,128)(2,1)S(1)}, bf16[2,128,128]{2,1,0:T(8,128)(2,1)S(1)}, u32[]{:S(2)}, u32[]{:S(2)}) collective-permute-start(bf16[2,128,128]{2,1,0:T(8,128)(2,1)S(1)} %add_convert_fusion.5.summed_ref), channel_id=1, source_target_pairs={{0,1},{1,0},{2,3},{3,2},{4,5},{5,4},{6,7},{7,6},{8,9},{9,8},{10,11... | collective-permute-start | bytes 196616 | tf_op jit(solution)/shard_map/ppermute | solution.py:308
  104.2 0.9 collective-permute-done.45.beside_ref
  105.1 2.8 %shard_map.115 = bf16[4,128,640]{2,1,0:T(8,128)(2,1)S(1)} custom-call(bf16[2,128,128]{2,1,0:T(8,128)(2,1)S(1)} %add_convert_fusion.5.summed_ref, bf16[2,128,128]{2,1,0:T(8,128)(2,1)S(1)} %collective-permute-done.45.beside_ref, bf16[2,4,2,640,128]{4,3,2,1,0:T(8,128)(2,1)S(1)} %bitcast.24, bf16[2,4,640,128]{3,2,1,0:T(8,128)(2,1)S(1)} %collective-permute-done.31.other_ref), custom_call_target="tpu_custom_call" | custom-call | tf_op jit(solution)/shard_map/pallas_call | solution.py:201
  108.0 2.8 %collective-permute-start.48 = (bf16[128,640]{1,0:T(8,128)(2,1)S(1)}, bf16[128,640]{1,0:T(8,128)(2,1)S(1)}, u32[]{:S(2)}, u32[]{:S(2)}) collective-permute-start(bf16[128,640]{1,0:T(8,128)(2,1)S(1)} %get-tuple-element.231), channel_id=1, source_target_pairs={{0,6},{1,7},{2,0},{3,1},{4,2},{5,3},{6,4},{7,5},{8,14},{9,15},{10,... | collective-permute-start | bytes 491528 | tf_op jit(solution)/shard_map/ppermute | solution.py:312
  111.1 0.7 collective-permute-start.46
  111.8 5.6 %collective-permute-done.48 = bf16[128,640]{1,0:T(8,128)(2,1)S(1)} collective-permute-done((bf16[128,640]{1,0:T(8,128)(2,1)S(1)}, bf16[128,640]{1,0:T(8,128)(2,1)S(1)}, u32[]{:S(2)}, u32[]{:S(2)}) %collective-permute-start.48) | collective-permute-done | bytes 163872 | tf_op jit(solution)/shard_map/ppermute | solution.py:312
  117.4 4.5 %collective-permute-done.46 = bf16[128,640]{1,0:T(8,128)(2,1)S(1)} collective-permute-done((bf16[128,640]{1,0:T(8,128)(2,1)S(1)}, bf16[128,640]{1,0:T(8,128)(2,1)S(1)}, u32[]{:S(2)}, u32[]{:S(2)}) %collective-permute-start.46) | collective-permute-done | bytes 163872 | tf_op jit(solution)/shard_map/ppermute | solution.py:312
  121.9 0.8 fusion.2
  (45 shorter events, 2.7 us)
Async XLA Ops:
  4.3 37.1 %copy-start.1 = (bf16[1,512,512]{2,1,0:T(8,128)(2,1)S(1)}, bf16[1,512,512]{2,1,0:T(8,128)(2,1)}, u32[]{:S(2)}) copy-start(bf16[1,512,512]{2,1,0:T(8,128)(2,1)} %param.12) | copy-start | bytes 1572868
  4.3 37.1 %copy-start.2 = (bf16[1,512,512]{2,1,0:T(8,128)(2,1)S(1)}, bf16[1,512,512]{2,1,0:T(8,128)(2,1)}, u32[]{:S(2)}) copy-start(bf16[1,512,512]{2,1,0:T(8,128)(2,1)} %param.14) | copy-start | bytes 1572868
  4.3 37.1 %copy-start.3 = (bf16[1,2,512,128]{3,2,1,0:T(8,128)(2,1)S(1)}, bf16[1,2,512,128]{3,2,1,0:T(8,128)(2,1)}, u32[]{:S(2)}) copy-start(bf16[1,2,512,128]{3,2,1,0:T(8,128)(2,1)} %param.13) | copy-start | bytes 786436
  4.3 15.5 %collective-permute-start = (bf16[2,256,128]{2,1,0:T(8,128)(2,1)S(1)}, bf16[2,256,128]{2,1,0:T(8,128)(2,1)S(1)}, u32[]{:S(2)}, u32[]{:S(2)}) collective-permute-start(bf16[2,256,128]{2,1,0:T(8,128)(2,1)S(1)} %get-tuple-element.61), channel_id=1, source_target_pairs={{0,112},{8,120},{64,48},{72,56},{1,113},{9,121},{65,49},{73,57},{2... | collective-permute-start | bytes 393224 | tf_op jit(solution)/shard_map/cond/branch_0_fun/ppermute | solution.py:252
  12.8 8.3 %collective-permute-start.1 = (bf16[2,256,128]{2,1,0:T(8,128)(2,1)S(1)}, bf16[2,256,128]{2,1,0:T(8,128)(2,1)S(1)}, u32[]{:S(2)}, u32[]{:S(2)}) collective-permute-start(bf16[2,256,128]{2,1,0:T(8,128)(2,1)S(1)} %get-tuple-element.62), channel_id=1, source_target_pairs={{0,96},{8,104},{64,32},{72,40},{1,97},{9,105},{65,33},{73,41},{2,9... | collective-permute-start | bytes 393224 | tf_op jit(solution)/shard_map/cond/branch_0_fun/ppermute | solution.py:252
  14.1 8.3 %collective-permute-start.2 = (bf16[2,256,128]{2,1,0:T(8,128)(2,1)S(1)}, bf16[2,256,128]{2,1,0:T(8,128)(2,1)S(1)}, u32[]{:S(2)}, u32[]{:S(2)}) collective-permute-start(bf16[2,256,128]{2,1,0:T(8,128)(2,1)S(1)} %get-tuple-element.80), channel_id=1, source_target_pairs={{0,80},{8,88},{64,16},{72,24},{1,81},{9,89},{65,17},{73,25},{2,82}... | collective-permute-start | bytes 393224 | tf_op jit(solution)/shard_map/cond/branch_0_fun/ppermute | solution.py:252
  15.4 9.6 %collective-permute-start.3 = (bf16[2,256,128]{2,1,0:T(8,128)(2,1)S(1)}, bf16[2,256,128]{2,1,0:T(8,128)(2,1)S(1)}, u32[]{:S(2)}, u32[]{:S(2)}) collective-permute-start(bf16[2,256,128]{2,1,0:T(8,128)(2,1)S(1)} %get-tuple-element.81), channel_id=1, source_target_pairs={{0,64},{8,72},{64,0},{72,8},{1,65},{9,73},{65,1},{73,9},{2,66},{10... | collective-permute-start | bytes 393224 | tf_op jit(solution)/shard_map/cond/branch_0_fun/ppermute | solution.py:252
  18.5 6.5 %collective-permute-start.4 = (bf16[2,256,128]{2,1,0:T(8,128)(2,1)S(1)}, bf16[2,256,128]{2,1,0:T(8,128)(2,1)S(1)}, u32[]{:S(2)}, u32[]{:S(2)}) collective-permute-start(bf16[2,256,128]{2,1,0:T(8,128)(2,1)S(1)} %get-tuple-element.82), channel_id=1, source_target_pairs={{0,48},{8,56},{64,112},{72,120},{1,49},{9,57},{65,113},{73,121},{2... | collective-permute-start | bytes 393224 | tf_op jit(solution)/shard_map/cond/branch_0_fun/ppermute | solution.py:252
  19.8 6.1 %collective-permute-start.5 = (bf16[2,256,128]{2,1,0:T(8,128)(2,1)S(1)}, bf16[2,256,128]{2,1,0:T(8,128)(2,1)S(1)}, u32[]{:S(2)}, u32[]{:S(2)}) collective-permute-start(bf16[2,256,128]{2,1,0:T(8,128)(2,1)S(1)} %get-tuple-element.83), channel_id=1, source_target_pairs={{0,32},{8,40},{64,96},{72,104},{1,33},{9,41},{65,97},{73,105},{2,3... | collective-permute-start | bytes 393224 | tf_op jit(solution)/shard_map/cond/branch_0_fun/ppermute | solution.py:252
  21.1 7.6 %collective-permute-start.6 = (bf16[2,256,128]{2,1,0:T(8,128)(2,1)S(1)}, bf16[2,256,128]{2,1,0:T(8,128)(2,1)S(1)}, u32[]{:S(2)}, u32[]{:S(2)}) collective-permute-start(bf16[2,256,128]{2,1,0:T(8,128)(2,1)S(1)} %get-tuple-element.84), channel_id=1, source_target_pairs={{0,16},{8,24},{64,80},{72,88},{1,17},{9,25},{65,81},{73,89},{2,18}... | collective-permute-start | bytes 393224 | tf_op jit(solution)/shard_map/cond/branch_0_fun/ppermute | solution.py:252
  28.8 15.2 %collective-permute-start.31 = (bf16[2,4,640,128]{3,2,1,0:T(8,128)(2,1)}, bf16[2,4,640,128]{3,2,1,0:T(8,128)(2,1)S(1)}, u32[]{:S(2)}, u32[]{:S(2)}) collective-permute-start(bf16[2,4,640,128]{3,2,1,0:T(8,128)(2,1)} %get-tuple-element.181), channel_id=1, source_target_pairs={{0,1},{1,0},{2,3},{3,2},{4,5},{5,4},{6,7},{7,6},{8,9},{9,8},{10,11... | collective-permute-start | bytes 3932168 | tf_op jit(solution)/shard_map/ppermute | solution.py:268
  30.8 6.6 %collective-permute-start.28 = (bf16[2,256,128]{2,1,0:T(8,128)(2,1)S(1)}, bf16[2,256,128]{2,1,0:T(8,128)(2,1)S(1)}, u32[]{:S(2)}, u32[]{:S(2)}) collective-permute-start(bf16[2,256,128]{2,1,0:T(8,128)(2,1)S(1)} %get-tuple-element.233), channel_id=1, source_target_pairs={{0,8},{8,0},{16,24},{24,16},{32,40},{40,32},{48,56},{56,48},{64,72... | collective-permute-start | bytes 393224 | tf_op jit(solution)/shard_map/ppermute | solution.py:225
  37.3 6.6 %collective-permute-start.29 = (bf16[2,256,128]{2,1,0:T(8,128)(2,1)S(1)}, bf16[2,256,128]{2,1,0:T(8,128)(2,1)S(1)}, u32[]{:S(2)}, u32[]{:S(2)}) collective-permute-start(bf16[2,256,128]{2,1,0:T(8,128)(2,1)S(1)} %broadcast_select_fusion.refs_1_.refs_0_), channel_id=1, source_target_pairs={{0,16},{8,24},{16,32},{24,40},{32,48},{40,56},{48,64},{56,72},{64,... | collective-permute-start | bytes 393224 | tf_op jit(solution)/shard_map/ppermute | solution.py:221
  39.6 4.3 %collective-permute-start.30 = (bf16[2,256,128]{2,1,0:T(8,128)(2,1)S(1)}, bf16[2,256,128]{2,1,0:T(8,128)(2,1)S(1)}, u32[]{:S(2)}, u32[]{:S(2)}) collective-permute-start(bf16[2,256,128]{2,1,0:T(8,128)(2,1)S(1)} %broadcast_select_fusion.refs_1_.refs_0_), channel_id=1, source_target_pairs={{0,112},{8,120},{16,0},{24,8},{32,16},{40,24},{48,32},{56,40},{64,... | collective-permute-start | bytes 393224 | tf_op jit(solution)/shard_map/ppermute | solution.py:221
  44.0 5.1 %collective-permute-start.32 = (bf16[2,256,128]{2,1,0:T(8,128)(2,1)S(1)}, bf16[2,256,128]{2,1,0:T(8,128)(2,1)S(1)}, u32[]{:S(2)}, u32[]{:S(2)}) collective-permute-start(bf16[2,256,128]{2,1,0:T(8,128)(2,1)S(1)} %collective-permute-done.29.refs_0_.refs_1_), channel_id=1, source_target_pairs={{0,16},{8,24},{16,32},{24,40},{32,48},{40,56},{48,64},{56,72},{64,... | collective-permute-start | bytes 393224 | tf_op jit(solution)/shard_map/ppermute | solution.py:221
  45.0 4.0 %collective-permute-start.33 = (bf16[2,256,128]{2,1,0:T(8,128)(2,1)S(1)}, bf16[2,256,128]{2,1,0:T(8,128)(2,1)S(1)}, u32[]{:S(2)}, u32[]{:S(2)}) collective-permute-start(bf16[2,256,128]{2,1,0:T(8,128)(2,1)S(1)} %collective-permute-done.30.refs_1_.refs_0_), channel_id=1, source_target_pairs={{0,112},{8,120},{16,0},{24,8},{32,16},{40,24},{48,32},{56,40},{64,... | collective-permute-start | bytes 393224 | tf_op jit(solution)/shard_map/ppermute | solution.py:221
  49.1 5.0 %collective-permute-start.34 = (bf16[2,256,128]{2,1,0:T(8,128)(2,1)S(1)}, bf16[2,256,128]{2,1,0:T(8,128)(2,1)S(1)}, u32[]{:S(2)}, u32[]{:S(2)}) collective-permute-start(bf16[2,256,128]{2,1,0:T(8,128)(2,1)S(1)} %collective-permute-done.32.refs_0_.refs_1_), channel_id=1, source_target_pairs={{0,16},{8,24},{16,32},{24,40},{32,48},{40,56},{48,64},{56,72},{64,... | collective-permute-start | bytes 393224 | tf_op jit(solution)/shard_map/ppermute | solution.py:221
  50.2 4.0 %collective-permute-start.35 = (bf16[2,256,128]{2,1,0:T(8,128)(2,1)S(1)}, bf16[2,256,128]{2,1,0:T(8,128)(2,1)S(1)}, u32[]{:S(2)}, u32[]{:S(2)}) collective-permute-start(bf16[2,256,128]{2,1,0:T(8,128)(2,1)S(1)} %collective-permute-done.33.refs_1_.refs_0_), channel_id=1, source_target_pairs={{0,112},{8,120},{16,0},{24,8},{32,16},{40,24},{48,32},{56,40},{64,... | collective-permute-start | bytes 393224 | tf_op jit(solution)/shard_map/ppermute | solution.py:221
  54.1 5.0 %collective-permute-start.36 = (bf16[2,256,128]{2,1,0:T(8,128)(2,1)S(1)}, bf16[2,256,128]{2,1,0:T(8,128)(2,1)S(1)}, u32[]{:S(2)}, u32[]{:S(2)}) collective-permute-start(bf16[2,256,128]{2,1,0:T(8,128)(2,1)S(1)} %collective-permute-done.34.refs_0_.refs_1_), channel_id=1, source_target_pairs={{0,16},{8,24},{16,32},{24,40},{32,48},{40,56},{48,64},{56,72},{64,... | collective-permute-start | bytes 393224 | tf_op jit(solution)/shard_map/ppermute | solution.py:221
  62.6 5.3 %collective-permute-start.37 = (bf16[2,256,128]{2,1,0:T(8,128)(2,1)S(1)}, bf16[2,256,128]{2,1,0:T(8,128)(2,1)S(1)}, u32[]{:S(2)}, u32[]{:S(2)}) collective-permute-start(bf16[2,256,128]{2,1,0:T(8,128)(2,1)S(1)} %get-tuple-element.195), channel_id=1, source_target_pairs={{0,16},{8,24},{16,32},{24,40},{32,48},{40,56},{48,64},{56,72},{64,... | collective-permute-start | bytes 393224 | tf_op jit(solution)/shard_map/ppermute | solution.py:221
  67.9 6.1 %collective-permute-start.38 = (bf16[2,256,128]{2,1,0:T(8,128)(2,1)S(1)}, bf16[2,256,128]{2,1,0:T(8,128)(2,1)S(1)}, u32[]{:S(2)}, u32[]{:S(2)}) collective-permute-start(bf16[2,256,128]{2,1,0:T(8,128)(2,1)S(1)} %add_convert_fusion.4), channel_id=1, source_target_pairs={{0,16},{8,24},{16,32},{24,40},{32,48},{40,56},{48,64},{56,72},{64,... | collective-permute-start | bytes 393224 | tf_op jit(solution)/shard_map/ppermute | solution.py:221
  69.3 5.1 %collective-permute-start.41 = (bf16[2,256,128]{2,1,0:T(8,128)(2,1)S(1)}, bf16[2,256,128]{2,1,0:T(8,128)(2,1)S(1)}, u32[]{:S(2)}, u32[]{:S(2)}) collective-permute-start(bf16[2,256,128]{2,1,0:T(8,128)(2,1)S(1)} %get-tuple-element.216), channel_id=1, source_target_pairs={{0,112},{8,120},{16,0},{24,8},{32,16},{40,24},{48,32},{56,40},{64,... | collective-permute-start | bytes 393224 | tf_op jit(solution)/shard_map/ppermute | solution.py:221
  74.1 7.2 %collective-permute-start.39 = (bf16[2,256,128]{2,1,0:T(8,128)(2,1)S(1)}, bf16[2,256,128]{2,1,0:T(8,128)(2,1)S(1)}, u32[]{:S(2)}, u32[]{:S(2)}) collective-permute-start(bf16[2,256,128]{2,1,0:T(8,128)(2,1)S(1)} %add_convert_fusion.3), channel_id=1, source_target_pairs={{0,16},{8,24},{16,32},{24,40},{32,48},{40,56},{48,64},{56,72},{64,... | collective-permute-start | bytes 393224 | tf_op jit(solution)/shard_map/ppermute | solution.py:221
  74.4 7.0 %collective-permute-start.42 = (bf16[2,256,128]{2,1,0:T(8,128)(2,1)S(1)}, bf16[2,256,128]{2,1,0:T(8,128)(2,1)S(1)}, u32[]{:S(2)}, u32[]{:S(2)}) collective-permute-start(bf16[2,256,128]{2,1,0:T(8,128)(2,1)S(1)} %add_convert_fusion.1), channel_id=1, source_target_pairs={{0,112},{8,120},{16,0},{24,8},{32,16},{40,24},{48,32},{56,40},{64,... | collective-permute-start | bytes 393224 | tf_op jit(solution)/shard_map/ppermute | solution.py:221
  80.2 1.0 copy-start.4
  81.3 6.1 %collective-permute-start.40 = (bf16[2,256,128]{2,1,0:T(8,128)(2,1)S(1)}, bf16[2,256,128]{2,1,0:T(8,128)(2,1)S(1)}, u32[]{:S(2)}, u32[]{:S(2)}) collective-permute-start(bf16[2,256,128]{2,1,0:T(8,128)(2,1)S(1)} %add_convert_fusion.2), channel_id=1, source_target_pairs={{0,16},{8,24},{16,32},{24,40},{32,48},{40,56},{48,64},{56,72},{64,... | collective-permute-start | bytes 393224 | tf_op jit(solution)/shard_map/ppermute | solution.py:221
  81.5 6.0 %collective-permute-start.43 = (bf16[2,256,128]{2,1,0:T(8,128)(2,1)S(1)}, bf16[2,256,128]{2,1,0:T(8,128)(2,1)S(1)}, u32[]{:S(2)}, u32[]{:S(2)}) collective-permute-start(bf16[2,256,128]{2,1,0:T(8,128)(2,1)S(1)} %add_convert_fusion), channel_id=1, source_target_pairs={{0,112},{8,120},{16,0},{24,8},{32,16},{40,24},{48,32},{56,40},{64,... | collective-permute-start | bytes 393224 | tf_op jit(solution)/shard_map/ppermute | solution.py:221
  84.2 1.2 copy-start.5
  87.5 7.4 %collective-permute-start.44 = (bf16[2,128,128]{2,1,0:T(8,128)(2,1)S(1)}, bf16[2,128,128]{2,1,0:T(8,128)(2,1)S(1)}, u32[]{:S(2)}, u32[]{:S(2)}) collective-permute-start(bf16[2,128,128]{2,1,0:T(8,128)(2,1)S(1)} %add_convert_fusion.6), channel_id=1, source_target_pairs={{0,8},{8,0},{16,24},{24,16},{32,40},{40,32},{48,56},{56,48},{64,72... | collective-permute-start | bytes 196616 | tf_op jit(solution)/shard_map/ppermute | solution.py:225
  90.3 14.8 %copy-start = (bf16[2,5120,128]{2,1,0:T(8,128)(2,1)S(1)}, bf16[2,5120,128]{2,1,0:T(8,128)(2,1)}, u32[]{:S(2)}) copy-start(bf16[2,5120,128]{2,1,0:T(8,128)(2,1)} %param.16) | copy-start | bytes 7864324
  94.9 10.2 %collective-permute-start.45 = (bf16[2,128,128]{2,1,0:T(8,128)(2,1)S(1)}, bf16[2,128,128]{2,1,0:T(8,128)(2,1)S(1)}, u32[]{:S(2)}, u32[]{:S(2)}) collective-permute-start(bf16[2,128,128]{2,1,0:T(8,128)(2,1)S(1)} %add_convert_fusion.5.summed_ref), channel_id=1, source_target_pairs={{0,1},{1,0},{2,3},{3,2},{4,5},{5,4},{6,7},{7,6},{8,9},{9,8},{10,11... | collective-permute-start | bytes 196616 | tf_op jit(solution)/shard_map/ppermute | solution.py:308
  108.0 9.4 %collective-permute-start.48 = (bf16[128,640]{1,0:T(8,128)(2,1)S(1)}, bf16[128,640]{1,0:T(8,128)(2,1)S(1)}, u32[]{:S(2)}, u32[]{:S(2)}) collective-permute-start(bf16[128,640]{1,0:T(8,128)(2,1)S(1)} %get-tuple-element.231), channel_id=1, source_target_pairs={{0,6},{1,7},{2,0},{3,1},{4,2},{5,3},{6,4},{7,5},{8,14},{9,15},{10,... | collective-permute-start | bytes 491528 | tf_op jit(solution)/shard_map/ppermute | solution.py:312
  110.8 6.7 %collective-permute-start.47 = (bf16[128,640]{1,0:T(8,128)(2,1)S(1)}, bf16[128,640]{1,0:T(8,128)(2,1)S(1)}, u32[]{:S(2)}, u32[]{:S(2)}) collective-permute-start(bf16[128,640]{1,0:T(8,128)(2,1)S(1)} %get-tuple-element.232), channel_id=1, source_target_pairs={{0,4},{1,5},{2,6},{3,7},{4,0},{5,1},{6,2},{7,3},{8,12},{9,13},{10,... | collective-permute-start | bytes 491528 | tf_op jit(solution)/shard_map/ppermute | solution.py:312
  111.1 10.8 %collective-permute-start.46 = (bf16[128,640]{1,0:T(8,128)(2,1)S(1)}, bf16[128,640]{1,0:T(8,128)(2,1)S(1)}, u32[]{:S(2)}, u32[]{:S(2)}) collective-permute-start(bf16[128,640]{1,0:T(8,128)(2,1)S(1)} %get-tuple-element.230), channel_id=1, source_target_pairs={{0,2},{1,3},{2,4},{3,5},{4,6},{5,7},{6,0},{7,1},{8,10},{9,11},{10,... | collective-permute-start | bytes 491528 | tf_op jit(solution)/shard_map/ppermute | solution.py:312
where the time goes:
time: 123 us
  starting transfers between devices  59.7 us (49%)
  Pallas kernels  34.4 us (28%)
  waiting for transfers between devices  22.1 us (18%)
  between operations  2.92 us (2%)
  local copies, waits for them, and re-layouts  2.31 us (2%)
    ppermute x14, starting transfers between devices, z_hop(): return lax.ppermute(x, 'group', ring(2 * SPLIT, step, 2))  21 us
    pallas_call x6, Pallas kernels, backward(): pl.pallas_call(functools.partial(backward_kernel, kinds, scale, scale2, f...  18.4 us
    ppermute x7, starting transfers between devices, body(): got[step] = lax.ppermute(pieces[step], 'group', pairs)  18 us
    pallas_call x5, Pallas kernels, forward(): pl.pallas_call(functools.partial(forward_kernel, kinds, scale2, first, la...  10.3 us
    ppermute x3, waiting for transfers between devices, on_device(): lax.ppermute(shares[k], 'tensor', ring(8, k, 2)).astype(jnp.float32)  10.1 us
    ppermute x1, starting transfers between devices, on_device(): beside = lax.ppermute(summed, 'tensor', swap(8))  9.29 us
    ppermute x7, waiting for transfers between devices, body(): got[step] = lax.ppermute(pieces[step], 'group', pairs)  6.3 us
    ppermute x2, starting transfers between devices, x_swap(): return lax.ppermute(x, 'group', swap(2 * SPLIT))  5.6 us
  transfers between devices with their start and end apart: 28, of which 12 were waited for; matrix products, arithmetic and copies ran while one was open for 0% of the time, Pallas kernels for 21%

commit v1 on v0

--- a/solution.py
+++ b/solution.py
@@ -37,7 +37,7 @@
     out_ref = refs[-1]
     dh = q_ref.shape[1] // heads
 
-    @pl.loop(0, heads)
+    @pl.loop(0, heads, unroll=2)
     def _(h):
         cols = pl.ds(pl.multiple_of(h * dh, dh), dh)
         q = q_ref[:, cols]
@@ -82,7 +82,7 @@
         out_specs=VMEM,
         out_shape=jax.ShapeDtypeStruct((heads, 8, rows), jnp.float32),
         cost_estimate=pl.CostEstimate(flops=4 * heads * rows * keys * dh, bytes_accessed=4 * q.size, transcendentals=heads * rows * keys),
-        compiler_params=pltpu.CompilerParams(vmem_limit_bytes=24 * 2**20),
+        compiler_params=pltpu.CompilerParams(vmem_limit_bytes=16 * 2**20),
     )(*lens, q, g, *blocks, *([] if first else [stats]))
 
 
@@ -96,7 +96,7 @@
     for acc in accs:
         acc[...] = jnp.zeros_like(acc)
 
-    @pl.loop(0, heads)
+    @pl.loop(0, heads, unroll=2)
     def _(h):
         cols = pl.ds(pl.multiple_of(h * dh, dh), dh)
         q = q_ref[:, cols]
@@ -142,37 +142,54 @@
         out_shape=[dq_shape] + [jax.ShapeDtypeStruct(b.shape, jnp.bfloat16) for b in blocks],
         scratch_shapes=[pltpu.VMEM(b.shape, jnp.float32) for b in blocks],
         cost_estimate=pl.CostEstimate(flops=10 * heads * rows * keys * dh, bytes_accessed=4 * q.size, transcendentals=heads * rows * keys),
-        compiler_params=pltpu.CompilerParams(vmem_limit_bytes=24 * 2**20),
+        compiler_params=pltpu.CompilerParams(vmem_limit_bytes=16 * 2**20),
     )(*lens, q, g, stats, *blocks, *([] if first else [dq]))
     return res[0], list(res[1:])
 
 
-def cut_kernel(keys, prefix_ref, weight_ref, *refs):
-    outs, lent_ref, sems = refs[:SPLIT], refs[SPLIT], refs[SPLIT + 1]
+def cut_kernel(keys, prefix_ref, *refs):
+    outs, sems = refs[:SPLIT], refs[SPLIT]
     z = lax.axis_index("group") // 2
-    core = lax.rem(lax.axis_index("tensor"), 2)
     copies = []
     for step in (4, 3, 5, 2, 6, 1, 7, 0):
         at = pl.multiple_of(lax.rem(z + step, SPLIT) * keys, keys)
         copies.append(pltpu.make_async_copy(prefix_ref.at[:, pl.ds(at, keys), :], outs[step], sems.at[step]))
-    copies.append(pltpu.make_async_copy(weight_ref.at[:, :, 1 - core], lent_ref, sems.at[SPLIT]))
     for copy in copies:
         copy.start()
     for copy in copies:
         copy.wait()
 
 
-def cut(prefix, by_core, keys):
+def cut(prefix, keys):
     shape = (prefix.shape[0], keys, prefix.shape[2])
-    lent = by_core.shape[:2] + by_core.shape[3:]
-    res = pl.pallas_call(
+    return pl.pallas_call(
         functools.partial(cut_kernel, keys),
-        in_specs=[ANY] * 2,
-        out_specs=[ANY] * SPLIT + [VMEM],
-        out_shape=[jax.ShapeDtypeStruct(shape, prefix.dtype)] * SPLIT + [jax.ShapeDtypeStruct(lent, by_core.dtype)],
-        scratch_shapes=[pltpu.SemaphoreType.DMA((SPLIT + 1,))],
-    )(prefix, by_core)
-    return res[:SPLIT], res[SPLIT]
+        in_specs=[ANY],
+        out_specs=[ANY] * SPLIT,
+        out_shape=[jax.ShapeDtypeStruct(shape, prefix.dtype)] * SPLIT,
+        scratch_shapes=[pltpu.SemaphoreType.DMA((SPLIT,))],
+    )(prefix)
+
+
+def lend_kernel(weight_ref, out_ref, sems):
+    core = lax.rem(lax.axis_index("tensor"), 2)
+    copies = []
+    for at in range(4):
+        copies.append(pltpu.make_async_copy(weight_ref.at[:, at, 1 - core], out_ref.at[:, at], sems.at[at]))
+        copies[-1].start()
+    for copy in copies:
+        copy.wait()
+
+
+def lend(by_core):
+    shape = by_core.shape[:2] + by_core.shape[3:]
+    return pl.pallas_call(
+        lend_kernel,
+        in_specs=[ANY],
+        out_specs=VMEM,
+        out_shape=jax.ShapeDtypeStruct(shape, by_core.dtype),
+        scratch_shapes=[pltpu.SemaphoreType.DMA((4,))],
+    )(by_core)
 
 
 def project_kernel(summed_ref, beside_ref, weight_ref, other_ref, out_ref, held_ref, sems):
@@ -204,7 +221,7 @@
         out_specs=VMEM,
         out_shape=jax.ShapeDtypeStruct((4, summed.shape[1], cols), jnp.bfloat16),
         scratch_shapes=[pltpu.VMEM((4, 2, 2, cols, dh), by_core.dtype), pltpu.SemaphoreType.DMA((4, 2))],
-        compiler_params=pltpu.CompilerParams(vmem_limit_bytes=24 * 2**20),
+        compiler_params=pltpu.CompilerParams(vmem_limit_bytes=16 * 2**20),
     )(summed, beside, by_core, other)
 
 
@@ -257,9 +274,10 @@
 
         return body
 
-    pieces, lent = cut(prefix, by_core, keys)
-    held = lax.switch(lax.rem(owner_z, half_way), [branch(k) for k in range(half_way)], *pieces)
-    held = jnp.where(x == owner[0] % 2, held, x_swap(held))
+    held = lax.switch(lax.rem(owner_z, half_way), [branch(k) for k in range(half_way)], *cut(prefix, keys))
+    held, by_core = lax.optimization_barrier((held, by_core))
+    swapped, lent = lax.optimization_barrier((x_swap(held), lend(by_core)))
+    held = jnp.where(x == owner[0] % 2, held, swapped)
 
     pieces = {0: held}
     new = [0]

time: 123 us -> 120 us (0.976)
  Pallas kernels: 34.4 us -> 31.7 us
    ppermute x2, waiting for transfers between devices: 3.8 us -> 0.18 us  [x_swap(): return lax.ppermute(x, 'group', swap(2 * SPLIT))]
    ppermute x14, waiting for transfers between devices: 0.99 us -> 4.28 us  [z_hop(): return lax.ppermute(x, 'group', ring(2 * SPLIT, step, 2))]
    pallas_call x6, Pallas kernels: 18.4 us -> 16.2 us  [backward(): pl.pallas_call(functools.partial(backward_kernel, kinds, scale, scale2, f...]
    pallas_call x5, Pallas kernels: 10.3 us -> 8.97 us  [forward(): pl.pallas_call(functools.partial(forward_kernel, kinds, scale2, first, la...]
    pallas_call x1 -> x2, Pallas kernels: 2.94 us -> 3.77 us  [the longest x1 2.39 us: lend(): pl.pallas_call(lend_kernel, in_specs=[ANY], out_specs=VMEM, out_shape=jax...]
  transfers between devices with their start and end apart: 28 -> 28, of which waited for: 12 -> 17; matrix products, arithmetic and copies ran while one was open for 0% -> 0% of each run, Pallas kernels for 21% -> 21%
where the time goes in v1:
time: 120 us
  starting transfers between devices  59.6 us (50%)
  Pallas kernels  31.7 us (26%)
  waiting for transfers between devices  21.8 us (18%)
  between operations  2.9 us (2%)
  local copies, waits for them, and re-layouts  2.31 us (2%)
    ppermute x14, starting transfers between devices, z_hop(): return lax.ppermute(x, 'group', ring(2 * SPLIT, step, 2))  20.6 us
    ppermute x7, starting transfers between devices, body(): got[step] = lax.ppermute(pieces[step], 'group', pairs)  17.9 us
    pallas_call x6, Pallas kernels, backward(): pl.pallas_call(functools.partial(backward_kernel, kinds, scale, scale2, f...  16.2 us
    ppermute x3, waiting for transfers between devices, on_device(): lax.ppermute(shares[k], 'tensor', ring(8, k, 2)).astype(jnp.float32)  10.1 us
    pallas_call x5, Pallas kernels, forward(): pl.pallas_call(functools.partial(forward_kernel, kinds, scale2, first, la...  8.97 us
    ppermute x1, starting transfers between devices, on_device(): beside = lax.ppermute(summed, 'tensor', swap(8))  8.65 us
    ppermute x7, waiting for transfers between devices, body(): got[step] = lax.ppermute(pieces[step], 'group', pairs)  6.3 us
    ppermute x2, starting transfers between devices, x_swap(): return lax.ppermute(x, 'group', swap(2 * SPLIT))  5.69 us
  transfers between devices with their start and end apart: 28, of which 17 were waited for; matrix products, arithmetic and copies ran while one was open for 0% of the time, Pallas kernels for 21%

profile of v1, /device:TPU:1, one launch (start us, length us, event | category | flops | bytes accessed | tf_op | source)
XLA Modules:
  0.0 119.5 jit_solution(9506598032467470665)
XLA Ops:
  1.3 1.4 %shard_map.103 = (bf16[2,256,128]{2,1,0:T(8,128)(2,1)S(1)}, bf16[2,256,128]{2,1,0:T(8,128)(2,1)S(1)}, bf16[2,256,128]{2,1,0:T(8,128)(2,1)S(1)}, bf16[2,256,128]{...) custom-call(bf16[2,2048,128]{2,1,0:T(8,128)(2,1)} %bitcast.49), custom_call_target="tpu_custom_call" | custom-call | tf_op jit(solution)/shard_map/pallas_call | solution.py:165
  2.7 24.3 %conditional.1 = (bf16[2,256,128]{2,1,0:T(8,128)(2,1)S(1)}) conditional(s32[]{:T(128)} %clamp.3, (s32[]{:T(128)}, bf16[2,256,128]{2,1,0:T(8,128)(2,1)S(1)}, bf16[2,256,128]{2,1,0:T(8,128)(2,1)S(1)}, bf16[2,256,128]{2,1,0:T(8,128)(2,1)S(1)}, bf16[2,256,128]{2,1,0:T(8,128)(2,1)S(1)}, ...), branch_computations={%region_0.1_spmd, %region_1.2_spmd, %region_2.3_spmd, %region_3.4_... | conditional | flops 458759 | bytes 4850022 | solution.py:277
  2.7 8.3 %collective-permute-start = (bf16[2,256,128]{2,1,0:T(8,128)(2,1)S(1)}, bf16[2,256,128]{2,1,0:T(8,128)(2,1)S(1)}, u32[]{:S(2)}, u32[]{:S(2)}) collective-permute-start(bf16[2,256,128]{2,1,0:T(8,128)(2,1)S(1)} %get-tuple-element.61), channel_id=1, source_target_pairs={{0,112},{8,120},{64,48},{72,56},{1,113},{9,121},{65,49},{73,57},{2... | collective-permute-start | bytes 393224 | tf_op jit(solution)/shard_map/cond/branch_0_fun/ppermute | solution.py:269
  11.1 1.3 %collective-permute-start.1 = (bf16[2,256,128]{2,1,0:T(8,128)(2,1)S(1)}, bf16[2,256,128]{2,1,0:T(8,128)(2,1)S(1)}, u32[]{:S(2)}, u32[]{:S(2)}) collective-permute-start(bf16[2,256,128]{2,1,0:T(8,128)(2,1)S(1)} %get-tuple-element.62), channel_id=1, source_target_pairs={{0,96},{8,104},{64,32},{72,40},{1,97},{9,105},{65,33},{73,41},{2,9... | collective-permute-start | bytes 393224 | tf_op jit(solution)/shard_map/cond/branch_0_fun/ppermute | solution.py:269
  12.4 1.3 %collective-permute-start.2 = (bf16[2,256,128]{2,1,0:T(8,128)(2,1)S(1)}, bf16[2,256,128]{2,1,0:T(8,128)(2,1)S(1)}, u32[]{:S(2)}, u32[]{:S(2)}) collective-permute-start(bf16[2,256,128]{2,1,0:T(8,128)(2,1)S(1)} %get-tuple-element.80), channel_id=1, source_target_pairs={{0,80},{8,88},{64,16},{72,24},{1,81},{9,89},{65,17},{73,25},{2,82}... | collective-permute-start | bytes 393224 | tf_op jit(solution)/shard_map/cond/branch_0_fun/ppermute | solution.py:269
  13.7 3.1 %collective-permute-start.3 = (bf16[2,256,128]{2,1,0:T(8,128)(2,1)S(1)}, bf16[2,256,128]{2,1,0:T(8,128)(2,1)S(1)}, u32[]{:S(2)}, u32[]{:S(2)}) collective-permute-start(bf16[2,256,128]{2,1,0:T(8,128)(2,1)S(1)} %get-tuple-element.81), channel_id=1, source_target_pairs={{0,64},{8,72},{64,0},{72,8},{1,65},{9,73},{65,1},{73,9},{2,66},{10... | collective-permute-start | bytes 393224 | tf_op jit(solution)/shard_map/cond/branch_0_fun/ppermute | solution.py:269
  16.7 1.3 %collective-permute-start.4 = (bf16[2,256,128]{2,1,0:T(8,128)(2,1)S(1)}, bf16[2,256,128]{2,1,0:T(8,128)(2,1)S(1)}, u32[]{:S(2)}, u32[]{:S(2)}) collective-permute-start(bf16[2,256,128]{2,1,0:T(8,128)(2,1)S(1)} %get-tuple-element.82), channel_id=1, source_target_pairs={{0,48},{8,56},{64,112},{72,120},{1,49},{9,57},{65,113},{73,121},{2... | collective-permute-start | bytes 393224 | tf_op jit(solution)/shard_map/cond/branch_0_fun/ppermute | solution.py:269
  18.1 1.3 %collective-permute-start.5 = (bf16[2,256,128]{2,1,0:T(8,128)(2,1)S(1)}, bf16[2,256,128]{2,1,0:T(8,128)(2,1)S(1)}, u32[]{:S(2)}, u32[]{:S(2)}) collective-permute-start(bf16[2,256,128]{2,1,0:T(8,128)(2,1)S(1)} %get-tuple-element.83), channel_id=1, source_target_pairs={{0,32},{8,40},{64,96},{72,104},{1,33},{9,41},{65,97},{73,105},{2,3... | collective-permute-start | bytes 393224 | tf_op jit(solution)/shard_map/cond/branch_0_fun/ppermute | solution.py:269
  19.4 1.3 %collective-permute-start.6 = (bf16[2,256,128]{2,1,0:T(8,128)(2,1)S(1)}, bf16[2,256,128]{2,1,0:T(8,128)(2,1)S(1)}, u32[]{:S(2)}, u32[]{:S(2)}) collective-permute-start(bf16[2,256,128]{2,1,0:T(8,128)(2,1)S(1)} %get-tuple-element.84), channel_id=1, source_target_pairs={{0,16},{8,24},{64,80},{72,88},{1,17},{9,25},{65,81},{73,89},{2,18}... | collective-permute-start | bytes 393224 | tf_op jit(solution)/shard_map/cond/branch_0_fun/ppermute | solution.py:269
  20.7 2.6 %collective-permute-done.3 = bf16[2,256,128]{2,1,0:T(8,128)(2,1)S(1)} collective-permute-done((bf16[2,256,128]{2,1,0:T(8,128)(2,1)S(1)}, bf16[2,256,128]{2,1,0:T(8,128)(2,1)S(1)}, u32[]{:S(2)}, u32[]{:S(2)}) %collective-permute-start.3) | collective-permute-done | bytes 131104 | tf_op jit(solution)/shard_map/cond/branch_0_fun/ppermute | solution.py:269
  23.3 0.9 collective-permute-done.5
  24.2 2.8 %collective-permute-done.6 = bf16[2,256,128]{2,1,0:T(8,128)(2,1)S(1)} collective-permute-done((bf16[2,256,128]{2,1,0:T(8,128)(2,1)S(1)}, bf16[2,256,128]{2,1,0:T(8,128)(2,1)S(1)}, u32[]{:S(2)}, u32[]{:S(2)}) %collective-permute-start.6) | collective-permute-done | bytes 131104 | tf_op jit(solution)/shard_map/cond/branch_0_fun/ppermute | solution.py:269
  27.1 2.8 %collective-permute-start.28 = (bf16[2,256,128]{2,1,0:T(8,128)(2,1)S(1)}, bf16[2,256,128]{2,1,0:T(8,128)(2,1)S(1)}, u32[]{:S(2)}, u32[]{:S(2)}) collective-permute-start(bf16[2,256,128]{2,1,0:T(8,128)(2,1)S(1)} %get-tuple-element.239), channel_id=1, source_target_pairs={{0,8},{8,0},{16,24},{24,16},{32,40},{40,32},{48,56},{56,48},{64,72... | collective-permute-start | bytes 393224 | tf_op jit(solution)/shard_map/ppermute | solution.py:242
  29.9 2.4 %shard_map.104 = bf16[2,4,640,128]{3,2,1,0:T(8,128)(2,1)} custom-call(bf16[2,4,2,640,128]{4,3,2,1,0:T(8,128)(2,1)} %bitcast.23), custom_call_target="tpu_custom_call" | custom-call | tf_op jit(solution)/shard_map/pallas_call | solution.py:186
  32.5 3.0 %collective-permute-start.31 = (bf16[2,4,640,128]{3,2,1,0:T(8,128)(2,1)}, bf16[2,4,640,128]{3,2,1,0:T(8,128)(2,1)S(1)}, u32[]{:S(2)}, u32[]{:S(2)}) collective-permute-start(bf16[2,4,640,128]{3,2,1,0:T(8,128)(2,1)} %shard_map.104), channel_id=1, source_target_pairs={{0,1},{1,0},{2,3},{3,2},{4,5},{5,4},{6,7},{7,6},{8,9},{9,8},{10,11... | collective-permute-start | bytes 3932168 | tf_op jit(solution)/shard_map/ppermute | solution.py:286
  35.5 2.3 %collective-permute-start.29 = (bf16[2,256,128]{2,1,0:T(8,128)(2,1)S(1)}, bf16[2,256,128]{2,1,0:T(8,128)(2,1)S(1)}, u32[]{:S(2)}, u32[]{:S(2)}) collective-permute-start(bf16[2,256,128]{2,1,0:T(8,128)(2,1)S(1)} %broadcast_select_fusion.refs_1_.refs_0_), channel_id=1, source_target_pairs={{0,16},{8,24},{16,32},{24,40},{32,48},{40,56},{48,64},{56,72},{64,... | collective-permute-start | bytes 393224 | tf_op jit(solution)/shard_map/ppermute | solution.py:238
  39.6 2.1 %shard_map.105.refs_2_ = f32[4,8,512]{2,1,0:T(8,128)S(1)} custom-call(s32[1]{0:T(128)S(6)} %copy.16.live_ref, s32[1]{0:T(128)S(6)} %copy.15.rows_ref, bf16[512,512]{1,0:T(8,128)(2,1)S(1)} %bitcast.25, bf16[512,512]{1,0:T(8,128)(2,1)S(1)} %bitcast.36, bf16[2,512,128]{2,1,0:T(8,128)(2,1)S(1)} %bitcast.47, ...), custom_call_target="tpu_custom_call" | custom-call | flops 805306368 | bytes 1048576 | tf_op jit(solution)/shard_map/pallas_call | solution.py:79
  43.0 2.3 %collective-permute-start.33 = (bf16[2,256,128]{2,1,0:T(8,128)(2,1)S(1)}, bf16[2,256,128]{2,1,0:T(8,128)(2,1)S(1)}, u32[]{:S(2)}, u32[]{:S(2)}) collective-permute-start(bf16[2,256,128]{2,1,0:T(8,128)(2,1)S(1)} %collective-permute-done.30.refs_1_.refs_0_), channel_id=1, source_target_pairs={{0,112},{8,120},{16,0},{24,8},{32,16},{40,24},{48,32},{56,40},{64,... | collective-permute-start | bytes 393224 | tf_op jit(solution)/shard_map/ppermute | solution.py:238
  45.3 1.9 %shard_map.106.refs_2_ = f32[4,8,512]{2,1,0:T(8,128)S(1)} custom-call(s32[1]{0:T(128)S(6)} %copy.16.live_ref, s32[1]{0:T(128)S(6)} %copy.15.rows_ref, bf16[512,512]{1,0:T(8,128)(2,1)S(1)} %bitcast.26, bf16[512,512]{1,0:T(8,128)(2,1)S(1)} %bitcast.37, bf16[2,256,128]{2,1,0:T(8,128)(2,1)S(1)} %collective-permute-done.29.refs_0_.refs_1_, ...), custom_call_target="tpu_custom_call" | custom-call | flops 536870912 | bytes 1048576 | tf_op jit(solution)/shard_map/pallas_call | solution.py:79
  47.7 1.4 %collective-permute-start.34 = (bf16[2,256,128]{2,1,0:T(8,128)(2,1)S(1)}, bf16[2,256,128]{2,1,0:T(8,128)(2,1)S(1)}, u32[]{:S(2)}, u32[]{:S(2)}) collective-permute-start(bf16[2,256,128]{2,1,0:T(8,128)(2,1)S(1)} %collective-permute-done.32.refs_0_.refs_1_), channel_id=1, source_target_pairs={{0,16},{8,24},{16,32},{24,40},{32,48},{40,56},{48,64},{56,72},{64,... | collective-permute-start | bytes 393224 | tf_op jit(solution)/shard_map/ppermute | solution.py:238
  49.1 1.3 %collective-permute-start.35 = (bf16[2,256,128]{2,1,0:T(8,128)(2,1)S(1)}, bf16[2,256,128]{2,1,0:T(8,128)(2,1)S(1)}, u32[]{:S(2)}, u32[]{:S(2)}) collective-permute-start(bf16[2,256,128]{2,1,0:T(8,128)(2,1)S(1)} %collective-permute-done.33.refs_1_.refs_0_), channel_id=1, source_target_pairs={{0,112},{8,120},{16,0},{24,8},{32,16},{40,24},{48,32},{56,40},{64,... | collective-permute-start | bytes 393224 | tf_op jit(solution)/shard_map/ppermute | solution.py:238
  50.4 1.9 %shard_map.107.refs_2_ = f32[4,8,512]{2,1,0:T(8,128)S(1)} custom-call(s32[1]{0:T(128)S(6)} %copy.16.live_ref, s32[1]{0:T(128)S(6)} %copy.15.rows_ref, bf16[512,512]{1,0:T(8,128)(2,1)S(1)} %bitcast.27, bf16[512,512]{1,0:T(8,128)(2,1)S(1)} %bitcast.38, bf16[2,256,128]{2,1,0:T(8,128)(2,1)S(1)} %collective-permute-done.32.refs_0_.refs_1_, ...), custom_call_target="tpu_custom_call" | custom-call | flops 536870912 | bytes 1048576 | tf_op jit(solution)/shard_map/pallas_call | solution.py:79
  52.9 2.5 %collective-permute-start.36 = (bf16[2,256,128]{2,1,0:T(8,128)(2,1)S(1)}, bf16[2,256,128]{2,1,0:T(8,128)(2,1)S(1)}, u32[]{:S(2)}, u32[]{:S(2)}) collective-permute-start(bf16[2,256,128]{2,1,0:T(8,128)(2,1)S(1)} %collective-permute-done.34.refs_0_.refs_1_), channel_id=1, source_target_pairs={{0,16},{8,24},{16,32},{24,40},{32,48},{40,56},{48,64},{56,72},{64,... | collective-permute-start | bytes 393224 | tf_op jit(solution)/shard_map/ppermute | solution.py:238
  55.4 1.9 %shard_map.108.refs_1_ = f32[4,8,512]{2,1,0:T(8,128)S(1)} custom-call(s32[1]{0:T(128)S(6)} %copy.16.live_ref, s32[1]{0:T(128)S(6)} %copy.15.rows_ref, bf16[512,512]{1,0:T(8,128)(2,1)S(1)} %bitcast.28, bf16[512,512]{1,0:T(8,128)(2,1)S(1)} %bitcast.39, bf16[2,256,128]{2,1,0:T(8,128)(2,1)S(1)} %collective-permute-done.34.refs_0_.refs_1_, ...), custom_call_target="tpu_custom_call" | custom-call | flops 536870912 | bytes 1048576 | tf_op jit(solution)/shard_map/pallas_call | solution.py:79
  57.9 1.1 shard_map.109.stat_ref
  59.0 1.6 %shard_map.110 = (f32[512,512]{1,0:T(8,128)S(1)}, bf16[2,256,128]{2,1,0:T(8,128)(2,1)S(1)}) custom-call(s32[1]{0:T(128)S(6)} %copy.16.live_ref, s32[1]{0:T(128)S(6)} %copy.15.rows_ref, bf16[512,512]{1,0:T(8,128)(2,1)S(1)} %bitcast.30, bf16[512,512]{1,0:T(8,128)(2,1)S(1)} %bitcast.41, f32[4,8,512]{2,1,0:T(8,128)S(1)} %shard_map.109.stat_ref, ...), custom_call_target="tpu_custom_call" | custom-call | flops 671088640 | bytes 1048576 | tf_op jit(solution)/shard_map/pallas_call | solution.py:138
  60.7 1.4 %collective-permute-start.37 = (bf16[2,256,128]{2,1,0:T(8,128)(2,1)S(1)}, bf16[2,256,128]{2,1,0:T(8,128)(2,1)S(1)}, u32[]{:S(2)}, u32[]{:S(2)}) collective-permute-start(bf16[2,256,128]{2,1,0:T(8,128)(2,1)S(1)} %get-tuple-element.201), channel_id=1, source_target_pairs={{0,16},{8,24},{16,32},{24,40},{32,48},{40,56},{48,64},{56,72},{64,... | collective-permute-start | bytes 393224 | tf_op jit(solution)/shard_map/ppermute | solution.py:238
  62.0 3.0 %shard_map.111 = (f32[512,512]{1,0:T(8,128)S(1)}, bf16[2,256,128]{2,1,0:T(8,128)(2,1)S(1)}, bf16[2,256,128]{2,1,0:T(8,128)(2,1)S(1)}) custom-call(s32[1]{0:T(128)S(6)} %copy.16.live_ref, s32[1]{0:T(128)S(6)} %copy.15.rows_ref, bf16[512,512]{1,0:T(8,128)(2,1)S(1)} %bitcast.31, bf16[512,512]{1,0:T(8,128)(2,1)S(1)} %bitcast.42, ...), custom_call_target="tpu_custom_call" | custom-call | flops 1342177280 | bytes 1048576 | tf_op jit(solution)/shard_map/pallas_call | solution.py:138
  65.0 0.8 collective-permute-done.37
  65.8 0.8 collective-permute-start.38
  66.6 2.0 %collective-permute-start.41 = (bf16[2,256,128]{2,1,0:T(8,128)(2,1)S(1)}, bf16[2,256,128]{2,1,0:T(8,128)(2,1)S(1)}, u32[]{:S(2)}, u32[]{:S(2)}) collective-permute-start(bf16[2,256,128]{2,1,0:T(8,128)(2,1)S(1)} %get-tuple-element.222), channel_id=1, source_target_pairs={{0,112},{8,120},{16,0},{24,8},{32,16},{40,24},{48,32},{56,40},{64,... | collective-permute-start | bytes 393224 | tf_op jit(solution)/shard_map/ppermute | solution.py:238
  68.6 3.0 %shard_map.112 = (f32[512,512]{1,0:T(8,128)S(1)}, bf16[2,256,128]{2,1,0:T(8,128)(2,1)S(1)}, bf16[2,256,128]{2,1,0:T(8,128)(2,1)S(1)}) custom-call(s32[1]{0:T(128)S(6)} %copy.16.live_ref, s32[1]{0:T(128)S(6)} %copy.15.rows_ref, bf16[512,512]{1,0:T(8,128)(2,1)S(1)} %bitcast.32, bf16[512,512]{1,0:T(8,128)(2,1)S(1)} %bitcast.43, ...), custom_call_target="tpu_custom_call" | custom-call | flops 1342177280 | bytes 1048576 | tf_op jit(solution)/shard_map/pallas_call | solution.py:138
  71.6 0.9 collective-permute-done.38
  72.7 2.7 %collective-permute-start.42 = (bf16[2,256,128]{2,1,0:T(8,128)(2,1)S(1)}, bf16[2,256,128]{2,1,0:T(8,128)(2,1)S(1)}, u32[]{:S(2)}, u32[]{:S(2)}) collective-permute-start(bf16[2,256,128]{2,1,0:T(8,128)(2,1)S(1)} %add_convert_fusion.1), channel_id=1, source_target_pairs={{0,112},{8,120},{16,0},{24,8},{32,16},{40,24},{48,32},{56,40},{64,... | collective-permute-start | bytes 393224 | tf_op jit(solution)/shard_map/ppermute | solution.py:238
  75.4 3.0 %shard_map.113 = (f32[512,512]{1,0:T(8,128)S(1)}, bf16[2,256,128]{2,1,0:T(8,128)(2,1)S(1)}, bf16[2,256,128]{2,1,0:T(8,128)(2,1)S(1)}) custom-call(s32[1]{0:T(128)S(6)} %copy.16.live_ref, s32[1]{0:T(128)S(6)} %copy.15.rows_ref, bf16[512,512]{1,0:T(8,128)(2,1)S(1)} %bitcast.33, bf16[512,512]{1,0:T(8,128)(2,1)S(1)} %bitcast.44, ...), custom_call_target="tpu_custom_call" | custom-call | flops 1342177280 | bytes 1048576 | tf_op jit(solution)/shard_map/pallas_call | solution.py:138
  78.4 1.0 copy-done.4
  79.6 2.9 %collective-permute-start.43 = (bf16[2,256,128]{2,1,0:T(8,128)(2,1)S(1)}, bf16[2,256,128]{2,1,0:T(8,128)(2,1)S(1)}, u32[]{:S(2)}, u32[]{:S(2)}) collective-permute-start(bf16[2,256,128]{2,1,0:T(8,128)(2,1)S(1)} %add_convert_fusion), channel_id=1, source_target_pairs={{0,112},{8,120},{16,0},{24,8},{32,16},{40,24},{48,32},{56,40},{64,... | collective-permute-start | bytes 393224 | tf_op jit(solution)/shard_map/ppermute | solution.py:238
  82.6 1.2 %copy-done.5 = f32[512,512]{1,0:T(8,128)S(1)} copy-done((f32[512,512]{1,0:T(8,128)S(1)}, f32[512,512]{1,0:T(8,128)}, u32[]{:S(2)}) %copy-start.5) | copy-done | bytes 1048600
  83.8 1.6 %shard_map.114 = (f32[512,512]{1,0:T(8,128)S(1)}, bf16[2,256,128]{2,1,0:T(8,128)(2,1)S(1)}) custom-call(s32[1]{0:T(128)S(6)} %copy.16.live_ref, s32[1]{0:T(128)S(6)} %copy.15.rows_ref, bf16[512,512]{1,0:T(8,128)(2,1)S(1)} %bitcast.34, bf16[512,512]{1,0:T(8,128)(2,1)S(1)} %bitcast.45, f32[4,8,512]{2,1,0:T(8,128)S(1)} %shard_map.109.stat_ref, ...), custom_call_target="tpu_custom_call" | custom-call | flops 671088640 | bytes 1048576 | tf_op jit(solution)/shard_map/pallas_call | solution.py:138
  85.6 2.9 %collective-permute-start.44 = (bf16[2,128,128]{2,1,0:T(8,128)(2,1)S(1)}, bf16[2,128,128]{2,1,0:T(8,128)(2,1)S(1)}, u32[]{:S(2)}, u32[]{:S(2)}) collective-permute-start(bf16[2,128,128]{2,1,0:T(8,128)(2,1)S(1)} %add_convert_fusion.6), channel_id=1, source_target_pairs={{0,8},{8,0},{16,24},{24,16},{32,40},{40,32},{48,56},{56,48},{64,72... | collective-permute-start | bytes 196616 | tf_op jit(solution)/shard_map/ppermute | solution.py:242
  88.4 3.9 %shard_map.115 = (bf16[512,512]{1,0:T(8,128)(2,1)}, bf16[2,512,128]{2,1,0:T(8,128)(2,1)}) custom-call(s32[1]{0:T(128)S(6)} %copy.16.live_ref, s32[1]{0:T(128)S(6)} %copy.15.rows_ref, bf16[512,512]{1,0:T(8,128)(2,1)S(1)} %bitcast.35, bf16[512,512]{1,0:T(8,128)(2,1)S(1)} %bitcast.46, f32[4,8,512]{2,1,0:T(8,128)S(1)} %shard_map.109.stat_ref, ...), custom_call_target="tpu_custom_call" | custom-call | flops 1342177280 | bytes 1048576 | tf_op jit(solution)/shard_map/pallas_call | solution.py:138
  92.4 8.7 %collective-permute-start.45 = (bf16[2,128,128]{2,1,0:T(8,128)(2,1)S(1)}, bf16[2,128,128]{2,1,0:T(8,128)(2,1)S(1)}, u32[]{:S(2)}, u32[]{:S(2)}) collective-permute-start(bf16[2,128,128]{2,1,0:T(8,128)(2,1)S(1)} %add_convert_fusion.5.summed_ref), channel_id=1, source_target_pairs={{0,1},{1,0},{2,3},{3,2},{4,5},{5,4},{6,7},{7,6},{8,9},{9,8},{10,11... | collective-permute-start | bytes 196616 | tf_op jit(solution)/shard_map/ppermute | solution.py:326
  101.1 0.9 collective-permute-done.45.beside_ref
  102.0 2.8 %shard_map.116 = bf16[4,128,640]{2,1,0:T(8,128)(2,1)S(1)} custom-call(bf16[2,128,128]{2,1,0:T(8,128)(2,1)S(1)} %add_convert_fusion.5.summed_ref, bf16[2,128,128]{2,1,0:T(8,128)(2,1)S(1)} %collective-permute-done.45.beside_ref, bf16[2,4,2,640,128]{4,3,2,1,0:T(8,128)(2,1)S(1)} %bitcast.24, bf16[2,4,640,128]{3,2,1,0:T(8,128)(2,1)S(1)} %collective-permute-done.31.other_ref), custom_call_target="tpu_custom_call" | custom-call | tf_op jit(solution)/shard_map/pallas_call | solution.py:218
  104.8 2.8 %collective-permute-start.48 = (bf16[128,640]{1,0:T(8,128)(2,1)S(1)}, bf16[128,640]{1,0:T(8,128)(2,1)S(1)}, u32[]{:S(2)}, u32[]{:S(2)}) collective-permute-start(bf16[128,640]{1,0:T(8,128)(2,1)S(1)} %get-tuple-element.237), channel_id=1, source_target_pairs={{0,6},{1,7},{2,0},{3,1},{4,2},{5,3},{6,4},{7,5},{8,14},{9,15},{10,... | collective-permute-start | bytes 491528 | tf_op jit(solution)/shard_map/ppermute | solution.py:330
  108.7 5.6 %collective-permute-done.48 = bf16[128,640]{1,0:T(8,128)(2,1)S(1)} collective-permute-done((bf16[128,640]{1,0:T(8,128)(2,1)S(1)}, bf16[128,640]{1,0:T(8,128)(2,1)S(1)}, u32[]{:S(2)}, u32[]{:S(2)}) %collective-permute-start.48) | collective-permute-done | bytes 163872 | tf_op jit(solution)/shard_map/ppermute | solution.py:330
  114.3 4.5 %collective-permute-done.46 = bf16[128,640]{1,0:T(8,128)(2,1)S(1)} collective-permute-done((bf16[128,640]{1,0:T(8,128)(2,1)S(1)}, bf16[128,640]{1,0:T(8,128)(2,1)S(1)}, u32[]{:S(2)}, u32[]{:S(2)}) %collective-permute-start.46) | collective-permute-done | bytes 163872 | tf_op jit(solution)/shard_map/ppermute | solution.py:330
  118.8 0.8 fusion.2
  (46 shorter events, 5.4 us)
Async XLA Ops:
  2.7 15.3 %collective-permute-start = (bf16[2,256,128]{2,1,0:T(8,128)(2,1)S(1)}, bf16[2,256,128]{2,1,0:T(8,128)(2,1)S(1)}, u32[]{:S(2)}, u32[]{:S(2)}) collective-permute-start(bf16[2,256,128]{2,1,0:T(8,128)(2,1)S(1)} %get-tuple-element.61), channel_id=1, source_target_pairs={{0,112},{8,120},{64,48},{72,56},{1,113},{9,121},{65,49},{73,57},{2... | collective-permute-start | bytes 393224 | tf_op jit(solution)/shard_map/cond/branch_0_fun/ppermute | solution.py:269
  11.1 8.3 %collective-permute-start.1 = (bf16[2,256,128]{2,1,0:T(8,128)(2,1)S(1)}, bf16[2,256,128]{2,1,0:T(8,128)(2,1)S(1)}, u32[]{:S(2)}, u32[]{:S(2)}) collective-permute-start(bf16[2,256,128]{2,1,0:T(8,128)(2,1)S(1)} %get-tuple-element.62), channel_id=1, source_target_pairs={{0,96},{8,104},{64,32},{72,40},{1,97},{9,105},{65,33},{73,41},{2,9... | collective-permute-start | bytes 393224 | tf_op jit(solution)/shard_map/cond/branch_0_fun/ppermute | solution.py:269
  12.4 8.3 %collective-permute-start.2 = (bf16[2,256,128]{2,1,0:T(8,128)(2,1)S(1)}, bf16[2,256,128]{2,1,0:T(8,128)(2,1)S(1)}, u32[]{:S(2)}, u32[]{:S(2)}) collective-permute-start(bf16[2,256,128]{2,1,0:T(8,128)(2,1)S(1)} %get-tuple-element.80), channel_id=1, source_target_pairs={{0,80},{8,88},{64,16},{72,24},{1,81},{9,89},{65,17},{73,25},{2,82}... | collective-permute-start | bytes 393224 | tf_op jit(solution)/shard_map/cond/branch_0_fun/ppermute | solution.py:269
  13.7 9.6 %collective-permute-start.3 = (bf16[2,256,128]{2,1,0:T(8,128)(2,1)S(1)}, bf16[2,256,128]{2,1,0:T(8,128)(2,1)S(1)}, u32[]{:S(2)}, u32[]{:S(2)}) collective-permute-start(bf16[2,256,128]{2,1,0:T(8,128)(2,1)S(1)} %get-tuple-element.81), channel_id=1, source_target_pairs={{0,64},{8,72},{64,0},{72,8},{1,65},{9,73},{65,1},{73,9},{2,66},{10... | collective-permute-start | bytes 393224 | tf_op jit(solution)/shard_map/cond/branch_0_fun/ppermute | solution.py:269
  16.7 6.5 %collective-permute-start.4 = (bf16[2,256,128]{2,1,0:T(8,128)(2,1)S(1)}, bf16[2,256,128]{2,1,0:T(8,128)(2,1)S(1)}, u32[]{:S(2)}, u32[]{:S(2)}) collective-permute-start(bf16[2,256,128]{2,1,0:T(8,128)(2,1)S(1)} %get-tuple-element.82), channel_id=1, source_target_pairs={{0,48},{8,56},{64,112},{72,120},{1,49},{9,57},{65,113},{73,121},{2... | collective-permute-start | bytes 393224 | tf_op jit(solution)/shard_map/cond/branch_0_fun/ppermute | solution.py:269
  18.1 6.1 %collective-permute-start.5 = (bf16[2,256,128]{2,1,0:T(8,128)(2,1)S(1)}, bf16[2,256,128]{2,1,0:T(8,128)(2,1)S(1)}, u32[]{:S(2)}, u32[]{:S(2)}) collective-permute-start(bf16[2,256,128]{2,1,0:T(8,128)(2,1)S(1)} %get-tuple-element.83), channel_id=1, source_target_pairs={{0,32},{8,40},{64,96},{72,104},{1,33},{9,41},{65,97},{73,105},{2,3... | collective-permute-start | bytes 393224 | tf_op jit(solution)/shard_map/cond/branch_0_fun/ppermute | solution.py:269
  19.4 7.6 %collective-permute-start.6 = (bf16[2,256,128]{2,1,0:T(8,128)(2,1)S(1)}, bf16[2,256,128]{2,1,0:T(8,128)(2,1)S(1)}, u32[]{:S(2)}, u32[]{:S(2)}) collective-permute-start(bf16[2,256,128]{2,1,0:T(8,128)(2,1)S(1)} %get-tuple-element.84), channel_id=1, source_target_pairs={{0,16},{8,24},{64,80},{72,88},{1,17},{9,25},{65,81},{73,89},{2,18}... | collective-permute-start | bytes 393224 | tf_op jit(solution)/shard_map/cond/branch_0_fun/ppermute | solution.py:269
  27.1 12.5 %copy-start.1 = (bf16[1,512,512]{2,1,0:T(8,128)(2,1)S(1)}, bf16[1,512,512]{2,1,0:T(8,128)(2,1)}, u32[]{:S(2)}) copy-start(bf16[1,512,512]{2,1,0:T(8,128)(2,1)} %param.12) | copy-start | bytes 1572868
  27.1 12.5 %copy-start.2 = (bf16[1,512,512]{2,1,0:T(8,128)(2,1)S(1)}, bf16[1,512,512]{2,1,0:T(8,128)(2,1)}, u32[]{:S(2)}) copy-start(bf16[1,512,512]{2,1,0:T(8,128)(2,1)} %param.14) | copy-start | bytes 1572868
  27.1 12.5 %copy-start.3 = (bf16[1,2,512,128]{3,2,1,0:T(8,128)(2,1)S(1)}, bf16[1,2,512,128]{3,2,1,0:T(8,128)(2,1)}, u32[]{:S(2)}) copy-start(bf16[1,2,512,128]{3,2,1,0:T(8,128)(2,1)} %param.13) | copy-start | bytes 786436
  27.1 5.4 %collective-permute-start.28 = (bf16[2,256,128]{2,1,0:T(8,128)(2,1)S(1)}, bf16[2,256,128]{2,1,0:T(8,128)(2,1)S(1)}, u32[]{:S(2)}, u32[]{:S(2)}) collective-permute-start(bf16[2,256,128]{2,1,0:T(8,128)(2,1)S(1)} %get-tuple-element.239), channel_id=1, source_target_pairs={{0,8},{8,0},{16,24},{24,16},{32,40},{40,32},{48,56},{56,48},{64,72... | collective-permute-start | bytes 393224 | tf_op jit(solution)/shard_map/ppermute | solution.py:242
  32.5 10.1 %collective-permute-start.31 = (bf16[2,4,640,128]{3,2,1,0:T(8,128)(2,1)}, bf16[2,4,640,128]{3,2,1,0:T(8,128)(2,1)S(1)}, u32[]{:S(2)}, u32[]{:S(2)}) collective-permute-start(bf16[2,4,640,128]{3,2,1,0:T(8,128)(2,1)} %shard_map.104), channel_id=1, source_target_pairs={{0,1},{1,0},{2,3},{3,2},{4,5},{5,4},{6,7},{7,6},{8,9},{9,8},{10,11... | collective-permute-start | bytes 3932168 | tf_op jit(solution)/shard_map/ppermute | solution.py:286
  35.5 6.4 %collective-permute-start.29 = (bf16[2,256,128]{2,1,0:T(8,128)(2,1)S(1)}, bf16[2,256,128]{2,1,0:T(8,128)(2,1)S(1)}, u32[]{:S(2)}, u32[]{:S(2)}) collective-permute-start(bf16[2,256,128]{2,1,0:T(8,128)(2,1)S(1)} %broadcast_select_fusion.refs_1_.refs_0_), channel_id=1, source_target_pairs={{0,16},{8,24},{16,32},{24,40},{32,48},{40,56},{48,64},{56,72},{64,... | collective-permute-start | bytes 393224 | tf_op jit(solution)/shard_map/ppermute | solution.py:238
  37.8 4.8 %collective-permute-start.30 = (bf16[2,256,128]{2,1,0:T(8,128)(2,1)S(1)}, bf16[2,256,128]{2,1,0:T(8,128)(2,1)S(1)}, u32[]{:S(2)}, u32[]{:S(2)}) collective-permute-start(bf16[2,256,128]{2,1,0:T(8,128)(2,1)S(1)} %broadcast_select_fusion.refs_1_.refs_0_), channel_id=1, source_target_pairs={{0,112},{8,120},{16,0},{24,8},{32,16},{40,24},{48,32},{56,40},{64,... | collective-permute-start | bytes 393224 | tf_op jit(solution)/shard_map/ppermute | solution.py:238
  42.6 5.0 %collective-permute-start.32 = (bf16[2,256,128]{2,1,0:T(8,128)(2,1)S(1)}, bf16[2,256,128]{2,1,0:T(8,128)(2,1)S(1)}, u32[]{:S(2)}, u32[]{:S(2)}) collective-permute-start(bf16[2,256,128]{2,1,0:T(8,128)(2,1)S(1)} %collective-permute-done.29.refs_0_.refs_1_), channel_id=1, source_target_pairs={{0,16},{8,24},{16,32},{24,40},{32,48},{40,56},{48,64},{56,72},{64,... | collective-permute-start | bytes 393224 | tf_op jit(solution)/shard_map/ppermute | solution.py:238
  43.0 4.6 %collective-permute-start.33 = (bf16[2,256,128]{2,1,0:T(8,128)(2,1)S(1)}, bf16[2,256,128]{2,1,0:T(8,128)(2,1)S(1)}, u32[]{:S(2)}, u32[]{:S(2)}) collective-permute-start(bf16[2,256,128]{2,1,0:T(8,128)(2,1)S(1)} %collective-permute-done.30.refs_1_.refs_0_), channel_id=1, source_target_pairs={{0,112},{8,120},{16,0},{24,8},{32,16},{40,24},{48,32},{56,40},{64,... | collective-permute-start | bytes 393224 | tf_op jit(solution)/shard_map/ppermute | solution.py:238
  47.7 5.0 %collective-permute-start.34 = (bf16[2,256,128]{2,1,0:T(8,128)(2,1)S(1)}, bf16[2,256,128]{2,1,0:T(8,128)(2,1)S(1)}, u32[]{:S(2)}, u32[]{:S(2)}) collective-permute-start(bf16[2,256,128]{2,1,0:T(8,128)(2,1)S(1)} %collective-permute-done.32.refs_0_.refs_1_), channel_id=1, source_target_pairs={{0,16},{8,24},{16,32},{24,40},{32,48},{40,56},{48,64},{56,72},{64,... | collective-permute-start | bytes 393224 | tf_op jit(solution)/shard_map/ppermute | solution.py:238
  49.1 3.8 %collective-permute-start.35 = (bf16[2,256,128]{2,1,0:T(8,128)(2,1)S(1)}, bf16[2,256,128]{2,1,0:T(8,128)(2,1)S(1)}, u32[]{:S(2)}, u32[]{:S(2)}) collective-permute-start(bf16[2,256,128]{2,1,0:T(8,128)(2,1)S(1)} %collective-permute-done.33.refs_1_.refs_0_), channel_id=1, source_target_pairs={{0,112},{8,120},{16,0},{24,8},{32,16},{40,24},{48,32},{56,40},{64,... | collective-permute-start | bytes 393224 | tf_op jit(solution)/shard_map/ppermute | solution.py:238
  52.9 5.0 %collective-permute-start.36 = (bf16[2,256,128]{2,1,0:T(8,128)(2,1)S(1)}, bf16[2,256,128]{2,1,0:T(8,128)(2,1)S(1)}, u32[]{:S(2)}, u32[]{:S(2)}) collective-permute-start(bf16[2,256,128]{2,1,0:T(8,128)(2,1)S(1)} %collective-permute-done.34.refs_0_.refs_1_), channel_id=1, source_target_pairs={{0,16},{8,24},{16,32},{24,40},{32,48},{40,56},{48,64},{56,72},{64,... | collective-permute-start | bytes 393224 | tf_op jit(solution)/shard_map/ppermute | solution.py:238
  60.7 5.1 %collective-permute-start.37 = (bf16[2,256,128]{2,1,0:T(8,128)(2,1)S(1)}, bf16[2,256,128]{2,1,0:T(8,128)(2,1)S(1)}, u32[]{:S(2)}, u32[]{:S(2)}) collective-permute-start(bf16[2,256,128]{2,1,0:T(8,128)(2,1)S(1)} %get-tuple-element.201), channel_id=1, source_target_pairs={{0,16},{8,24},{16,32},{24,40},{32,48},{40,56},{48,64},{56,72},{64,... | collective-permute-start | bytes 393224 | tf_op jit(solution)/shard_map/ppermute | solution.py:238
  65.8 6.7 %collective-permute-start.38 = (bf16[2,256,128]{2,1,0:T(8,128)(2,1)S(1)}, bf16[2,256,128]{2,1,0:T(8,128)(2,1)S(1)}, u32[]{:S(2)}, u32[]{:S(2)}) collective-permute-start(bf16[2,256,128]{2,1,0:T(8,128)(2,1)S(1)} %add_convert_fusion.4), channel_id=1, source_target_pairs={{0,16},{8,24},{16,32},{24,40},{32,48},{40,56},{48,64},{56,72},{64,... | collective-permute-start | bytes 393224 | tf_op jit(solution)/shard_map/ppermute | solution.py:238
  66.6 6.0 %collective-permute-start.41 = (bf16[2,256,128]{2,1,0:T(8,128)(2,1)S(1)}, bf16[2,256,128]{2,1,0:T(8,128)(2,1)S(1)}, u32[]{:S(2)}, u32[]{:S(2)}) collective-permute-start(bf16[2,256,128]{2,1,0:T(8,128)(2,1)S(1)} %get-tuple-element.222), channel_id=1, source_target_pairs={{0,112},{8,120},{16,0},{24,8},{32,16},{40,24},{48,32},{56,40},{64,... | collective-permute-start | bytes 393224 | tf_op jit(solution)/shard_map/ppermute | solution.py:238
  72.5 6.9 %collective-permute-start.39 = (bf16[2,256,128]{2,1,0:T(8,128)(2,1)S(1)}, bf16[2,256,128]{2,1,0:T(8,128)(2,1)S(1)}, u32[]{:S(2)}, u32[]{:S(2)}) collective-permute-start(bf16[2,256,128]{2,1,0:T(8,128)(2,1)S(1)} %add_convert_fusion.3), channel_id=1, source_target_pairs={{0,16},{8,24},{16,32},{24,40},{32,48},{40,56},{48,64},{56,72},{64,... | collective-permute-start | bytes 393224 | tf_op jit(solution)/shard_map/ppermute | solution.py:238
  72.7 6.9 %collective-permute-start.42 = (bf16[2,256,128]{2,1,0:T(8,128)(2,1)S(1)}, bf16[2,256,128]{2,1,0:T(8,128)(2,1)S(1)}, u32[]{:S(2)}, u32[]{:S(2)}) collective-permute-start(bf16[2,256,128]{2,1,0:T(8,128)(2,1)S(1)} %add_convert_fusion.1), channel_id=1, source_target_pairs={{0,112},{8,120},{16,0},{24,8},{32,16},{40,24},{48,32},{56,40},{64,... | collective-permute-start | bytes 393224 | tf_op jit(solution)/shard_map/ppermute | solution.py:238
  78.4 1.0 copy-start.4
  79.5 6.1 %collective-permute-start.40 = (bf16[2,256,128]{2,1,0:T(8,128)(2,1)S(1)}, bf16[2,256,128]{2,1,0:T(8,128)(2,1)S(1)}, u32[]{:S(2)}, u32[]{:S(2)}) collective-permute-start(bf16[2,256,128]{2,1,0:T(8,128)(2,1)S(1)} %add_convert_fusion.2), channel_id=1, source_target_pairs={{0,16},{8,24},{16,32},{24,40},{32,48},{40,56},{48,64},{56,72},{64,... | collective-permute-start | bytes 393224 | tf_op jit(solution)/shard_map/ppermute | solution.py:238
  79.6 5.9 %collective-permute-start.43 = (bf16[2,256,128]{2,1,0:T(8,128)(2,1)S(1)}, bf16[2,256,128]{2,1,0:T(8,128)(2,1)S(1)}, u32[]{:S(2)}, u32[]{:S(2)}) collective-permute-start(bf16[2,256,128]{2,1,0:T(8,128)(2,1)S(1)} %add_convert_fusion), channel_id=1, source_target_pairs={{0,112},{8,120},{16,0},{24,8},{32,16},{40,24},{48,32},{56,40},{64,... | collective-permute-start | bytes 393224 | tf_op jit(solution)/shard_map/ppermute | solution.py:238
  82.6 1.2 %copy-start.5 = (f32[512,512]{1,0:T(8,128)S(1)}, f32[512,512]{1,0:T(8,128)}, u32[]{:S(2)}) copy-start(f32[512,512]{1,0:T(8,128)} %copy-done.4) | copy-start | bytes 3145732
  85.6 6.8 %collective-permute-start.44 = (bf16[2,128,128]{2,1,0:T(8,128)(2,1)S(1)}, bf16[2,128,128]{2,1,0:T(8,128)(2,1)S(1)}, u32[]{:S(2)}, u32[]{:S(2)}) collective-permute-start(bf16[2,128,128]{2,1,0:T(8,128)(2,1)S(1)} %add_convert_fusion.6), channel_id=1, source_target_pairs={{0,8},{8,0},{16,24},{24,16},{32,40},{40,32},{48,56},{56,48},{64,72... | collective-permute-start | bytes 196616 | tf_op jit(solution)/shard_map/ppermute | solution.py:242
  88.4 13.5 %copy-start = (bf16[2,5120,128]{2,1,0:T(8,128)(2,1)S(1)}, bf16[2,5120,128]{2,1,0:T(8,128)(2,1)}, u32[]{:S(2)}) copy-start(bf16[2,5120,128]{2,1,0:T(8,128)(2,1)} %param.16) | copy-start | bytes 7864324
  92.4 9.6 %collective-permute-start.45 = (bf16[2,128,128]{2,1,0:T(8,128)(2,1)S(1)}, bf16[2,128,128]{2,1,0:T(8,128)(2,1)S(1)}, u32[]{:S(2)}, u32[]{:S(2)}) collective-permute-start(bf16[2,128,128]{2,1,0:T(8,128)(2,1)S(1)} %add_convert_fusion.5.summed_ref), channel_id=1, source_target_pairs={{0,1},{1,0},{2,3},{3,2},{4,5},{5,4},{6,7},{7,6},{8,9},{9,8},{10,11... | collective-permute-start | bytes 196616 | tf_op jit(solution)/shard_map/ppermute | solution.py:326
  104.8 9.4 %collective-permute-start.48 = (bf16[128,640]{1,0:T(8,128)(2,1)S(1)}, bf16[128,640]{1,0:T(8,128)(2,1)S(1)}, u32[]{:S(2)}, u32[]{:S(2)}) collective-permute-start(bf16[128,640]{1,0:T(8,128)(2,1)S(1)} %get-tuple-element.237), channel_id=1, source_target_pairs={{0,6},{1,7},{2,0},{3,1},{4,2},{5,3},{6,4},{7,5},{8,14},{9,15},{10,... | collective-permute-start | bytes 491528 | tf_op jit(solution)/shard_map/ppermute | solution.py:330
  107.6 6.7 %collective-permute-start.47 = (bf16[128,640]{1,0:T(8,128)(2,1)S(1)}, bf16[128,640]{1,0:T(8,128)(2,1)S(1)}, u32[]{:S(2)}, u32[]{:S(2)}) collective-permute-start(bf16[128,640]{1,0:T(8,128)(2,1)S(1)} %get-tuple-element.238), channel_id=1, source_target_pairs={{0,4},{1,5},{2,6},{3,7},{4,0},{5,1},{6,2},{7,3},{8,12},{9,13},{10,... | collective-permute-start | bytes 491528 | tf_op jit(solution)/shard_map/ppermute | solution.py:330
  108.0 10.8 %collective-permute-start.46 = (bf16[128,640]{1,0:T(8,128)(2,1)S(1)}, bf16[128,640]{1,0:T(8,128)(2,1)S(1)}, u32[]{:S(2)}, u32[]{:S(2)}) collective-permute-start(bf16[128,640]{1,0:T(8,128)(2,1)S(1)} %get-tuple-element.236), channel_id=1, source_target_pairs={{0,2},{1,3},{2,4},{3,5},{4,6},{5,7},{6,0},{7,1},{8,10},{9,11},{10,... | collective-permute-start | bytes 491528 | tf_op jit(solution)/shard_map/ppermute | solution.py:330

commit v2 on v1

--- a/solution.py
+++ b/solution.py
@@ -192,35 +192,25 @@
     )(by_core)
 
 
-def project_kernel(summed_ref, beside_ref, weight_ref, other_ref, out_ref, held_ref, sems):
+def project_kernel(summed_ref, beside_ref, weight_ref, other_ref, out_ref):
     tensor = lax.axis_index("tensor")
     y, core = tensor // 2, lax.rem(tensor, 2)
-    copies = []
     for step in range(4):
         at = lax.rem(y + step, 4)
-        mine = pltpu.make_async_copy(weight_ref.at[:, at, core], held_ref.at[step, 0], sems.at[step, 0])
-        theirs = pltpu.make_async_copy(other_ref.at[:, at], held_ref.at[step, 1], sems.at[step, 1])
-        mine.start()
-        theirs.start()
-        copies.append((mine, theirs))
-    for step in range(4):
         acc = None
-        for c, rows in enumerate((summed_ref, beside_ref)):
-            copies[step][c].wait()
-            for j in range(2):
-                part = dot(rows[j], held_ref[step, c, j], LAST)
+        for j in range(2):
+            for rows, block in ((summed_ref[j], weight_ref[j, at, core]), (beside_ref[j], other_ref[j, at])):
+                part = dot(rows, block, LAST)
                 acc = part if acc is None else acc + part
         out_ref[step] = acc.astype(out_ref.dtype)
 
 
 def project(summed, beside, by_core, other):
-    cols, dh = by_core.shape[3:]
     return pl.pallas_call(
         project_kernel,
-        in_specs=[VMEM] * 2 + [ANY] * 2,
+        in_specs=[VMEM] * 4,
         out_specs=VMEM,
-        out_shape=jax.ShapeDtypeStruct((4, summed.shape[1], cols), jnp.bfloat16),
-        scratch_shapes=[pltpu.VMEM((4, 2, 2, cols, dh), by_core.dtype), pltpu.SemaphoreType.DMA((4, 2))],
+        out_shape=jax.ShapeDtypeStruct((4, summed.shape[1], by_core.shape[3]), jnp.bfloat16),
         compiler_params=pltpu.CompilerParams(vmem_limit_bytes=16 * 2**20),
     )(summed, beside, by_core, other)
 
@@ -264,7 +254,7 @@
     def branch(holder):
         def body(*pieces):
             got = {}
-            for step in (4, 3, 5, 2, 6, 1, 7):
+            for step in (1, 7, 2, 6, 3, 5, 4):
                 pairs = [(2 * at + c, 2 * ((at + step) % SPLIT) + c) for at in (holder, holder + half_way) for c in (0, 1)]
                 got[step] = lax.ppermute(pieces[step], "group", pairs)
             held = pieces[0]

time: 120 us -> 117 us (0.975)
  starting transfers between devices: 59.6 us -> 47.2 us
  waiting for transfers between devices: 21.8 us -> 32.9 us
  Pallas kernels: 31.7 us -> 30 us
    ppermute x7, starting transfers between devices: 17.9 us -> 5.92 us  [body(): got[step] = lax.ppermute(pieces[step], 'group', pairs)]
    ppermute x7, waiting for transfers between devices: 6.3 us -> 15.2 us  [body(): got[step] = lax.ppermute(pieces[step], 'group', pairs)]
    ppermute x14, waiting for transfers between devices: 4.28 us -> 6.53 us  [z_hop(): return lax.ppermute(x, 'group', ring(2 * SPLIT, step, 2))]
    ppermute x14, starting transfers between devices: 20.6 us -> 18.4 us  [z_hop(): return lax.ppermute(x, 'group', ring(2 * SPLIT, step, 2))]
    pallas_call x1, Pallas kernels: 2.8 us -> 1.08 us  [project(): pl.pallas_call(project_kernel, in_specs=[VMEM] * 4, out_specs=VMEM, out_s...]
    ppermute x1, starting transfers between devices: 3.01 us -> 4.71 us  [on_device(): other = lax.ppermute(lent, 'tensor', swap(8))]
  transfers between devices with their start and end apart: 28 -> 28, of which waited for: 17 -> 15; matrix products, arithmetic and copies ran while one was open for 0% -> 0% of each run, Pallas kernels for 21% -> 21%
where the time goes in v2:
time: 117 us
  starting transfers between devices  47.2 us (40%)
  waiting for transfers between devices  32.9 us (28%)
  Pallas kernels  30 us (26%)
  between operations  2.91 us (2%)
  local copies, waits for them, and re-layouts  2.31 us (2%)
    ppermute x14, starting transfers between devices, z_hop(): return lax.ppermute(x, 'group', ring(2 * SPLIT, step, 2))  18.4 us
    pallas_call x6, Pallas kernels, backward(): pl.pallas_call(functools.partial(backward_kernel, kinds, scale, scale2, f...  16.2 us
    ppermute x7, waiting for transfers between devices, body(): got[step] = lax.ppermute(pieces[step], 'group', pairs)  15.2 us
    ppermute x3, waiting for transfers between devices, on_device(): lax.ppermute(shares[k], 'tensor', ring(8, k, 2)).astype(jnp.float32)  10.1 us
    pallas_call x5, Pallas kernels, forward(): pl.pallas_call(functools.partial(forward_kernel, kinds, scale2, first, la...  8.98 us
    ppermute x1, starting transfers between devices, on_device(): beside = lax.ppermute(summed, 'tensor', swap(8))  8.66 us
    ppermute x14, waiting for transfers between devices, z_hop(): return lax.ppermute(x, 'group', ring(2 * SPLIT, step, 2))  6.53 us
    ppermute x7, starting transfers between devices, body(): got[step] = lax.ppermute(pieces[step], 'group', pairs)  5.92 us
  transfers between devices with their start and end apart: 28, of which 15 were waited for; matrix products, arithmetic and copies ran while one was open for 0% of the time, Pallas kernels for 21%

profile of v2, /device:TPU:1, one launch (start us, length us, event | category | flops | bytes accessed | tf_op | source)
XLA Modules:
  0.0 116.5 jit_solution(16003987476673261615)
XLA Ops:
  1.3 1.4 %shard_map.103 = (bf16[2,256,128]{2,1,0:T(8,128)(2,1)S(1)}, bf16[2,256,128]{2,1,0:T(8,128)(2,1)S(1)}, bf16[2,256,128]{2,1,0:T(8,128)(2,1)S(1)}, bf16[2,256,128]{...) custom-call(bf16[2,2048,128]{2,1,0:T(8,128)(2,1)} %bitcast.49), custom_call_target="tpu_custom_call" | custom-call | tf_op jit(solution)/shard_map/pallas_call | solution.py:165
  2.7 21.3 %conditional.1 = (bf16[2,256,128]{2,1,0:T(8,128)(2,1)S(1)}) conditional(s32[]{:T(128)} %clamp.3, (s32[]{:T(128)}, bf16[2,256,128]{2,1,0:T(8,128)(2,1)S(1)}, bf16[2,256,128]{2,1,0:T(8,128)(2,1)S(1)}, bf16[2,256,128]{2,1,0:T(8,128)(2,1)S(1)}, bf16[2,256,128]{2,1,0:T(8,128)(2,1)S(1)}, ...), branch_computations={%region_0.1_spmd, %region_1.2_spmd, %region_2.3_spmd, %region_3.4_... | conditional | flops 458759 | bytes 4850022 | solution.py:267
  2.7 1.3 %collective-permute-start.7 = (bf16[2,256,128]{2,1,0:T(8,128)(2,1)S(1)}, bf16[2,256,128]{2,1,0:T(8,128)(2,1)S(1)}, u32[]{:S(2)}, u32[]{:S(2)}) collective-permute-start(bf16[2,256,128]{2,1,0:T(8,128)(2,1)S(1)} %get-tuple-element.87), channel_id=1, source_target_pairs={{16,0},{24,8},{80,64},{88,72},{17,1},{25,9},{81,65},{89,73},{18,2}... | collective-permute-start | bytes 393224 | tf_op jit(solution)/shard_map/cond/branch_1_fun/ppermute | solution.py:259
  4.0 0.7 collective-permute-start.8
  4.7 0.7 collective-permute-start.9
  5.4 0.7 collective-permute-start.10
  6.1 1.3 %collective-permute-start.11 = (bf16[2,256,128]{2,1,0:T(8,128)(2,1)S(1)}, bf16[2,256,128]{2,1,0:T(8,128)(2,1)S(1)}, u32[]{:S(2)}, u32[]{:S(2)}) collective-permute-start(bf16[2,256,128]{2,1,0:T(8,128)(2,1)S(1)} %get-tuple-element.91), channel_id=1, source_target_pairs={{16,64},{24,72},{80,0},{88,8},{17,65},{25,73},{81,1},{89,9},{18,66... | collective-permute-start | bytes 393224 | tf_op jit(solution)/shard_map/cond/branch_1_fun/ppermute | solution.py:259
  7.4 1.5 %collective-permute-done.7 = bf16[2,256,128]{2,1,0:T(8,128)(2,1)S(1)} collective-permute-done((bf16[2,256,128]{2,1,0:T(8,128)(2,1)S(1)}, bf16[2,256,128]{2,1,0:T(8,128)(2,1)S(1)}, u32[]{:S(2)}, u32[]{:S(2)}) %collective-permute-start.7) | collective-permute-done | bytes 131104 | tf_op jit(solution)/shard_map/cond/branch_1_fun/ppermute | solution.py:259
  8.8 0.7 collective-permute-start.12
  9.5 0.7 collective-permute-start.13
  10.2 13.7 %collective-permute-done.11 = bf16[2,256,128]{2,1,0:T(8,128)(2,1)S(1)} collective-permute-done((bf16[2,256,128]{2,1,0:T(8,128)(2,1)S(1)}, bf16[2,256,128]{2,1,0:T(8,128)(2,1)S(1)}, u32[]{:S(2)}, u32[]{:S(2)}) %collective-permute-start.11) | collective-permute-done | bytes 131104 | tf_op jit(solution)/shard_map/cond/branch_1_fun/ppermute | solution.py:259
  24.1 2.8 %collective-permute-start.28 = (bf16[2,256,128]{2,1,0:T(8,128)(2,1)S(1)}, bf16[2,256,128]{2,1,0:T(8,128)(2,1)S(1)}, u32[]{:S(2)}, u32[]{:S(2)}) collective-permute-start(bf16[2,256,128]{2,1,0:T(8,128)(2,1)S(1)} %get-tuple-element.239), channel_id=1, source_target_pairs={{0,8},{8,0},{16,24},{24,16},{32,40},{40,32},{48,56},{56,48},{64,72... | collective-permute-start | bytes 393224 | tf_op jit(solution)/shard_map/ppermute | solution.py:232
  26.9 2.4 %shard_map.104 = bf16[2,4,640,128]{3,2,1,0:T(8,128)(2,1)} custom-call(bf16[2,4,2,640,128]{4,3,2,1,0:T(8,128)(2,1)} %bitcast.23), custom_call_target="tpu_custom_call" | custom-call | tf_op jit(solution)/shard_map/pallas_call | solution.py:186
  29.5 4.7 %collective-permute-start.31 = (bf16[2,4,640,128]{3,2,1,0:T(8,128)(2,1)}, bf16[2,4,640,128]{3,2,1,0:T(8,128)(2,1)S(1)}, u32[]{:S(2)}, u32[]{:S(2)}) collective-permute-start(bf16[2,4,640,128]{3,2,1,0:T(8,128)(2,1)} %shard_map.104), channel_id=1, source_target_pairs={{0,1},{1,0},{2,3},{3,2},{4,5},{5,4},{6,7},{7,6},{8,9},{9,8},{10,11... | collective-permute-start | bytes 3932168 | tf_op jit(solution)/shard_map/ppermute | solution.py:276
  34.2 1.5 %collective-permute-start.29 = (bf16[2,256,128]{2,1,0:T(8,128)(2,1)S(1)}, bf16[2,256,128]{2,1,0:T(8,128)(2,1)S(1)}, u32[]{:S(2)}, u32[]{:S(2)}) collective-permute-start(bf16[2,256,128]{2,1,0:T(8,128)(2,1)S(1)} %broadcast_select_fusion.refs_1_.refs_0_), channel_id=1, source_target_pairs={{0,16},{8,24},{16,32},{24,40},{32,48},{40,56},{48,64},{56,72},{64,... | collective-permute-start | bytes 393224 | tf_op jit(solution)/shard_map/ppermute | solution.py:228
  35.8 1.7 %collective-permute-start.30 = (bf16[2,256,128]{2,1,0:T(8,128)(2,1)S(1)}, bf16[2,256,128]{2,1,0:T(8,128)(2,1)S(1)}, u32[]{:S(2)}, u32[]{:S(2)}) collective-permute-start(bf16[2,256,128]{2,1,0:T(8,128)(2,1)S(1)} %broadcast_select_fusion.refs_1_.refs_0_), channel_id=1, source_target_pairs={{0,112},{8,120},{16,0},{24,8},{32,16},{40,24},{48,32},{56,40},{64,... | collective-permute-start | bytes 393224 | tf_op jit(solution)/shard_map/ppermute | solution.py:228
  38.7 2.1 %shard_map.105.refs_2_ = f32[4,8,512]{2,1,0:T(8,128)S(1)} custom-call(s32[1]{0:T(128)S(6)} %copy.16.live_ref, s32[1]{0:T(128)S(6)} %copy.15.rows_ref, bf16[512,512]{1,0:T(8,128)(2,1)S(1)} %bitcast.25, bf16[512,512]{1,0:T(8,128)(2,1)S(1)} %bitcast.36, bf16[2,512,128]{2,1,0:T(8,128)(2,1)S(1)} %bitcast.47, ...), custom_call_target="tpu_custom_call" | custom-call | flops 805306368 | bytes 1048576 | tf_op jit(solution)/shard_map/pallas_call | solution.py:79
  41.6 1.1 collective-permute-start.32
  42.8 1.5 %collective-permute-start.33 = (bf16[2,256,128]{2,1,0:T(8,128)(2,1)S(1)}, bf16[2,256,128]{2,1,0:T(8,128)(2,1)S(1)}, u32[]{:S(2)}, u32[]{:S(2)}) collective-permute-start(bf16[2,256,128]{2,1,0:T(8,128)(2,1)S(1)} %collective-permute-done.30.refs_1_.refs_0_), channel_id=1, source_target_pairs={{0,112},{8,120},{16,0},{24,8},{32,16},{40,24},{48,32},{56,40},{64,... | collective-permute-start | bytes 393224 | tf_op jit(solution)/shard_map/ppermute | solution.py:228
  44.3 1.9 %shard_map.106.refs_2_ = f32[4,8,512]{2,1,0:T(8,128)S(1)} custom-call(s32[1]{0:T(128)S(6)} %copy.16.live_ref, s32[1]{0:T(128)S(6)} %copy.15.rows_ref, bf16[512,512]{1,0:T(8,128)(2,1)S(1)} %bitcast.26, bf16[512,512]{1,0:T(8,128)(2,1)S(1)} %bitcast.37, bf16[2,256,128]{2,1,0:T(8,128)(2,1)S(1)} %collective-permute-done.29.refs_0_.refs_1_, ...), custom_call_target="tpu_custom_call" | custom-call | flops 536870912 | bytes 1048576 | tf_op jit(solution)/shard_map/pallas_call | solution.py:79
  46.2 0.8 collective-permute-done.32.refs_0_.refs_1_
  47.3 2.5 %collective-permute-start.35 = (bf16[2,256,128]{2,1,0:T(8,128)(2,1)S(1)}, bf16[2,256,128]{2,1,0:T(8,128)(2,1)S(1)}, u32[]{:S(2)}, u32[]{:S(2)}) collective-permute-start(bf16[2,256,128]{2,1,0:T(8,128)(2,1)S(1)} %collective-permute-done.33.refs_1_.refs_0_), channel_id=1, source_target_pairs={{0,112},{8,120},{16,0},{24,8},{32,16},{40,24},{48,32},{56,40},{64,... | collective-permute-start | bytes 393224 | tf_op jit(solution)/shard_map/ppermute | solution.py:228
  49.8 1.9 %shard_map.107.refs_2_ = f32[4,8,512]{2,1,0:T(8,128)S(1)} custom-call(s32[1]{0:T(128)S(6)} %copy.16.live_ref, s32[1]{0:T(128)S(6)} %copy.15.rows_ref, bf16[512,512]{1,0:T(8,128)(2,1)S(1)} %bitcast.27, bf16[512,512]{1,0:T(8,128)(2,1)S(1)} %bitcast.38, bf16[2,256,128]{2,1,0:T(8,128)(2,1)S(1)} %collective-permute-done.32.refs_0_.refs_1_, ...), custom_call_target="tpu_custom_call" | custom-call | flops 536870912 | bytes 1048576 | tf_op jit(solution)/shard_map/pallas_call | solution.py:79
  52.1 1.2 %collective-permute-start.36 = (bf16[2,256,128]{2,1,0:T(8,128)(2,1)S(1)}, bf16[2,256,128]{2,1,0:T(8,128)(2,1)S(1)}, u32[]{:S(2)}, u32[]{:S(2)}) collective-permute-start(bf16[2,256,128]{2,1,0:T(8,128)(2,1)S(1)} %collective-permute-done.34.refs_0_.refs_1_), channel_id=1, source_target_pairs={{0,16},{8,24},{16,32},{24,40},{32,48},{40,56},{48,64},{56,72},{64,... | collective-permute-start | bytes 393224 | tf_op jit(solution)/shard_map/ppermute | solution.py:228
  53.3 1.9 %shard_map.108.refs_1_ = f32[4,8,512]{2,1,0:T(8,128)S(1)} custom-call(s32[1]{0:T(128)S(6)} %copy.16.live_ref, s32[1]{0:T(128)S(6)} %copy.15.rows_ref, bf16[512,512]{1,0:T(8,128)(2,1)S(1)} %bitcast.28, bf16[512,512]{1,0:T(8,128)(2,1)S(1)} %bitcast.39, bf16[2,256,128]{2,1,0:T(8,128)(2,1)S(1)} %collective-permute-done.34.refs_0_.refs_1_, ...), custom_call_target="tpu_custom_call" | custom-call | flops 536870912 | bytes 1048576 | tf_op jit(solution)/shard_map/pallas_call | solution.py:79
  55.2 1.9 %collective-permute-done.36.refs_0_ = bf16[2,256,128]{2,1,0:T(8,128)(2,1)S(1)} collective-permute-done((bf16[2,256,128]{2,1,0:T(8,128)(2,1)S(1)}, bf16[2,256,128]{2,1,0:T(8,128)(2,1)S(1)}, u32[]{:S(2)}, u32[]{:S(2)}) %collective-permute-start.36) | collective-permute-done | bytes 131104 | tf_op jit(solution)/shard_map/ppermute | solution.py:228
  57.1 1.1 shard_map.109.stat_ref
  58.3 1.6 %shard_map.110 = (f32[512,512]{1,0:T(8,128)S(1)}, bf16[2,256,128]{2,1,0:T(8,128)(2,1)S(1)}) custom-call(s32[1]{0:T(128)S(6)} %copy.16.live_ref, s32[1]{0:T(128)S(6)} %copy.15.rows_ref, bf16[512,512]{1,0:T(8,128)(2,1)S(1)} %bitcast.30, bf16[512,512]{1,0:T(8,128)(2,1)S(1)} %bitcast.41, f32[4,8,512]{2,1,0:T(8,128)S(1)} %shard_map.109.stat_ref, ...), custom_call_target="tpu_custom_call" | custom-call | flops 671088640 | bytes 1048576 | tf_op jit(solution)/shard_map/pallas_call | solution.py:138
  60.0 3.0 %shard_map.111 = (f32[512,512]{1,0:T(8,128)S(1)}, bf16[2,256,128]{2,1,0:T(8,128)(2,1)S(1)}, bf16[2,256,128]{2,1,0:T(8,128)(2,1)S(1)}) custom-call(s32[1]{0:T(128)S(6)} %copy.16.live_ref, s32[1]{0:T(128)S(6)} %copy.15.rows_ref, bf16[512,512]{1,0:T(8,128)(2,1)S(1)} %bitcast.31, bf16[512,512]{1,0:T(8,128)(2,1)S(1)} %bitcast.42, ...), custom_call_target="tpu_custom_call" | custom-call | flops 1342177280 | bytes 1048576 | tf_op jit(solution)/shard_map/pallas_call | solution.py:138
  63.0 2.0 %collective-permute-done.37 = bf16[2,256,128]{2,1,0:T(8,128)(2,1)S(1)} collective-permute-done((bf16[2,256,128]{2,1,0:T(8,128)(2,1)S(1)}, bf16[2,256,128]{2,1,0:T(8,128)(2,1)S(1)}, u32[]{:S(2)}, u32[]{:S(2)}) %collective-permute-start.37) | collective-permute-done | bytes 131104 | tf_op jit(solution)/shard_map/ppermute | solution.py:228
  65.1 2.7 %collective-permute-start.41 = (bf16[2,256,128]{2,1,0:T(8,128)(2,1)S(1)}, bf16[2,256,128]{2,1,0:T(8,128)(2,1)S(1)}, u32[]{:S(2)}, u32[]{:S(2)}) collective-permute-start(bf16[2,256,128]{2,1,0:T(8,128)(2,1)S(1)} %get-tuple-element.222), channel_id=1, source_target_pairs={{0,112},{8,120},{16,0},{24,8},{32,16},{40,24},{48,32},{56,40},{64,... | collective-permute-start | bytes 393224 | tf_op jit(solution)/shard_map/ppermute | solution.py:228
  67.8 3.0 %shard_map.112 = (f32[512,512]{1,0:T(8,128)S(1)}, bf16[2,256,128]{2,1,0:T(8,128)(2,1)S(1)}, bf16[2,256,128]{2,1,0:T(8,128)(2,1)S(1)}) custom-call(s32[1]{0:T(128)S(6)} %copy.16.live_ref, s32[1]{0:T(128)S(6)} %copy.15.rows_ref, bf16[512,512]{1,0:T(8,128)(2,1)S(1)} %bitcast.32, bf16[512,512]{1,0:T(8,128)(2,1)S(1)} %bitcast.43, ...), custom_call_target="tpu_custom_call" | custom-call | flops 1342177280 | bytes 1048576 | tf_op jit(solution)/shard_map/pallas_call | solution.py:138
  71.4 2.7 %collective-permute-start.42 = (bf16[2,256,128]{2,1,0:T(8,128)(2,1)S(1)}, bf16[2,256,128]{2,1,0:T(8,128)(2,1)S(1)}, u32[]{:S(2)}, u32[]{:S(2)}) collective-permute-start(bf16[2,256,128]{2,1,0:T(8,128)(2,1)S(1)} %add_convert_fusion.1), channel_id=1, source_target_pairs={{0,112},{8,120},{16,0},{24,8},{32,16},{40,24},{48,32},{56,40},{64,... | collective-permute-start | bytes 393224 | tf_op jit(solution)/shard_map/ppermute | solution.py:228
  74.2 3.0 %shard_map.113 = (f32[512,512]{1,0:T(8,128)S(1)}, bf16[2,256,128]{2,1,0:T(8,128)(2,1)S(1)}, bf16[2,256,128]{2,1,0:T(8,128)(2,1)S(1)}) custom-call(s32[1]{0:T(128)S(6)} %copy.16.live_ref, s32[1]{0:T(128)S(6)} %copy.15.rows_ref, bf16[512,512]{1,0:T(8,128)(2,1)S(1)} %bitcast.33, bf16[512,512]{1,0:T(8,128)(2,1)S(1)} %bitcast.44, ...), custom_call_target="tpu_custom_call" | custom-call | flops 1342177280 | bytes 1048576 | tf_op jit(solution)/shard_map/pallas_call | solution.py:138
  77.2 1.0 copy-done.4
  78.4 2.9 %collective-permute-start.43 = (bf16[2,256,128]{2,1,0:T(8,128)(2,1)S(1)}, bf16[2,256,128]{2,1,0:T(8,128)(2,1)S(1)}, u32[]{:S(2)}, u32[]{:S(2)}) collective-permute-start(bf16[2,256,128]{2,1,0:T(8,128)(2,1)S(1)} %add_convert_fusion), channel_id=1, source_target_pairs={{0,112},{8,120},{16,0},{24,8},{32,16},{40,24},{48,32},{56,40},{64,... | collective-permute-start | bytes 393224 | tf_op jit(solution)/shard_map/ppermute | solution.py:228
  81.3 1.2 %copy-done.5 = f32[512,512]{1,0:T(8,128)S(1)} copy-done((f32[512,512]{1,0:T(8,128)S(1)}, f32[512,512]{1,0:T(8,128)}, u32[]{:S(2)}) %copy-start.5) | copy-done | bytes 1048600
  82.6 1.6 %shard_map.114 = (f32[512,512]{1,0:T(8,128)S(1)}, bf16[2,256,128]{2,1,0:T(8,128)(2,1)S(1)}) custom-call(s32[1]{0:T(128)S(6)} %copy.16.live_ref, s32[1]{0:T(128)S(6)} %copy.15.rows_ref, bf16[512,512]{1,0:T(8,128)(2,1)S(1)} %bitcast.34, bf16[512,512]{1,0:T(8,128)(2,1)S(1)} %bitcast.45, f32[4,8,512]{2,1,0:T(8,128)S(1)} %shard_map.109.stat_ref, ...), custom_call_target="tpu_custom_call" | custom-call | flops 671088640 | bytes 1048576 | tf_op jit(solution)/shard_map/pallas_call | solution.py:138
  84.3 2.8 %collective-permute-start.44 = (bf16[2,128,128]{2,1,0:T(8,128)(2,1)S(1)}, bf16[2,128,128]{2,1,0:T(8,128)(2,1)S(1)}, u32[]{:S(2)}, u32[]{:S(2)}) collective-permute-start(bf16[2,128,128]{2,1,0:T(8,128)(2,1)S(1)} %add_convert_fusion.6), channel_id=1, source_target_pairs={{0,8},{8,0},{16,24},{24,16},{32,40},{40,32},{48,56},{56,48},{64,72... | collective-permute-start | bytes 196616 | tf_op jit(solution)/shard_map/ppermute | solution.py:232
  87.2 3.9 %shard_map.115 = (bf16[512,512]{1,0:T(8,128)(2,1)}, bf16[2,512,128]{2,1,0:T(8,128)(2,1)}) custom-call(s32[1]{0:T(128)S(6)} %copy.16.live_ref, s32[1]{0:T(128)S(6)} %copy.15.rows_ref, bf16[512,512]{1,0:T(8,128)(2,1)S(1)} %bitcast.35, bf16[512,512]{1,0:T(8,128)(2,1)S(1)} %bitcast.46, f32[4,8,512]{2,1,0:T(8,128)S(1)} %shard_map.109.stat_ref, ...), custom_call_target="tpu_custom_call" | custom-call | flops 1342177280 | bytes 1048576 | tf_op jit(solution)/shard_map/pallas_call | solution.py:138
  91.2 8.7 %collective-permute-start.45 = (bf16[2,128,128]{2,1,0:T(8,128)(2,1)S(1)}, bf16[2,128,128]{2,1,0:T(8,128)(2,1)S(1)}, u32[]{:S(2)}, u32[]{:S(2)}) collective-permute-start(bf16[2,128,128]{2,1,0:T(8,128)(2,1)S(1)} %add_convert_fusion.5.summed_ref), channel_id=1, source_target_pairs={{0,1},{1,0},{2,3},{3,2},{4,5},{5,4},{6,7},{7,6},{8,9},{9,8},{10,11... | collective-permute-start | bytes 196616 | tf_op jit(solution)/shard_map/ppermute | solution.py:316
  99.8 0.9 collective-permute-done.45.beside_ref
  100.7 1.1 shard_map.116
  101.9 2.8 %collective-permute-start.48 = (bf16[128,640]{1,0:T(8,128)(2,1)S(1)}, bf16[128,640]{1,0:T(8,128)(2,1)S(1)}, u32[]{:S(2)}, u32[]{:S(2)}) collective-permute-start(bf16[128,640]{1,0:T(8,128)(2,1)S(1)} %get-tuple-element.237), channel_id=1, source_target_pairs={{0,6},{1,7},{2,0},{3,1},{4,2},{5,3},{6,4},{7,5},{8,14},{9,15},{10,... | collective-permute-start | bytes 491528 | tf_op jit(solution)/shard_map/ppermute | solution.py:320
  105.0 0.7 collective-permute-start.46
  105.7 5.5 %collective-permute-done.48 = bf16[128,640]{1,0:T(8,128)(2,1)S(1)} collective-permute-done((bf16[128,640]{1,0:T(8,128)(2,1)S(1)}, bf16[128,640]{1,0:T(8,128)(2,1)S(1)}, u32[]{:S(2)}, u32[]{:S(2)}) %collective-permute-start.48) | collective-permute-done | bytes 163872 | tf_op jit(solution)/shard_map/ppermute | solution.py:320
  111.3 4.5 %collective-permute-done.46 = bf16[128,640]{1,0:T(8,128)(2,1)S(1)} collective-permute-done((bf16[128,640]{1,0:T(8,128)(2,1)S(1)}, bf16[128,640]{1,0:T(8,128)(2,1)S(1)}, u32[]{:S(2)}, u32[]{:S(2)}) %collective-permute-start.46) | collective-permute-done | bytes 163872 | tf_op jit(solution)/shard_map/ppermute | solution.py:320
  115.8 0.8 fusion.2
  (46 shorter events, 3.3 us)
Async XLA Ops:
  2.7 6.1 %collective-permute-start.7 = (bf16[2,256,128]{2,1,0:T(8,128)(2,1)S(1)}, bf16[2,256,128]{2,1,0:T(8,128)(2,1)S(1)}, u32[]{:S(2)}, u32[]{:S(2)}) collective-permute-start(bf16[2,256,128]{2,1,0:T(8,128)(2,1)S(1)} %get-tuple-element.87), channel_id=1, source_target_pairs={{16,0},{24,8},{80,64},{88,72},{17,1},{25,9},{81,65},{89,73},{18,2}... | collective-permute-start | bytes 393224 | tf_op jit(solution)/shard_map/cond/branch_1_fun/ppermute | solution.py:259
  4.0 5.5 %collective-permute-start.8 = (bf16[2,256,128]{2,1,0:T(8,128)(2,1)S(1)}, bf16[2,256,128]{2,1,0:T(8,128)(2,1)S(1)}, u32[]{:S(2)}, u32[]{:S(2)}) collective-permute-start(bf16[2,256,128]{2,1,0:T(8,128)(2,1)S(1)} %get-tuple-element.88), channel_id=1, source_target_pairs={{16,112},{24,120},{80,48},{88,56},{17,113},{25,121},{81,49},{89,57... | collective-permute-start | bytes 393224 | tf_op jit(solution)/shard_map/cond/branch_1_fun/ppermute | solution.py:259
  4.7 5.5 %collective-permute-start.9 = (bf16[2,256,128]{2,1,0:T(8,128)(2,1)S(1)}, bf16[2,256,128]{2,1,0:T(8,128)(2,1)S(1)}, u32[]{:S(2)}, u32[]{:S(2)}) collective-permute-start(bf16[2,256,128]{2,1,0:T(8,128)(2,1)S(1)} %get-tuple-element.89), channel_id=1, source_target_pairs={{16,96},{24,104},{80,32},{88,40},{17,97},{25,105},{81,33},{89,41},... | collective-permute-start | bytes 393224 | tf_op jit(solution)/shard_map/cond/branch_1_fun/ppermute | solution.py:259
  5.4 4.8 %collective-permute-start.10 = (bf16[2,256,128]{2,1,0:T(8,128)(2,1)S(1)}, bf16[2,256,128]{2,1,0:T(8,128)(2,1)S(1)}, u32[]{:S(2)}, u32[]{:S(2)}) collective-permute-start(bf16[2,256,128]{2,1,0:T(8,128)(2,1)S(1)} %get-tuple-element.90), channel_id=1, source_target_pairs={{16,80},{24,88},{80,16},{88,24},{17,81},{25,89},{81,17},{89,25},{1... | collective-permute-start | bytes 393224 | tf_op jit(solution)/shard_map/cond/branch_1_fun/ppermute | solution.py:259
  6.1 17.9 %collective-permute-start.11 = (bf16[2,256,128]{2,1,0:T(8,128)(2,1)S(1)}, bf16[2,256,128]{2,1,0:T(8,128)(2,1)S(1)}, u32[]{:S(2)}, u32[]{:S(2)}) collective-permute-start(bf16[2,256,128]{2,1,0:T(8,128)(2,1)S(1)} %get-tuple-element.91), channel_id=1, source_target_pairs={{16,64},{24,72},{80,0},{88,8},{17,65},{25,73},{81,1},{89,9},{18,66... | collective-permute-start | bytes 393224 | tf_op jit(solution)/shard_map/cond/branch_1_fun/ppermute | solution.py:259
  8.8 15.1 %collective-permute-start.12 = (bf16[2,256,128]{2,1,0:T(8,128)(2,1)S(1)}, bf16[2,256,128]{2,1,0:T(8,128)(2,1)S(1)}, u32[]{:S(2)}, u32[]{:S(2)}) collective-permute-start(bf16[2,256,128]{2,1,0:T(8,128)(2,1)S(1)} %get-tuple-element.92), channel_id=1, source_target_pairs={{16,48},{24,56},{80,112},{88,120},{17,49},{25,57},{81,113},{89,121... | collective-permute-start | bytes 393224 | tf_op jit(solution)/shard_map/cond/branch_1_fun/ppermute | solution.py:259
  9.5 14.5 %collective-permute-start.13 = (bf16[2,256,128]{2,1,0:T(8,128)(2,1)S(1)}, bf16[2,256,128]{2,1,0:T(8,128)(2,1)S(1)}, u32[]{:S(2)}, u32[]{:S(2)}) collective-permute-start(bf16[2,256,128]{2,1,0:T(8,128)(2,1)S(1)} %get-tuple-element.93), channel_id=1, source_target_pairs={{16,32},{24,40},{80,96},{88,104},{17,33},{25,41},{81,97},{89,105},... | collective-permute-start | bytes 393224 | tf_op jit(solution)/shard_map/cond/branch_1_fun/ppermute | solution.py:259
  24.0 14.7 %copy-start.1 = (bf16[1,512,512]{2,1,0:T(8,128)(2,1)S(1)}, bf16[1,512,512]{2,1,0:T(8,128)(2,1)}, u32[]{:S(2)}) copy-start(bf16[1,512,512]{2,1,0:T(8,128)(2,1)} %param.12) | copy-start | bytes 1572868
  24.1 14.7 %copy-start.2 = (bf16[1,512,512]{2,1,0:T(8,128)(2,1)S(1)}, bf16[1,512,512]{2,1,0:T(8,128)(2,1)}, u32[]{:S(2)}) copy-start(bf16[1,512,512]{2,1,0:T(8,128)(2,1)} %param.14) | copy-start | bytes 1572868
  24.1 14.7 %copy-start.3 = (bf16[1,2,512,128]{3,2,1,0:T(8,128)(2,1)S(1)}, bf16[1,2,512,128]{3,2,1,0:T(8,128)(2,1)}, u32[]{:S(2)}) copy-start(bf16[1,2,512,128]{3,2,1,0:T(8,128)(2,1)} %param.13) | copy-start | bytes 786436
  24.1 5.4 %collective-permute-start.28 = (bf16[2,256,128]{2,1,0:T(8,128)(2,1)S(1)}, bf16[2,256,128]{2,1,0:T(8,128)(2,1)S(1)}, u32[]{:S(2)}, u32[]{:S(2)}) collective-permute-start(bf16[2,256,128]{2,1,0:T(8,128)(2,1)S(1)} %get-tuple-element.239), channel_id=1, source_target_pairs={{0,8},{8,0},{16,24},{24,16},{32,40},{40,32},{48,56},{56,48},{64,72... | collective-permute-start | bytes 393224 | tf_op jit(solution)/shard_map/ppermute | solution.py:232
  29.5 12.1 %collective-permute-start.31 = (bf16[2,4,640,128]{3,2,1,0:T(8,128)(2,1)}, bf16[2,4,640,128]{3,2,1,0:T(8,128)(2,1)S(1)}, u32[]{:S(2)}, u32[]{:S(2)}) collective-permute-start(bf16[2,4,640,128]{3,2,1,0:T(8,128)(2,1)} %shard_map.104), channel_id=1, source_target_pairs={{0,1},{1,0},{2,3},{3,2},{4,5},{5,4},{6,7},{7,6},{8,9},{9,8},{10,11... | collective-permute-start | bytes 3932168 | tf_op jit(solution)/shard_map/ppermute | solution.py:276
  34.2 7.0 %collective-permute-start.29 = (bf16[2,256,128]{2,1,0:T(8,128)(2,1)S(1)}, bf16[2,256,128]{2,1,0:T(8,128)(2,1)S(1)}, u32[]{:S(2)}, u32[]{:S(2)}) collective-permute-start(bf16[2,256,128]{2,1,0:T(8,128)(2,1)S(1)} %broadcast_select_fusion.refs_1_.refs_0_), channel_id=1, source_target_pairs={{0,16},{8,24},{16,32},{24,40},{32,48},{40,56},{48,64},{56,72},{64,... | collective-permute-start | bytes 393224 | tf_op jit(solution)/shard_map/ppermute | solution.py:228
  35.8 5.9 %collective-permute-start.30 = (bf16[2,256,128]{2,1,0:T(8,128)(2,1)S(1)}, bf16[2,256,128]{2,1,0:T(8,128)(2,1)S(1)}, u32[]{:S(2)}, u32[]{:S(2)}) collective-permute-start(bf16[2,256,128]{2,1,0:T(8,128)(2,1)S(1)} %broadcast_select_fusion.refs_1_.refs_0_), channel_id=1, source_target_pairs={{0,112},{8,120},{16,0},{24,8},{32,16},{40,24},{48,32},{56,40},{64,... | collective-permute-start | bytes 393224 | tf_op jit(solution)/shard_map/ppermute | solution.py:228
  41.6 5.5 %collective-permute-start.32 = (bf16[2,256,128]{2,1,0:T(8,128)(2,1)S(1)}, bf16[2,256,128]{2,1,0:T(8,128)(2,1)S(1)}, u32[]{:S(2)}, u32[]{:S(2)}) collective-permute-start(bf16[2,256,128]{2,1,0:T(8,128)(2,1)S(1)} %collective-permute-done.29.refs_0_.refs_1_), channel_id=1, source_target_pairs={{0,16},{8,24},{16,32},{24,40},{32,48},{40,56},{48,64},{56,72},{64,... | collective-permute-start | bytes 393224 | tf_op jit(solution)/shard_map/ppermute | solution.py:228
  42.8 4.3 %collective-permute-start.33 = (bf16[2,256,128]{2,1,0:T(8,128)(2,1)S(1)}, bf16[2,256,128]{2,1,0:T(8,128)(2,1)S(1)}, u32[]{:S(2)}, u32[]{:S(2)}) collective-permute-start(bf16[2,256,128]{2,1,0:T(8,128)(2,1)S(1)} %collective-permute-done.30.refs_1_.refs_0_), channel_id=1, source_target_pairs={{0,112},{8,120},{16,0},{24,8},{32,16},{40,24},{48,32},{56,40},{64,... | collective-permute-start | bytes 393224 | tf_op jit(solution)/shard_map/ppermute | solution.py:228
  47.1 5.0 %collective-permute-start.34 = (bf16[2,256,128]{2,1,0:T(8,128)(2,1)S(1)}, bf16[2,256,128]{2,1,0:T(8,128)(2,1)S(1)}, u32[]{:S(2)}, u32[]{:S(2)}) collective-permute-start(bf16[2,256,128]{2,1,0:T(8,128)(2,1)S(1)} %collective-permute-done.32.refs_0_.refs_1_), channel_id=1, source_target_pairs={{0,16},{8,24},{16,32},{24,40},{32,48},{40,56},{48,64},{56,72},{64,... | collective-permute-start | bytes 393224 | tf_op jit(solution)/shard_map/ppermute | solution.py:228
  47.3 4.8 %collective-permute-start.35 = (bf16[2,256,128]{2,1,0:T(8,128)(2,1)S(1)}, bf16[2,256,128]{2,1,0:T(8,128)(2,1)S(1)}, u32[]{:S(2)}, u32[]{:S(2)}) collective-permute-start(bf16[2,256,128]{2,1,0:T(8,128)(2,1)S(1)} %collective-permute-done.33.refs_1_.refs_0_), channel_id=1, source_target_pairs={{0,112},{8,120},{16,0},{24,8},{32,16},{40,24},{48,32},{56,40},{64,... | collective-permute-start | bytes 393224 | tf_op jit(solution)/shard_map/ppermute | solution.py:228
  52.1 5.0 %collective-permute-start.36 = (bf16[2,256,128]{2,1,0:T(8,128)(2,1)S(1)}, bf16[2,256,128]{2,1,0:T(8,128)(2,1)S(1)}, u32[]{:S(2)}, u32[]{:S(2)}) collective-permute-start(bf16[2,256,128]{2,1,0:T(8,128)(2,1)S(1)} %collective-permute-done.34.refs_0_.refs_1_), channel_id=1, source_target_pairs={{0,16},{8,24},{16,32},{24,40},{32,48},{40,56},{48,64},{56,72},{64,... | collective-permute-start | bytes 393224 | tf_op jit(solution)/shard_map/ppermute | solution.py:228
  59.9 5.1 %collective-permute-start.37 = (bf16[2,256,128]{2,1,0:T(8,128)(2,1)S(1)}, bf16[2,256,128]{2,1,0:T(8,128)(2,1)S(1)}, u32[]{:S(2)}, u32[]{:S(2)}) collective-permute-start(bf16[2,256,128]{2,1,0:T(8,128)(2,1)S(1)} %get-tuple-element.201), channel_id=1, source_target_pairs={{0,16},{8,24},{16,32},{24,40},{32,48},{40,56},{48,64},{56,72},{64,... | collective-permute-start | bytes 393224 | tf_op jit(solution)/shard_map/ppermute | solution.py:228
  65.1 6.2 %collective-permute-start.38 = (bf16[2,256,128]{2,1,0:T(8,128)(2,1)S(1)}, bf16[2,256,128]{2,1,0:T(8,128)(2,1)S(1)}, u32[]{:S(2)}, u32[]{:S(2)}) collective-permute-start(bf16[2,256,128]{2,1,0:T(8,128)(2,1)S(1)} %add_convert_fusion.4), channel_id=1, source_target_pairs={{0,16},{8,24},{16,32},{24,40},{32,48},{40,56},{48,64},{56,72},{64,... | collective-permute-start | bytes 393224 | tf_op jit(solution)/shard_map/ppermute | solution.py:228
  65.1 6.2 %collective-permute-start.41 = (bf16[2,256,128]{2,1,0:T(8,128)(2,1)S(1)}, bf16[2,256,128]{2,1,0:T(8,128)(2,1)S(1)}, u32[]{:S(2)}, u32[]{:S(2)}) collective-permute-start(bf16[2,256,128]{2,1,0:T(8,128)(2,1)S(1)} %get-tuple-element.222), channel_id=1, source_target_pairs={{0,112},{8,120},{16,0},{24,8},{32,16},{40,24},{48,32},{56,40},{64,... | collective-permute-start | bytes 393224 | tf_op jit(solution)/shard_map/ppermute | solution.py:228
  71.3 6.9 %collective-permute-start.39 = (bf16[2,256,128]{2,1,0:T(8,128)(2,1)S(1)}, bf16[2,256,128]{2,1,0:T(8,128)(2,1)S(1)}, u32[]{:S(2)}, u32[]{:S(2)}) collective-permute-start(bf16[2,256,128]{2,1,0:T(8,128)(2,1)S(1)} %add_convert_fusion.3), channel_id=1, source_target_pairs={{0,16},{8,24},{16,32},{24,40},{32,48},{40,56},{48,64},{56,72},{64,... | collective-permute-start | bytes 393224 | tf_op jit(solution)/shard_map/ppermute | solution.py:228
  71.4 6.9 %collective-permute-start.42 = (bf16[2,256,128]{2,1,0:T(8,128)(2,1)S(1)}, bf16[2,256,128]{2,1,0:T(8,128)(2,1)S(1)}, u32[]{:S(2)}, u32[]{:S(2)}) collective-permute-start(bf16[2,256,128]{2,1,0:T(8,128)(2,1)S(1)} %add_convert_fusion.1), channel_id=1, source_target_pairs={{0,112},{8,120},{16,0},{24,8},{32,16},{40,24},{48,32},{56,40},{64,... | collective-permute-start | bytes 393224 | tf_op jit(solution)/shard_map/ppermute | solution.py:228
  77.2 1.0 copy-start.4
  78.2 6.1 %collective-permute-start.40 = (bf16[2,256,128]{2,1,0:T(8,128)(2,1)S(1)}, bf16[2,256,128]{2,1,0:T(8,128)(2,1)S(1)}, u32[]{:S(2)}, u32[]{:S(2)}) collective-permute-start(bf16[2,256,128]{2,1,0:T(8,128)(2,1)S(1)} %add_convert_fusion.2), channel_id=1, source_target_pairs={{0,16},{8,24},{16,32},{24,40},{32,48},{40,56},{48,64},{56,72},{64,... | collective-permute-start | bytes 393224 | tf_op jit(solution)/shard_map/ppermute | solution.py:228
  78.4 5.9 %collective-permute-start.43 = (bf16[2,256,128]{2,1,0:T(8,128)(2,1)S(1)}, bf16[2,256,128]{2,1,0:T(8,128)(2,1)S(1)}, u32[]{:S(2)}, u32[]{:S(2)}) collective-permute-start(bf16[2,256,128]{2,1,0:T(8,128)(2,1)S(1)} %add_convert_fusion), channel_id=1, source_target_pairs={{0,112},{8,120},{16,0},{24,8},{32,16},{40,24},{48,32},{56,40},{64,... | collective-permute-start | bytes 393224 | tf_op jit(solution)/shard_map/ppermute | solution.py:228
  81.3 1.2 %copy-start.5 = (f32[512,512]{1,0:T(8,128)S(1)}, f32[512,512]{1,0:T(8,128)}, u32[]{:S(2)}) copy-start(f32[512,512]{1,0:T(8,128)} %copy-done.4) | copy-start | bytes 3145732
  84.3 6.8 %collective-permute-start.44 = (bf16[2,128,128]{2,1,0:T(8,128)(2,1)S(1)}, bf16[2,128,128]{2,1,0:T(8,128)(2,1)S(1)}, u32[]{:S(2)}, u32[]{:S(2)}) collective-permute-start(bf16[2,128,128]{2,1,0:T(8,128)(2,1)S(1)} %add_convert_fusion.6), channel_id=1, source_target_pairs={{0,8},{8,0},{16,24},{24,16},{32,40},{40,32},{48,56},{56,48},{64,72... | collective-permute-start | bytes 196616 | tf_op jit(solution)/shard_map/ppermute | solution.py:232
  87.2 13.5 %copy-start = (bf16[2,5120,128]{2,1,0:T(8,128)(2,1)S(1)}, bf16[2,5120,128]{2,1,0:T(8,128)(2,1)}, u32[]{:S(2)}) copy-start(bf16[2,5120,128]{2,1,0:T(8,128)(2,1)} %param.16) | copy-start | bytes 7864324
  91.2 9.6 %collective-permute-start.45 = (bf16[2,128,128]{2,1,0:T(8,128)(2,1)S(1)}, bf16[2,128,128]{2,1,0:T(8,128)(2,1)S(1)}, u32[]{:S(2)}, u32[]{:S(2)}) collective-permute-start(bf16[2,128,128]{2,1,0:T(8,128)(2,1)S(1)} %add_convert_fusion.5.summed_ref), channel_id=1, source_target_pairs={{0,1},{1,0},{2,3},{3,2},{4,5},{5,4},{6,7},{7,6},{8,9},{9,8},{10,11... | collective-permute-start | bytes 196616 | tf_op jit(solution)/shard_map/ppermute | solution.py:316
  101.9 9.4 %collective-permute-start.48 = (bf16[128,640]{1,0:T(8,128)(2,1)S(1)}, bf16[128,640]{1,0:T(8,128)(2,1)S(1)}, u32[]{:S(2)}, u32[]{:S(2)}) collective-permute-start(bf16[128,640]{1,0:T(8,128)(2,1)S(1)} %get-tuple-element.237), channel_id=1, source_target_pairs={{0,6},{1,7},{2,0},{3,1},{4,2},{5,3},{6,4},{7,5},{8,14},{9,15},{10,... | collective-permute-start | bytes 491528 | tf_op jit(solution)/shard_map/ppermute | solution.py:320
  104.6 6.6 %collective-permute-start.47 = (bf16[128,640]{1,0:T(8,128)(2,1)S(1)}, bf16[128,640]{1,0:T(8,128)(2,1)S(1)}, u32[]{:S(2)}, u32[]{:S(2)}) collective-permute-start(bf16[128,640]{1,0:T(8,128)(2,1)S(1)} %get-tuple-element.238), channel_id=1, source_target_pairs={{0,4},{1,5},{2,6},{3,7},{4,0},{5,1},{6,2},{7,3},{8,12},{9,13},{10,... | collective-permute-start | bytes 491528 | tf_op jit(solution)/shard_map/ppermute | solution.py:320
  105.0 10.8 %collective-permute-start.46 = (bf16[128,640]{1,0:T(8,128)(2,1)S(1)}, bf16[128,640]{1,0:T(8,128)(2,1)S(1)}, u32[]{:S(2)}, u32[]{:S(2)}) collective-permute-start(bf16[128,640]{1,0:T(8,128)(2,1)S(1)} %get-tuple-element.236), channel_id=1, source_target_pairs={{0,2},{1,3},{2,4},{3,5},{4,6},{5,7},{6,0},{7,1},{8,10},{9,11},{10,... | collective-permute-start | bytes 491528 | tf_op jit(solution)/shard_map/ppermute | solution.py:320

commit v3 on v2

--- a/solution.py
+++ b/solution.py
@@ -316,7 +316,7 @@
     beside = lax.ppermute(summed, "tensor", swap(8))
     shares = project(summed, beside, by_core, other)
     result = shares[0].astype(jnp.float32)
-    for k in (1, 2, 3):
+    for k in (2, 3, 1):
         result = result + lax.ppermute(shares[k], "tensor", ring(8, k, 2)).astype(jnp.float32)
     return dq[None], own_grad[None], result.astype(jnp.bfloat16)
 

time: 117 us -> 115 us (0.983)
  waiting for transfers between devices: 32.9 us -> 18.7 us
  starting transfers between devices: 47.2 us -> 60.2 us
    ppermute x7, starting transfers between devices: 5.92 us -> 17.9 us  [body(): got[step] = lax.ppermute(pieces[step], 'group', pairs)]
    ppermute x7, waiting for transfers between devices: 15.2 us -> 6.3 us  [body(): got[step] = lax.ppermute(pieces[step], 'group', pairs)]
    ppermute x3, waiting for transfers between devices: 10.1 us -> 7 us  [on_device(): lax.ppermute(shares[k], 'tensor', ring(8, k, 2)).astype(jnp.float32)]
    ppermute x14, waiting for transfers between devices: 6.53 us -> 4.28 us  [z_hop(): return lax.ppermute(x, 'group', ring(2 * SPLIT, step, 2))]
    ppermute x14, starting transfers between devices: 18.4 us -> 20.6 us  [z_hop(): return lax.ppermute(x, 'group', ring(2 * SPLIT, step, 2))]
    ppermute x1, starting transfers between devices: 4.71 us -> 3.01 us  [on_device(): other = lax.ppermute(lent, 'tensor', swap(8))]
  transfers between devices with their start and end apart: 28 -> 28, of which waited for: 15 -> 16; matrix products, arithmetic and copies ran while one was open for 0% -> 0% of each run, Pallas kernels for 21% -> 22%
where the time goes in v3:
time: 115 us
  starting transfers between devices  60.2 us (52%)
  Pallas kernels  30 us (26%)
  waiting for transfers between devices  18.7 us (16%)
  between operations  2.9 us (3%)
  local copies, waits for them, and re-layouts  2.31 us (2%)
    ppermute x14, starting transfers between devices, z_hop(): return lax.ppermute(x, 'group', ring(2 * SPLIT, step, 2))  20.6 us
    ppermute x7, starting transfers between devices, body(): got[step] = lax.ppermute(pieces[step], 'group', pairs)  17.9 us
    pallas_call x6, Pallas kernels, backward(): pl.pallas_call(functools.partial(backward_kernel, kinds, scale, scale2, f...  16.2 us
    pallas_call x5, Pallas kernels, forward(): pl.pallas_call(functools.partial(forward_kernel, kinds, scale2, first, la...  8.97 us
    ppermute x1, starting transfers between devices, on_device(): beside = lax.ppermute(summed, 'tensor', swap(8))  8.65 us
    ppermute x3, waiting for transfers between devices, on_device(): lax.ppermute(shares[k], 'tensor', ring(8, k, 2)).astype(jnp.float32)  7 us
    ppermute x7, waiting for transfers between devices, body(): got[step] = lax.ppermute(pieces[step], 'group', pairs)  6.3 us
    ppermute x2, starting transfers between devices, x_swap(): return lax.ppermute(x, 'group', swap(2 * SPLIT))  5.69 us
  transfers between devices with their start and end apart: 28, of which 16 were waited for; matrix products, arithmetic and copies ran while one was open for 0% of the time, Pallas kernels for 22%

profile of v3, /device:TPU:1, one launch (start us, length us, event | category | flops | bytes accessed | tf_op | source)
XLA Modules:
  0.0 115.3 jit_solution(16957624978416271123)
XLA Ops:
  1.3 1.4 %shard_map.103 = (bf16[2,256,128]{2,1,0:T(8,128)(2,1)S(1)}, bf16[2,256,128]{2,1,0:T(8,128)(2,1)S(1)}, bf16[2,256,128]{2,1,0:T(8,128)(2,1)S(1)}, bf16[2,256,128]{...) custom-call(bf16[2,2048,128]{2,1,0:T(8,128)(2,1)} %bitcast.49), custom_call_target="tpu_custom_call" | custom-call | tf_op jit(solution)/shard_map/pallas_call | solution.py:165
  2.7 24.3 %conditional.1 = (bf16[2,256,128]{2,1,0:T(8,128)(2,1)S(1)}) conditional(s32[]{:T(128)} %clamp.3, (s32[]{:T(128)}, bf16[2,256,128]{2,1,0:T(8,128)(2,1)S(1)}, bf16[2,256,128]{2,1,0:T(8,128)(2,1)S(1)}, bf16[2,256,128]{2,1,0:T(8,128)(2,1)S(1)}, bf16[2,256,128]{2,1,0:T(8,128)(2,1)S(1)}, ...), branch_computations={%region_0.1_spmd, %region_1.2_spmd, %region_2.3_spmd, %region_3.4_... | conditional | flops 458759 | bytes 4850022 | solution.py:267
  2.7 8.3 %collective-permute-start = (bf16[2,256,128]{2,1,0:T(8,128)(2,1)S(1)}, bf16[2,256,128]{2,1,0:T(8,128)(2,1)S(1)}, u32[]{:S(2)}, u32[]{:S(2)}) collective-permute-start(bf16[2,256,128]{2,1,0:T(8,128)(2,1)S(1)} %get-tuple-element.61), channel_id=1, source_target_pairs={{0,112},{8,120},{64,48},{72,56},{1,113},{9,121},{65,49},{73,57},{2... | collective-permute-start | bytes 393224 | tf_op jit(solution)/shard_map/cond/branch_0_fun/ppermute | solution.py:259
  11.1 1.3 %collective-permute-start.1 = (bf16[2,256,128]{2,1,0:T(8,128)(2,1)S(1)}, bf16[2,256,128]{2,1,0:T(8,128)(2,1)S(1)}, u32[]{:S(2)}, u32[]{:S(2)}) collective-permute-start(bf16[2,256,128]{2,1,0:T(8,128)(2,1)S(1)} %get-tuple-element.62), channel_id=1, source_target_pairs={{0,96},{8,104},{64,32},{72,40},{1,97},{9,105},{65,33},{73,41},{2,9... | collective-permute-start | bytes 393224 | tf_op jit(solution)/shard_map/cond/branch_0_fun/ppermute | solution.py:259
  12.4 1.3 %collective-permute-start.2 = (bf16[2,256,128]{2,1,0:T(8,128)(2,1)S(1)}, bf16[2,256,128]{2,1,0:T(8,128)(2,1)S(1)}, u32[]{:S(2)}, u32[]{:S(2)}) collective-permute-start(bf16[2,256,128]{2,1,0:T(8,128)(2,1)S(1)} %get-tuple-element.80), channel_id=1, source_target_pairs={{0,80},{8,88},{64,16},{72,24},{1,81},{9,89},{65,17},{73,25},{2,82}... | collective-permute-start | bytes 393224 | tf_op jit(solution)/shard_map/cond/branch_0_fun/ppermute | solution.py:259
  13.7 3.1 %collective-permute-start.3 = (bf16[2,256,128]{2,1,0:T(8,128)(2,1)S(1)}, bf16[2,256,128]{2,1,0:T(8,128)(2,1)S(1)}, u32[]{:S(2)}, u32[]{:S(2)}) collective-permute-start(bf16[2,256,128]{2,1,0:T(8,128)(2,1)S(1)} %get-tuple-element.81), channel_id=1, source_target_pairs={{0,64},{8,72},{64,0},{72,8},{1,65},{9,73},{65,1},{73,9},{2,66},{10... | collective-permute-start | bytes 393224 | tf_op jit(solution)/shard_map/cond/branch_0_fun/ppermute | solution.py:259
  16.7 1.3 %collective-permute-start.4 = (bf16[2,256,128]{2,1,0:T(8,128)(2,1)S(1)}, bf16[2,256,128]{2,1,0:T(8,128)(2,1)S(1)}, u32[]{:S(2)}, u32[]{:S(2)}) collective-permute-start(bf16[2,256,128]{2,1,0:T(8,128)(2,1)S(1)} %get-tuple-element.82), channel_id=1, source_target_pairs={{0,48},{8,56},{64,112},{72,120},{1,49},{9,57},{65,113},{73,121},{2... | collective-permute-start | bytes 393224 | tf_op jit(solution)/shard_map/cond/branch_0_fun/ppermute | solution.py:259
  18.1 1.3 %collective-permute-start.5 = (bf16[2,256,128]{2,1,0:T(8,128)(2,1)S(1)}, bf16[2,256,128]{2,1,0:T(8,128)(2,1)S(1)}, u32[]{:S(2)}, u32[]{:S(2)}) collective-permute-start(bf16[2,256,128]{2,1,0:T(8,128)(2,1)S(1)} %get-tuple-element.83), channel_id=1, source_target_pairs={{0,32},{8,40},{64,96},{72,104},{1,33},{9,41},{65,97},{73,105},{2,3... | collective-permute-start | bytes 393224 | tf_op jit(solution)/shard_map/cond/branch_0_fun/ppermute | solution.py:259
  19.4 1.3 %collective-permute-start.6 = (bf16[2,256,128]{2,1,0:T(8,128)(2,1)S(1)}, bf16[2,256,128]{2,1,0:T(8,128)(2,1)S(1)}, u32[]{:S(2)}, u32[]{:S(2)}) collective-permute-start(bf16[2,256,128]{2,1,0:T(8,128)(2,1)S(1)} %get-tuple-element.84), channel_id=1, source_target_pairs={{0,16},{8,24},{64,80},{72,88},{1,17},{9,25},{65,81},{73,89},{2,18}... | collective-permute-start | bytes 393224 | tf_op jit(solution)/shard_map/cond/branch_0_fun/ppermute | solution.py:259
  20.7 2.6 %collective-permute-done.3 = bf16[2,256,128]{2,1,0:T(8,128)(2,1)S(1)} collective-permute-done((bf16[2,256,128]{2,1,0:T(8,128)(2,1)S(1)}, bf16[2,256,128]{2,1,0:T(8,128)(2,1)S(1)}, u32[]{:S(2)}, u32[]{:S(2)}) %collective-permute-start.3) | collective-permute-done | bytes 131104 | tf_op jit(solution)/shard_map/cond/branch_0_fun/ppermute | solution.py:259
  23.3 0.9 collective-permute-done.5
  24.2 2.8 %collective-permute-done.6 = bf16[2,256,128]{2,1,0:T(8,128)(2,1)S(1)} collective-permute-done((bf16[2,256,128]{2,1,0:T(8,128)(2,1)S(1)}, bf16[2,256,128]{2,1,0:T(8,128)(2,1)S(1)}, u32[]{:S(2)}, u32[]{:S(2)}) %collective-permute-start.6) | collective-permute-done | bytes 131104 | tf_op jit(solution)/shard_map/cond/branch_0_fun/ppermute | solution.py:259
  27.1 2.8 %collective-permute-start.28 = (bf16[2,256,128]{2,1,0:T(8,128)(2,1)S(1)}, bf16[2,256,128]{2,1,0:T(8,128)(2,1)S(1)}, u32[]{:S(2)}, u32[]{:S(2)}) collective-permute-start(bf16[2,256,128]{2,1,0:T(8,128)(2,1)S(1)} %get-tuple-element.239), channel_id=1, source_target_pairs={{0,8},{8,0},{16,24},{24,16},{32,40},{40,32},{48,56},{56,48},{64,72... | collective-permute-start | bytes 393224 | tf_op jit(solution)/shard_map/ppermute | solution.py:232
  29.9 2.4 %shard_map.104 = bf16[2,4,640,128]{3,2,1,0:T(8,128)(2,1)} custom-call(bf16[2,4,2,640,128]{4,3,2,1,0:T(8,128)(2,1)} %bitcast.23), custom_call_target="tpu_custom_call" | custom-call | tf_op jit(solution)/shard_map/pallas_call | solution.py:186
  32.5 3.0 %collective-permute-start.31 = (bf16[2,4,640,128]{3,2,1,0:T(8,128)(2,1)}, bf16[2,4,640,128]{3,2,1,0:T(8,128)(2,1)S(1)}, u32[]{:S(2)}, u32[]{:S(2)}) collective-permute-start(bf16[2,4,640,128]{3,2,1,0:T(8,128)(2,1)} %shard_map.104), channel_id=1, source_target_pairs={{0,1},{1,0},{2,3},{3,2},{4,5},{5,4},{6,7},{7,6},{8,9},{9,8},{10,11... | collective-permute-start | bytes 3932168 | tf_op jit(solution)/shard_map/ppermute | solution.py:276
  35.5 2.3 %collective-permute-start.29 = (bf16[2,256,128]{2,1,0:T(8,128)(2,1)S(1)}, bf16[2,256,128]{2,1,0:T(8,128)(2,1)S(1)}, u32[]{:S(2)}, u32[]{:S(2)}) collective-permute-start(bf16[2,256,128]{2,1,0:T(8,128)(2,1)S(1)} %broadcast_select_fusion.refs_1_.refs_0_), channel_id=1, source_target_pairs={{0,16},{8,24},{16,32},{24,40},{32,48},{40,56},{48,64},{56,72},{64,... | collective-permute-start | bytes 393224 | tf_op jit(solution)/shard_map/ppermute | solution.py:228
  39.6 2.1 %shard_map.105.refs_2_ = f32[4,8,512]{2,1,0:T(8,128)S(1)} custom-call(s32[1]{0:T(128)S(6)} %copy.16.live_ref, s32[1]{0:T(128)S(6)} %copy.15.rows_ref, bf16[512,512]{1,0:T(8,128)(2,1)S(1)} %bitcast.25, bf16[512,512]{1,0:T(8,128)(2,1)S(1)} %bitcast.36, bf16[2,512,128]{2,1,0:T(8,128)(2,1)S(1)} %bitcast.47, ...), custom_call_target="tpu_custom_call" | custom-call | flops 805306368 | bytes 1048576 | tf_op jit(solution)/shard_map/pallas_call | solution.py:79
  43.0 2.3 %collective-permute-start.33 = (bf16[2,256,128]{2,1,0:T(8,128)(2,1)S(1)}, bf16[2,256,128]{2,1,0:T(8,128)(2,1)S(1)}, u32[]{:S(2)}, u32[]{:S(2)}) collective-permute-start(bf16[2,256,128]{2,1,0:T(8,128)(2,1)S(1)} %collective-permute-done.30.refs_1_.refs_0_), channel_id=1, source_target_pairs={{0,112},{8,120},{16,0},{24,8},{32,16},{40,24},{48,32},{56,40},{64,... | collective-permute-start | bytes 393224 | tf_op jit(solution)/shard_map/ppermute | solution.py:228
  45.3 1.9 %shard_map.106.refs_2_ = f32[4,8,512]{2,1,0:T(8,128)S(1)} custom-call(s32[1]{0:T(128)S(6)} %copy.16.live_ref, s32[1]{0:T(128)S(6)} %copy.15.rows_ref, bf16[512,512]{1,0:T(8,128)(2,1)S(1)} %bitcast.26, bf16[512,512]{1,0:T(8,128)(2,1)S(1)} %bitcast.37, bf16[2,256,128]{2,1,0:T(8,128)(2,1)S(1)} %collective-permute-done.29.refs_0_.refs_1_, ...), custom_call_target="tpu_custom_call" | custom-call | flops 536870912 | bytes 1048576 | tf_op jit(solution)/shard_map/pallas_call | solution.py:79
  47.7 1.4 %collective-permute-start.34 = (bf16[2,256,128]{2,1,0:T(8,128)(2,1)S(1)}, bf16[2,256,128]{2,1,0:T(8,128)(2,1)S(1)}, u32[]{:S(2)}, u32[]{:S(2)}) collective-permute-start(bf16[2,256,128]{2,1,0:T(8,128)(2,1)S(1)} %collective-permute-done.32.refs_0_.refs_1_), channel_id=1, source_target_pairs={{0,16},{8,24},{16,32},{24,40},{32,48},{40,56},{48,64},{56,72},{64,... | collective-permute-start | bytes 393224 | tf_op jit(solution)/shard_map/ppermute | solution.py:228
  49.1 1.3 %collective-permute-start.35 = (bf16[2,256,128]{2,1,0:T(8,128)(2,1)S(1)}, bf16[2,256,128]{2,1,0:T(8,128)(2,1)S(1)}, u32[]{:S(2)}, u32[]{:S(2)}) collective-permute-start(bf16[2,256,128]{2,1,0:T(8,128)(2,1)S(1)} %collective-permute-done.33.refs_1_.refs_0_), channel_id=1, source_target_pairs={{0,112},{8,120},{16,0},{24,8},{32,16},{40,24},{48,32},{56,40},{64,... | collective-permute-start | bytes 393224 | tf_op jit(solution)/shard_map/ppermute | solution.py:228
  50.4 1.9 %shard_map.107.refs_2_ = f32[4,8,512]{2,1,0:T(8,128)S(1)} custom-call(s32[1]{0:T(128)S(6)} %copy.16.live_ref, s32[1]{0:T(128)S(6)} %copy.15.rows_ref, bf16[512,512]{1,0:T(8,128)(2,1)S(1)} %bitcast.27, bf16[512,512]{1,0:T(8,128)(2,1)S(1)} %bitcast.38, bf16[2,256,128]{2,1,0:T(8,128)(2,1)S(1)} %collective-permute-done.32.refs_0_.refs_1_, ...), custom_call_target="tpu_custom_call" | custom-call | flops 536870912 | bytes 1048576 | tf_op jit(solution)/shard_map/pallas_call | solution.py:79
  52.9 2.5 %collective-permute-start.36 = (bf16[2,256,128]{2,1,0:T(8,128)(2,1)S(1)}, bf16[2,256,128]{2,1,0:T(8,128)(2,1)S(1)}, u32[]{:S(2)}, u32[]{:S(2)}) collective-permute-start(bf16[2,256,128]{2,1,0:T(8,128)(2,1)S(1)} %collective-permute-done.34.refs_0_.refs_1_), channel_id=1, source_target_pairs={{0,16},{8,24},{16,32},{24,40},{32,48},{40,56},{48,64},{56,72},{64,... | collective-permute-start | bytes 393224 | tf_op jit(solution)/shard_map/ppermute | solution.py:228
  55.4 1.9 %shard_map.108.refs_1_ = f32[4,8,512]{2,1,0:T(8,128)S(1)} custom-call(s32[1]{0:T(128)S(6)} %copy.16.live_ref, s32[1]{0:T(128)S(6)} %copy.15.rows_ref, bf16[512,512]{1,0:T(8,128)(2,1)S(1)} %bitcast.28, bf16[512,512]{1,0:T(8,128)(2,1)S(1)} %bitcast.39, bf16[2,256,128]{2,1,0:T(8,128)(2,1)S(1)} %collective-permute-done.34.refs_0_.refs_1_, ...), custom_call_target="tpu_custom_call" | custom-call | flops 536870912 | bytes 1048576 | tf_op jit(solution)/shard_map/pallas_call | solution.py:79
  57.9 1.1 shard_map.109.stat_ref
  59.0 1.6 %shard_map.110 = (f32[512,512]{1,0:T(8,128)S(1)}, bf16[2,256,128]{2,1,0:T(8,128)(2,1)S(1)}) custom-call(s32[1]{0:T(128)S(6)} %copy.16.live_ref, s32[1]{0:T(128)S(6)} %copy.15.rows_ref, bf16[512,512]{1,0:T(8,128)(2,1)S(1)} %bitcast.30, bf16[512,512]{1,0:T(8,128)(2,1)S(1)} %bitcast.41, f32[4,8,512]{2,1,0:T(8,128)S(1)} %shard_map.109.stat_ref, ...), custom_call_target="tpu_custom_call" | custom-call | flops 671088640 | bytes 1048576 | tf_op jit(solution)/shard_map/pallas_call | solution.py:138
  60.7 1.4 %collective-permute-start.37 = (bf16[2,256,128]{2,1,0:T(8,128)(2,1)S(1)}, bf16[2,256,128]{2,1,0:T(8,128)(2,1)S(1)}, u32[]{:S(2)}, u32[]{:S(2)}) collective-permute-start(bf16[2,256,128]{2,1,0:T(8,128)(2,1)S(1)} %get-tuple-element.201), channel_id=1, source_target_pairs={{0,16},{8,24},{16,32},{24,40},{32,48},{40,56},{48,64},{56,72},{64,... | collective-permute-start | bytes 393224 | tf_op jit(solution)/shard_map/ppermute | solution.py:228
  62.0 3.0 %shard_map.111 = (f32[512,512]{1,0:T(8,128)S(1)}, bf16[2,256,128]{2,1,0:T(8,128)(2,1)S(1)}, bf16[2,256,128]{2,1,0:T(8,128)(2,1)S(1)}) custom-call(s32[1]{0:T(128)S(6)} %copy.16.live_ref, s32[1]{0:T(128)S(6)} %copy.15.rows_ref, bf16[512,512]{1,0:T(8,128)(2,1)S(1)} %bitcast.31, bf16[512,512]{1,0:T(8,128)(2,1)S(1)} %bitcast.42, ...), custom_call_target="tpu_custom_call" | custom-call | flops 1342177280 | bytes 1048576 | tf_op jit(solution)/shard_map/pallas_call | solution.py:138
  65.8 0.8 collective-permute-start.38
  66.6 2.0 %collective-permute-start.41 = (bf16[2,256,128]{2,1,0:T(8,128)(2,1)S(1)}, bf16[2,256,128]{2,1,0:T(8,128)(2,1)S(1)}, u32[]{:S(2)}, u32[]{:S(2)}) collective-permute-start(bf16[2,256,128]{2,1,0:T(8,128)(2,1)S(1)} %get-tuple-element.222), channel_id=1, source_target_pairs={{0,112},{8,120},{16,0},{24,8},{32,16},{40,24},{48,32},{56,40},{64,... | collective-permute-start | bytes 393224 | tf_op jit(solution)/shard_map/ppermute | solution.py:228
  68.6 3.0 %shard_map.112 = (f32[512,512]{1,0:T(8,128)S(1)}, bf16[2,256,128]{2,1,0:T(8,128)(2,1)S(1)}, bf16[2,256,128]{2,1,0:T(8,128)(2,1)S(1)}) custom-call(s32[1]{0:T(128)S(6)} %copy.16.live_ref, s32[1]{0:T(128)S(6)} %copy.15.rows_ref, bf16[512,512]{1,0:T(8,128)(2,1)S(1)} %bitcast.32, bf16[512,512]{1,0:T(8,128)(2,1)S(1)} %bitcast.43, ...), custom_call_target="tpu_custom_call" | custom-call | flops 1342177280 | bytes 1048576 | tf_op jit(solution)/shard_map/pallas_call | solution.py:138
  71.6 0.9 collective-permute-done.38
  72.7 2.7 %collective-permute-start.42 = (bf16[2,256,128]{2,1,0:T(8,128)(2,1)S(1)}, bf16[2,256,128]{2,1,0:T(8,128)(2,1)S(1)}, u32[]{:S(2)}, u32[]{:S(2)}) collective-permute-start(bf16[2,256,128]{2,1,0:T(8,128)(2,1)S(1)} %add_convert_fusion.1), channel_id=1, source_target_pairs={{0,112},{8,120},{16,0},{24,8},{32,16},{40,24},{48,32},{56,40},{64,... | collective-permute-start | bytes 393224 | tf_op jit(solution)/shard_map/ppermute | solution.py:228
  75.4 3.0 %shard_map.113 = (f32[512,512]{1,0:T(8,128)S(1)}, bf16[2,256,128]{2,1,0:T(8,128)(2,1)S(1)}, bf16[2,256,128]{2,1,0:T(8,128)(2,1)S(1)}) custom-call(s32[1]{0:T(128)S(6)} %copy.16.live_ref, s32[1]{0:T(128)S(6)} %copy.15.rows_ref, bf16[512,512]{1,0:T(8,128)(2,1)S(1)} %bitcast.33, bf16[512,512]{1,0:T(8,128)(2,1)S(1)} %bitcast.44, ...), custom_call_target="tpu_custom_call" | custom-call | flops 1342177280 | bytes 1048576 | tf_op jit(solution)/shard_map/pallas_call | solution.py:138
  78.4 1.0 copy-done.4
  79.6 2.9 %collective-permute-start.43 = (bf16[2,256,128]{2,1,0:T(8,128)(2,1)S(1)}, bf16[2,256,128]{2,1,0:T(8,128)(2,1)S(1)}, u32[]{:S(2)}, u32[]{:S(2)}) collective-permute-start(bf16[2,256,128]{2,1,0:T(8,128)(2,1)S(1)} %add_convert_fusion), channel_id=1, source_target_pairs={{0,112},{8,120},{16,0},{24,8},{32,16},{40,24},{48,32},{56,40},{64,... | collective-permute-start | bytes 393224 | tf_op jit(solution)/shard_map/ppermute | solution.py:228
  82.6 1.2 %copy-done.5 = f32[512,512]{1,0:T(8,128)S(1)} copy-done((f32[512,512]{1,0:T(8,128)S(1)}, f32[512,512]{1,0:T(8,128)}, u32[]{:S(2)}) %copy-start.5) | copy-done | bytes 1048600
  83.8 1.6 %shard_map.114 = (f32[512,512]{1,0:T(8,128)S(1)}, bf16[2,256,128]{2,1,0:T(8,128)(2,1)S(1)}) custom-call(s32[1]{0:T(128)S(6)} %copy.16.live_ref, s32[1]{0:T(128)S(6)} %copy.15.rows_ref, bf16[512,512]{1,0:T(8,128)(2,1)S(1)} %bitcast.34, bf16[512,512]{1,0:T(8,128)(2,1)S(1)} %bitcast.45, f32[4,8,512]{2,1,0:T(8,128)S(1)} %shard_map.109.stat_ref, ...), custom_call_target="tpu_custom_call" | custom-call | flops 671088640 | bytes 1048576 | tf_op jit(solution)/shard_map/pallas_call | solution.py:138
  85.6 2.9 %collective-permute-start.44 = (bf16[2,128,128]{2,1,0:T(8,128)(2,1)S(1)}, bf16[2,128,128]{2,1,0:T(8,128)(2,1)S(1)}, u32[]{:S(2)}, u32[]{:S(2)}) collective-permute-start(bf16[2,128,128]{2,1,0:T(8,128)(2,1)S(1)} %add_convert_fusion.6), channel_id=1, source_target_pairs={{0,8},{8,0},{16,24},{24,16},{32,40},{40,32},{48,56},{56,48},{64,72... | collective-permute-start | bytes 196616 | tf_op jit(solution)/shard_map/ppermute | solution.py:232
  88.4 3.9 %shard_map.115 = (bf16[512,512]{1,0:T(8,128)(2,1)}, bf16[2,512,128]{2,1,0:T(8,128)(2,1)}) custom-call(s32[1]{0:T(128)S(6)} %copy.16.live_ref, s32[1]{0:T(128)S(6)} %copy.15.rows_ref, bf16[512,512]{1,0:T(8,128)(2,1)S(1)} %bitcast.35, bf16[512,512]{1,0:T(8,128)(2,1)S(1)} %bitcast.46, f32[4,8,512]{2,1,0:T(8,128)S(1)} %shard_map.109.stat_ref, ...), custom_call_target="tpu_custom_call" | custom-call | flops 1342177280 | bytes 1048576 | tf_op jit(solution)/shard_map/pallas_call | solution.py:138
  92.4 8.7 %collective-permute-start.45 = (bf16[2,128,128]{2,1,0:T(8,128)(2,1)S(1)}, bf16[2,128,128]{2,1,0:T(8,128)(2,1)S(1)}, u32[]{:S(2)}, u32[]{:S(2)}) collective-permute-start(bf16[2,128,128]{2,1,0:T(8,128)(2,1)S(1)} %add_convert_fusion.5.summed_ref), channel_id=1, source_target_pairs={{0,1},{1,0},{2,3},{3,2},{4,5},{5,4},{6,7},{7,6},{8,9},{9,8},{10,11... | collective-permute-start | bytes 196616 | tf_op jit(solution)/shard_map/ppermute | solution.py:316
  101.1 0.9 collective-permute-done.45.beside_ref
  102.0 1.1 shard_map.116
  103.1 1.4 %collective-permute-start.48 = (bf16[128,640]{1,0:T(8,128)(2,1)S(1)}, bf16[128,640]{1,0:T(8,128)(2,1)S(1)}, u32[]{:S(2)}, u32[]{:S(2)}) collective-permute-start(bf16[128,640]{1,0:T(8,128)(2,1)S(1)} %get-tuple-element.237), channel_id=1, source_target_pairs={{0,2},{1,3},{2,4},{3,5},{4,6},{5,7},{6,0},{7,1},{8,10},{9,11},{10,... | collective-permute-start | bytes 491528 | tf_op jit(solution)/shard_map/ppermute | solution.py:320
  104.5 1.5 %collective-permute-start.47 = (bf16[128,640]{1,0:T(8,128)(2,1)S(1)}, bf16[128,640]{1,0:T(8,128)(2,1)S(1)}, u32[]{:S(2)}, u32[]{:S(2)}) collective-permute-start(bf16[128,640]{1,0:T(8,128)(2,1)S(1)} %get-tuple-element.238), channel_id=1, source_target_pairs={{0,6},{1,7},{2,0},{3,1},{4,2},{5,3},{6,4},{7,5},{8,14},{9,15},{10,... | collective-permute-start | bytes 491528 | tf_op jit(solution)/shard_map/ppermute | solution.py:320
  106.0 1.6 %collective-permute-start.46 = (bf16[128,640]{1,0:T(8,128)(2,1)S(1)}, bf16[128,640]{1,0:T(8,128)(2,1)S(1)}, u32[]{:S(2)}, u32[]{:S(2)}) collective-permute-start(bf16[128,640]{1,0:T(8,128)(2,1)S(1)} %get-tuple-element.236), channel_id=1, source_target_pairs={{0,4},{1,5},{2,6},{3,7},{4,0},{5,1},{6,2},{7,3},{8,12},{9,13},{10,... | collective-permute-start | bytes 491528 | tf_op jit(solution)/shard_map/ppermute | solution.py:320
  107.6 2.4 %collective-permute-done.48 = bf16[128,640]{1,0:T(8,128)(2,1)S(1)} collective-permute-done((bf16[128,640]{1,0:T(8,128)(2,1)S(1)}, bf16[128,640]{1,0:T(8,128)(2,1)S(1)}, u32[]{:S(2)}, u32[]{:S(2)}) %collective-permute-start.48) | collective-permute-done | bytes 163872 | tf_op jit(solution)/shard_map/ppermute | solution.py:320
  109.9 4.6 %collective-permute-done.46 = bf16[128,640]{1,0:T(8,128)(2,1)S(1)} collective-permute-done((bf16[128,640]{1,0:T(8,128)(2,1)S(1)}, bf16[128,640]{1,0:T(8,128)(2,1)S(1)}, u32[]{:S(2)}, u32[]{:S(2)}) %collective-permute-start.46) | collective-permute-done | bytes 163872 | tf_op jit(solution)/shard_map/ppermute | solution.py:320
  (46 shorter events, 5.8 us)
Async XLA Ops:
  2.7 15.3 %collective-permute-start = (bf16[2,256,128]{2,1,0:T(8,128)(2,1)S(1)}, bf16[2,256,128]{2,1,0:T(8,128)(2,1)S(1)}, u32[]{:S(2)}, u32[]{:S(2)}) collective-permute-start(bf16[2,256,128]{2,1,0:T(8,128)(2,1)S(1)} %get-tuple-element.61), channel_id=1, source_target_pairs={{0,112},{8,120},{64,48},{72,56},{1,113},{9,121},{65,49},{73,57},{2... | collective-permute-start | bytes 393224 | tf_op jit(solution)/shard_map/cond/branch_0_fun/ppermute | solution.py:259
  11.1 8.3 %collective-permute-start.1 = (bf16[2,256,128]{2,1,0:T(8,128)(2,1)S(1)}, bf16[2,256,128]{2,1,0:T(8,128)(2,1)S(1)}, u32[]{:S(2)}, u32[]{:S(2)}) collective-permute-start(bf16[2,256,128]{2,1,0:T(8,128)(2,1)S(1)} %get-tuple-element.62), channel_id=1, source_target_pairs={{0,96},{8,104},{64,32},{72,40},{1,97},{9,105},{65,33},{73,41},{2,9... | collective-permute-start | bytes 393224 | tf_op jit(solution)/shard_map/cond/branch_0_fun/ppermute | solution.py:259
  12.4 8.3 %collective-permute-start.2 = (bf16[2,256,128]{2,1,0:T(8,128)(2,1)S(1)}, bf16[2,256,128]{2,1,0:T(8,128)(2,1)S(1)}, u32[]{:S(2)}, u32[]{:S(2)}) collective-permute-start(bf16[2,256,128]{2,1,0:T(8,128)(2,1)S(1)} %get-tuple-element.80), channel_id=1, source_target_pairs={{0,80},{8,88},{64,16},{72,24},{1,81},{9,89},{65,17},{73,25},{2,82}... | collective-permute-start | bytes 393224 | tf_op jit(solution)/shard_map/cond/branch_0_fun/ppermute | solution.py:259
  13.7 9.6 %collective-permute-start.3 = (bf16[2,256,128]{2,1,0:T(8,128)(2,1)S(1)}, bf16[2,256,128]{2,1,0:T(8,128)(2,1)S(1)}, u32[]{:S(2)}, u32[]{:S(2)}) collective-permute-start(bf16[2,256,128]{2,1,0:T(8,128)(2,1)S(1)} %get-tuple-element.81), channel_id=1, source_target_pairs={{0,64},{8,72},{64,0},{72,8},{1,65},{9,73},{65,1},{73,9},{2,66},{10... | collective-permute-start | bytes 393224 | tf_op jit(solution)/shard_map/cond/branch_0_fun/ppermute | solution.py:259
  16.7 6.5 %collective-permute-start.4 = (bf16[2,256,128]{2,1,0:T(8,128)(2,1)S(1)}, bf16[2,256,128]{2,1,0:T(8,128)(2,1)S(1)}, u32[]{:S(2)}, u32[]{:S(2)}) collective-permute-start(bf16[2,256,128]{2,1,0:T(8,128)(2,1)S(1)} %get-tuple-element.82), channel_id=1, source_target_pairs={{0,48},{8,56},{64,112},{72,120},{1,49},{9,57},{65,113},{73,121},{2... | collective-permute-start | bytes 393224 | tf_op jit(solution)/shard_map/cond/branch_0_fun/ppermute | solution.py:259
  18.1 6.1 %collective-permute-start.5 = (bf16[2,256,128]{2,1,0:T(8,128)(2,1)S(1)}, bf16[2,256,128]{2,1,0:T(8,128)(2,1)S(1)}, u32[]{:S(2)}, u32[]{:S(2)}) collective-permute-start(bf16[2,256,128]{2,1,0:T(8,128)(2,1)S(1)} %get-tuple-element.83), channel_id=1, source_target_pairs={{0,32},{8,40},{64,96},{72,104},{1,33},{9,41},{65,97},{73,105},{2,3... | collective-permute-start | bytes 393224 | tf_op jit(solution)/shard_map/cond/branch_0_fun/ppermute | solution.py:259
  19.4 7.6 %collective-permute-start.6 = (bf16[2,256,128]{2,1,0:T(8,128)(2,1)S(1)}, bf16[2,256,128]{2,1,0:T(8,128)(2,1)S(1)}, u32[]{:S(2)}, u32[]{:S(2)}) collective-permute-start(bf16[2,256,128]{2,1,0:T(8,128)(2,1)S(1)} %get-tuple-element.84), channel_id=1, source_target_pairs={{0,16},{8,24},{64,80},{72,88},{1,17},{9,25},{65,81},{73,89},{2,18}... | collective-permute-start | bytes 393224 | tf_op jit(solution)/shard_map/cond/branch_0_fun/ppermute | solution.py:259
  27.1 12.5 %copy-start.1 = (bf16[1,512,512]{2,1,0:T(8,128)(2,1)S(1)}, bf16[1,512,512]{2,1,0:T(8,128)(2,1)}, u32[]{:S(2)}) copy-start(bf16[1,512,512]{2,1,0:T(8,128)(2,1)} %param.12) | copy-start | bytes 1572868
  27.1 12.5 %copy-start.2 = (bf16[1,512,512]{2,1,0:T(8,128)(2,1)S(1)}, bf16[1,512,512]{2,1,0:T(8,128)(2,1)}, u32[]{:S(2)}) copy-start(bf16[1,512,512]{2,1,0:T(8,128)(2,1)} %param.14) | copy-start | bytes 1572868
  27.1 12.5 %copy-start.3 = (bf16[1,2,512,128]{3,2,1,0:T(8,128)(2,1)S(1)}, bf16[1,2,512,128]{3,2,1,0:T(8,128)(2,1)}, u32[]{:S(2)}) copy-start(bf16[1,2,512,128]{3,2,1,0:T(8,128)(2,1)} %param.13) | copy-start | bytes 786436
  27.1 5.4 %collective-permute-start.28 = (bf16[2,256,128]{2,1,0:T(8,128)(2,1)S(1)}, bf16[2,256,128]{2,1,0:T(8,128)(2,1)S(1)}, u32[]{:S(2)}, u32[]{:S(2)}) collective-permute-start(bf16[2,256,128]{2,1,0:T(8,128)(2,1)S(1)} %get-tuple-element.239), channel_id=1, source_target_pairs={{0,8},{8,0},{16,24},{24,16},{32,40},{40,32},{48,56},{56,48},{64,72... | collective-permute-start | bytes 393224 | tf_op jit(solution)/shard_map/ppermute | solution.py:232
  32.5 10.1 %collective-permute-start.31 = (bf16[2,4,640,128]{3,2,1,0:T(8,128)(2,1)}, bf16[2,4,640,128]{3,2,1,0:T(8,128)(2,1)S(1)}, u32[]{:S(2)}, u32[]{:S(2)}) collective-permute-start(bf16[2,4,640,128]{3,2,1,0:T(8,128)(2,1)} %shard_map.104), channel_id=1, source_target_pairs={{0,1},{1,0},{2,3},{3,2},{4,5},{5,4},{6,7},{7,6},{8,9},{9,8},{10,11... | collective-permute-start | bytes 3932168 | tf_op jit(solution)/shard_map/ppermute | solution.py:276
  35.5 6.4 %collective-permute-start.29 = (bf16[2,256,128]{2,1,0:T(8,128)(2,1)S(1)}, bf16[2,256,128]{2,1,0:T(8,128)(2,1)S(1)}, u32[]{:S(2)}, u32[]{:S(2)}) collective-permute-start(bf16[2,256,128]{2,1,0:T(8,128)(2,1)S(1)} %broadcast_select_fusion.refs_1_.refs_0_), channel_id=1, source_target_pairs={{0,16},{8,24},{16,32},{24,40},{32,48},{40,56},{48,64},{56,72},{64,... | collective-permute-start | bytes 393224 | tf_op jit(solution)/shard_map/ppermute | solution.py:228
  37.8 4.8 %collective-permute-start.30 = (bf16[2,256,128]{2,1,0:T(8,128)(2,1)S(1)}, bf16[2,256,128]{2,1,0:T(8,128)(2,1)S(1)}, u32[]{:S(2)}, u32[]{:S(2)}) collective-permute-start(bf16[2,256,128]{2,1,0:T(8,128)(2,1)S(1)} %broadcast_select_fusion.refs_1_.refs_0_), channel_id=1, source_target_pairs={{0,112},{8,120},{16,0},{24,8},{32,16},{40,24},{48,32},{56,40},{64,... | collective-permute-start | bytes 393224 | tf_op jit(solution)/shard_map/ppermute | solution.py:228
  42.6 5.0 %collective-permute-start.32 = (bf16[2,256,128]{2,1,0:T(8,128)(2,1)S(1)}, bf16[2,256,128]{2,1,0:T(8,128)(2,1)S(1)}, u32[]{:S(2)}, u32[]{:S(2)}) collective-permute-start(bf16[2,256,128]{2,1,0:T(8,128)(2,1)S(1)} %collective-permute-done.29.refs_0_.refs_1_), channel_id=1, source_target_pairs={{0,16},{8,24},{16,32},{24,40},{32,48},{40,56},{48,64},{56,72},{64,... | collective-permute-start | bytes 393224 | tf_op jit(solution)/shard_map/ppermute | solution.py:228
  43.0 4.6 %collective-permute-start.33 = (bf16[2,256,128]{2,1,0:T(8,128)(2,1)S(1)}, bf16[2,256,128]{2,1,0:T(8,128)(2,1)S(1)}, u32[]{:S(2)}, u32[]{:S(2)}) collective-permute-start(bf16[2,256,128]{2,1,0:T(8,128)(2,1)S(1)} %collective-permute-done.30.refs_1_.refs_0_), channel_id=1, source_target_pairs={{0,112},{8,120},{16,0},{24,8},{32,16},{40,24},{48,32},{56,40},{64,... | collective-permute-start | bytes 393224 | tf_op jit(solution)/shard_map/ppermute | solution.py:228
  47.7 5.0 %collective-permute-start.34 = (bf16[2,256,128]{2,1,0:T(8,128)(2,1)S(1)}, bf16[2,256,128]{2,1,0:T(8,128)(2,1)S(1)}, u32[]{:S(2)}, u32[]{:S(2)}) collective-permute-start(bf16[2,256,128]{2,1,0:T(8,128)(2,1)S(1)} %collective-permute-done.32.refs_0_.refs_1_), channel_id=1, source_target_pairs={{0,16},{8,24},{16,32},{24,40},{32,48},{40,56},{48,64},{56,72},{64,... | collective-permute-start | bytes 393224 | tf_op jit(solution)/shard_map/ppermute | solution.py:228
  49.1 3.8 %collective-permute-start.35 = (bf16[2,256,128]{2,1,0:T(8,128)(2,1)S(1)}, bf16[2,256,128]{2,1,0:T(8,128)(2,1)S(1)}, u32[]{:S(2)}, u32[]{:S(2)}) collective-permute-start(bf16[2,256,128]{2,1,0:T(8,128)(2,1)S(1)} %collective-permute-done.33.refs_1_.refs_0_), channel_id=1, source_target_pairs={{0,112},{8,120},{16,0},{24,8},{32,16},{40,24},{48,32},{56,40},{64,... | collective-permute-start | bytes 393224 | tf_op jit(solution)/shard_map/ppermute | solution.py:228
  52.9 5.0 %collective-permute-start.36 = (bf16[2,256,128]{2,1,0:T(8,128)(2,1)S(1)}, bf16[2,256,128]{2,1,0:T(8,128)(2,1)S(1)}, u32[]{:S(2)}, u32[]{:S(2)}) collective-permute-start(bf16[2,256,128]{2,1,0:T(8,128)(2,1)S(1)} %collective-permute-done.34.refs_0_.refs_1_), channel_id=1, source_target_pairs={{0,16},{8,24},{16,32},{24,40},{32,48},{40,56},{48,64},{56,72},{64,... | collective-permute-start | bytes 393224 | tf_op jit(solution)/shard_map/ppermute | solution.py:228
  60.7 5.1 %collective-permute-start.37 = (bf16[2,256,128]{2,1,0:T(8,128)(2,1)S(1)}, bf16[2,256,128]{2,1,0:T(8,128)(2,1)S(1)}, u32[]{:S(2)}, u32[]{:S(2)}) collective-permute-start(bf16[2,256,128]{2,1,0:T(8,128)(2,1)S(1)} %get-tuple-element.201), channel_id=1, source_target_pairs={{0,16},{8,24},{16,32},{24,40},{32,48},{40,56},{48,64},{56,72},{64,... | collective-permute-start | bytes 393224 | tf_op jit(solution)/shard_map/ppermute | solution.py:228
  65.8 6.7 %collective-permute-start.38 = (bf16[2,256,128]{2,1,0:T(8,128)(2,1)S(1)}, bf16[2,256,128]{2,1,0:T(8,128)(2,1)S(1)}, u32[]{:S(2)}, u32[]{:S(2)}) collective-permute-start(bf16[2,256,128]{2,1,0:T(8,128)(2,1)S(1)} %add_convert_fusion.4), channel_id=1, source_target_pairs={{0,16},{8,24},{16,32},{24,40},{32,48},{40,56},{48,64},{56,72},{64,... | collective-permute-start | bytes 393224 | tf_op jit(solution)/shard_map/ppermute | solution.py:228
  66.6 6.0 %collective-permute-start.41 = (bf16[2,256,128]{2,1,0:T(8,128)(2,1)S(1)}, bf16[2,256,128]{2,1,0:T(8,128)(2,1)S(1)}, u32[]{:S(2)}, u32[]{:S(2)}) collective-permute-start(bf16[2,256,128]{2,1,0:T(8,128)(2,1)S(1)} %get-tuple-element.222), channel_id=1, source_target_pairs={{0,112},{8,120},{16,0},{24,8},{32,16},{40,24},{48,32},{56,40},{64,... | collective-permute-start | bytes 393224 | tf_op jit(solution)/shard_map/ppermute | solution.py:228
  72.5 6.9 %collective-permute-start.39 = (bf16[2,256,128]{2,1,0:T(8,128)(2,1)S(1)}, bf16[2,256,128]{2,1,0:T(8,128)(2,1)S(1)}, u32[]{:S(2)}, u32[]{:S(2)}) collective-permute-start(bf16[2,256,128]{2,1,0:T(8,128)(2,1)S(1)} %add_convert_fusion.3), channel_id=1, source_target_pairs={{0,16},{8,24},{16,32},{24,40},{32,48},{40,56},{48,64},{56,72},{64,... | collective-permute-start | bytes 393224 | tf_op jit(solution)/shard_map/ppermute | solution.py:228
  72.7 6.9 %collective-permute-start.42 = (bf16[2,256,128]{2,1,0:T(8,128)(2,1)S(1)}, bf16[2,256,128]{2,1,0:T(8,128)(2,1)S(1)}, u32[]{:S(2)}, u32[]{:S(2)}) collective-permute-start(bf16[2,256,128]{2,1,0:T(8,128)(2,1)S(1)} %add_convert_fusion.1), channel_id=1, source_target_pairs={{0,112},{8,120},{16,0},{24,8},{32,16},{40,24},{48,32},{56,40},{64,... | collective-permute-start | bytes 393224 | tf_op jit(solution)/shard_map/ppermute | solution.py:228
  78.4 1.0 copy-start.4
  79.5 6.1 %collective-permute-start.40 = (bf16[2,256,128]{2,1,0:T(8,128)(2,1)S(1)}, bf16[2,256,128]{2,1,0:T(8,128)(2,1)S(1)}, u32[]{:S(2)}, u32[]{:S(2)}) collective-permute-start(bf16[2,256,128]{2,1,0:T(8,128)(2,1)S(1)} %add_convert_fusion.2), channel_id=1, source_target_pairs={{0,16},{8,24},{16,32},{24,40},{32,48},{40,56},{48,64},{56,72},{64,... | collective-permute-start | bytes 393224 | tf_op jit(solution)/shard_map/ppermute | solution.py:228
  79.6 5.9 %collective-permute-start.43 = (bf16[2,256,128]{2,1,0:T(8,128)(2,1)S(1)}, bf16[2,256,128]{2,1,0:T(8,128)(2,1)S(1)}, u32[]{:S(2)}, u32[]{:S(2)}) collective-permute-start(bf16[2,256,128]{2,1,0:T(8,128)(2,1)S(1)} %add_convert_fusion), channel_id=1, source_target_pairs={{0,112},{8,120},{16,0},{24,8},{32,16},{40,24},{48,32},{56,40},{64,... | collective-permute-start | bytes 393224 | tf_op jit(solution)/shard_map/ppermute | solution.py:228
  82.6 1.2 %copy-start.5 = (f32[512,512]{1,0:T(8,128)S(1)}, f32[512,512]{1,0:T(8,128)}, u32[]{:S(2)}) copy-start(f32[512,512]{1,0:T(8,128)} %copy-done.4) | copy-start | bytes 3145732
  85.6 6.8 %collective-permute-start.44 = (bf16[2,128,128]{2,1,0:T(8,128)(2,1)S(1)}, bf16[2,128,128]{2,1,0:T(8,128)(2,1)S(1)}, u32[]{:S(2)}, u32[]{:S(2)}) collective-permute-start(bf16[2,128,128]{2,1,0:T(8,128)(2,1)S(1)} %add_convert_fusion.6), channel_id=1, source_target_pairs={{0,8},{8,0},{16,24},{24,16},{32,40},{40,32},{48,56},{56,48},{64,72... | collective-permute-start | bytes 196616 | tf_op jit(solution)/shard_map/ppermute | solution.py:232
  88.4 13.5 %copy-start = (bf16[2,5120,128]{2,1,0:T(8,128)(2,1)S(1)}, bf16[2,5120,128]{2,1,0:T(8,128)(2,1)}, u32[]{:S(2)}) copy-start(bf16[2,5120,128]{2,1,0:T(8,128)(2,1)} %param.16) | copy-start | bytes 7864324
  92.4 9.6 %collective-permute-start.45 = (bf16[2,128,128]{2,1,0:T(8,128)(2,1)S(1)}, bf16[2,128,128]{2,1,0:T(8,128)(2,1)S(1)}, u32[]{:S(2)}, u32[]{:S(2)}) collective-permute-start(bf16[2,128,128]{2,1,0:T(8,128)(2,1)S(1)} %add_convert_fusion.5.summed_ref), channel_id=1, source_target_pairs={{0,1},{1,0},{2,3},{3,2},{4,5},{5,4},{6,7},{7,6},{8,9},{9,8},{10,11... | collective-permute-start | bytes 196616 | tf_op jit(solution)/shard_map/ppermute | solution.py:316
  103.1 6.8 %collective-permute-start.48 = (bf16[128,640]{1,0:T(8,128)(2,1)S(1)}, bf16[128,640]{1,0:T(8,128)(2,1)S(1)}, u32[]{:S(2)}, u32[]{:S(2)}) collective-permute-start(bf16[128,640]{1,0:T(8,128)(2,1)S(1)} %get-tuple-element.237), channel_id=1, source_target_pairs={{0,2},{1,3},{2,4},{3,5},{4,6},{5,7},{6,0},{7,1},{8,10},{9,11},{10,... | collective-permute-start | bytes 491528 | tf_op jit(solution)/shard_map/ppermute | solution.py:320
  104.5 5.4 %collective-permute-start.47 = (bf16[128,640]{1,0:T(8,128)(2,1)S(1)}, bf16[128,640]{1,0:T(8,128)(2,1)S(1)}, u32[]{:S(2)}, u32[]{:S(2)}) collective-permute-start(bf16[128,640]{1,0:T(8,128)(2,1)S(1)} %get-tuple-element.238), channel_id=1, source_target_pairs={{0,6},{1,7},{2,0},{3,1},{4,2},{5,3},{6,4},{7,5},{8,14},{9,15},{10,... | collective-permute-start | bytes 491528 | tf_op jit(solution)/shard_map/ppermute | solution.py:320
  106.0 8.6 %collective-permute-start.46 = (bf16[128,640]{1,0:T(8,128)(2,1)S(1)}, bf16[128,640]{1,0:T(8,128)(2,1)S(1)}, u32[]{:S(2)}, u32[]{:S(2)}) collective-permute-start(bf16[128,640]{1,0:T(8,128)(2,1)S(1)} %get-tuple-element.236), channel_id=1, source_target_pairs={{0,4},{1,5},{2,6},{3,7},{4,0},{5,1},{6,2},{7,3},{8,12},{9,13},{10,... | collective-permute-start | bytes 491528 | tf_op jit(solution)/shard_map/ppermute | solution.py:320
